TPU v7x, 32 devices: a whole 2x2x4 slice. The times are simulated.
32 devices in a mesh: row: 2 (over y), seq: 16 (over z, x, core).
Axes of the slice: x: 2, y: 2, z: 4, core: 2. Of those that a mesh axis runs over, the one named last changes fastest.
Arguments:
- frames: bfloat16 [2, 4096, 1024], P('row', 'seq'), may hold values from -6 to 6
- seg_lengths: int32 [2, 4], P('row'), may hold values from 1 to 3968, 4096 in all within a row
- ln1_gain: float32 [1024], replicated, may hold values from 0.5 to 1.5
- ln1_bias: float32 [1024], replicated, may hold values from -3 to 3
- w_qkv: bfloat16 [1024, 3072], replicated, may hold values from -0.1875 to 0.1875
- bias_qv: float32 [2048], replicated, may hold values from -3 to 3
- w_out: bfloat16 [1024, 1024], replicated, may hold values from -0.75 to 0.75
- bias_out: float32 [1024], replicated, may hold values from -3 to 3
- ln2_gain: float32 [1024], replicated, may hold values from 0.5 to 1.5
- ln2_bias: float32 [1024], replicated, may hold values from -3 to 3
- w_up: bfloat16 [1024, 4096], replicated, may hold values from -0.1875 to 0.1875
- bias_up: float32 [4096], replicated, may hold values from -3 to 3
- w_down: bfloat16 [4096, 1024], replicated, may hold values from -0.09375 to 0.09375
- bias_down: float32 [1024], replicated, may hold values from -6 to 6
- grad_out: bfloat16 [2, 4096, 1024], P('row', 'seq'), may hold values from -6 to 6
Outputs:
- out_frames: bfloat16 [2, 4096, 1024], P('row', 'seq')
- grad_frames: bfloat16 [2, 4096, 1024], P('row', 'seq')
- grad_ln1_gain: float32 [1024], P('seq')
- grad_ln1_bias: float32 [1024], P('seq')
- grad_w_qkv: float32 [1024, 3072], P('seq')
- grad_bias_qv: float32 [2048], P('seq')
- grad_w_out: float32 [1024, 1024], P('seq')
- grad_bias_out: float32 [1024], P('seq')
- grad_ln2_gain: float32 [1024], P('seq')
- grad_ln2_bias: float32 [1024], P('seq')
- grad_w_up: float32 [1024, 4096], P('seq')
- grad_bias_up: float32 [4096], P('seq')
- grad_w_down: float32 [4096, 1024], P('seq')
- grad_bias_down: float32 [1024], P('seq')
Inputs may be any that keep to these rules, and one draw needn't show every extreme that they name: `seg_lengths`: the 4 segments of a packed row in order; their lengths sum to 4096.
All inputs are finite; a program needn't handle non-finite values.
Results may differ from a plain program's by a relative error of at most 0.024.
Values may be sent and summed in bfloat16 or wider, within the bound.
No kernel may reach another device: no remote copies, remote signals or barrier semaphores. Data moves between devices by JAX's collectives and lax.ppermute only.
A program may use at most 256 MiB of HBM per device.

v0:
```python
import jax
import jax.numpy as jnp
from jax import lax
from jax.sharding import PartitionSpec as P

HEADS = 16
HEAD_DIM = 64


EPSILON = 1e-05
NEGATIVE = -1e30


def normalize(values, norm_gain, norm_shift):
    centre = jnp.mean(values, axis=-1, keepdims=True)
    centred = values - centre
    second = jnp.mean(centred * centred, axis=-1, keepdims=True)
    return centred * lax.rsqrt(second + EPSILON) * norm_gain + norm_shift


def smooth_gate(values):
    return jax.nn.gelu(values, approximate=False)


def segment_first(lengths, positions):
    offsets = jnp.cumsum(lengths, dtype=jnp.int32) - lengths
    reached = offsets[None, :] <= positions[:, None]
    return jnp.max(jnp.where(reached, offsets[None, :], 0), axis=1)


def inner_rows(left, right):
    return lax.dot_general(
        left, right, (((0,), (0,)), ((), ())), preferred_element_type=jnp.float32
    )


def times_transposed(left, right):
    return lax.dot_general(
        left, right, (((1,), (1,)), ((), ())), preferred_element_type=jnp.float32
    )


def masked_scores(query_rows, key_rows, query_pos, query_first, key_pos, score_scale):
    query_split = query_rows.reshape(query_rows.shape[0], HEADS, HEAD_DIM)
    key_split = key_rows.reshape(key_rows.shape[0], HEADS, HEAD_DIM)
    raw_scores = (
        jnp.einsum("qhd,khd->hqk", query_split, key_split, preferred_element_type=jnp.float32)
        * score_scale
    )
    allowed = (key_pos[None, :] <= query_pos[:, None]) & (key_pos[None, :] >= query_first[:, None])
    return jnp.where(allowed[None], raw_scores, NEGATIVE)


def split_blocks(arrays, shard_rows):
    row_count = arrays[0].shape[0]
    block_rows = 2 * shard_rows
    block_count = row_count // block_rows
    shaped = tuple(
        (member.reshape((block_count, block_rows) + member.shape[1:]) for member in arrays)
    )
    starts = block_rows * lax.iota(jnp.int32, block_count)
    return (shaped + (starts,), block_rows)


def per_device(
    frames,
    seg_lengths,
    ln1_gain,
    ln1_bias,
    w_qkv,
    bias_qv,
    w_out,
    bias_out,
    ln2_gain,
    ln2_bias,
    w_up,
    bias_up,
    w_down,
    bias_down,
    grad_out,
):
    tokens = frames.shape[1]
    feature = frames.shape[2]
    score_scale = HEAD_DIM ** (-0.5)
    lengths = seg_lengths[0]
    first_pos = lax.axis_index("seq") * tokens
    last_pos = first_pos + tokens - 1
    query_pos = first_pos + lax.iota(jnp.int32, tokens)
    query_first = segment_first(lengths, query_pos)
    lowest_first = jnp.min(query_first)
    full_rows = tokens * lax.axis_size("seq")
    stream = frames[0].astype(jnp.float32)
    normed, first_norm_back = jax.vjp(normalize, stream, ln1_gain, ln1_bias)
    normed_low = normed.astype(jnp.bfloat16)
    bias_full = jnp.concatenate(
        [bias_qv[:feature], jnp.zeros((feature,), jnp.float32), bias_qv[feature:]]
    )
    projected = (jnp.dot(normed_low, w_qkv, preferred_element_type=jnp.float32) + bias_full).astype(
        jnp.bfloat16
    )
    queries = projected[:, :feature]
    key_rows = projected[:, feature : 2 * feature]
    value_rows = projected[:, 2 * feature :]
    empty_rows = jnp.zeros((tokens, feature), jnp.float32)
    start_top = jnp.full((tokens, HEADS), NEGATIVE, jnp.float32)
    start_total = jnp.zeros((tokens, HEADS), jnp.float32)
    carried = (empty_rows, start_top, start_total)
    blocks, block_rows = split_blocks(
        (
            lax.all_gather(key_rows, "seq", axis=0, tiled=True),
            lax.all_gather(value_rows, "seq", axis=0, tiled=True),
        ),
        tokens,
    )

    def forward_visit(inner, block_data):
        key_block, value_block, block_start = block_data
        key_pos = block_start + lax.iota(jnp.int32, block_rows)

        def attend(current):
            summed_now, top_now, total_now = current
            scores = masked_scores(queries, key_block, query_pos, query_first, key_pos, score_scale)
            top_next = jnp.maximum(top_now, jnp.max(scores, axis=2).T)
            weights = jnp.exp(scores - top_next.T[:, :, None])
            fading = jnp.exp(top_now - top_next)
            total_next = total_now * fading + jnp.sum(weights, axis=2).T
            value_split = value_block.reshape(block_rows, HEADS, HEAD_DIM)
            gained = jnp.einsum(
                "hqk,khd->qhd",
                weights.astype(jnp.bfloat16),
                value_split,
                preferred_element_type=jnp.float32,
            )
            summed_next = summed_now.reshape(tokens, HEADS, HEAD_DIM) * fading[:, :, None] + gained
            return (summed_next.reshape(tokens, feature), top_next, total_next)

        def unchanged(current):
            return current

        active_block = (block_start <= last_pos) & (block_start + block_rows > lowest_first)
        return (lax.cond(active_block, attend, unchanged, inner), None)

    carried, unused_out = lax.scan(forward_visit, carried, blocks)
    summed, row_top, row_total = carried
    attended = (summed.reshape(tokens, HEADS, HEAD_DIM) / row_total[:, :, None]).reshape(
        tokens, feature
    )
    attended_low = attended.astype(jnp.bfloat16)
    branch = jnp.dot(attended_low, w_out, preferred_element_type=jnp.float32) + bias_out
    residual = stream + branch
    normed_two, second_norm_back = jax.vjp(normalize, residual, ln2_gain, ln2_bias)
    normed_two_low = normed_two.astype(jnp.bfloat16)
    up_proj = jnp.dot(normed_two_low, w_up, preferred_element_type=jnp.float32) + bias_up
    activated, gate_back = jax.vjp(smooth_gate, up_proj)
    hidden = activated.astype(jnp.bfloat16)
    out_frames = (
        residual + (jnp.dot(hidden, w_down, preferred_element_type=jnp.float32) + bias_down)
    ).astype(jnp.bfloat16)
    cotangent_low = grad_out[0]
    cotangent = cotangent_low.astype(jnp.float32)
    grad_w_down = inner_rows(hidden, cotangent_low)
    grad_bias_down = jnp.sum(cotangent, axis=0)
    (up_grad,) = gate_back(times_transposed(cotangent_low, w_down))
    up_grad_low = up_grad.astype(jnp.bfloat16)
    grad_w_up = inner_rows(normed_two_low, up_grad_low)
    grad_bias_up = jnp.sum(up_grad_low, axis=0, dtype=jnp.float32)
    residual_part, grad_ln2_gain, grad_ln2_bias = second_norm_back(
        times_transposed(up_grad_low, w_up)
    )
    residual_grad = cotangent + residual_part
    branch_grad = residual_grad.astype(jnp.bfloat16)
    grad_w_out = inner_rows(attended_low, branch_grad)
    grad_bias_out = jnp.sum(branch_grad, axis=0, dtype=jnp.float32)
    attended_grad = times_transposed(branch_grad, w_out).reshape(tokens, HEADS, HEAD_DIM)
    summed_grad = (
        (attended_grad / row_total[:, :, None]).reshape(tokens, feature).astype(jnp.bfloat16)
    )
    delta = jnp.sum(attended_grad * attended.reshape(tokens, HEADS, HEAD_DIM), axis=2)
    shift_term = delta / row_total
    query_split_mine = queries.reshape(tokens, HEADS, HEAD_DIM)
    grad_split_mine = summed_grad.reshape(tokens, HEADS, HEAD_DIM)
    carried = (
        jnp.zeros((tokens, feature), jnp.float32),
        jnp.zeros((full_rows, 2 * feature), jnp.float32),
    )
    blocks, key_block_rows = split_blocks(
        (
            lax.all_gather(key_rows, "seq", axis=0, tiled=True),
            lax.all_gather(value_rows, "seq", axis=0, tiled=True),
        ),
        tokens,
    )

    def key_visit(inner, block_data):
        key_block, value_block, block_start = block_data
        key_pos = block_start + lax.iota(jnp.int32, key_block_rows)

        def differentiate(unused_arg):
            scores = masked_scores(queries, key_block, query_pos, query_first, key_pos, score_scale)
            weights = jnp.exp(scores - row_top.T[:, :, None])
            key_split = key_block.reshape(key_block_rows, HEADS, HEAD_DIM)
            value_split = value_block.reshape(key_block_rows, HEADS, HEAD_DIM)
            through = jnp.einsum(
                "qhd,khd->hqk", grad_split_mine, value_split, preferred_element_type=jnp.float32
            )
            score_grad = (weights * (through - shift_term.T[:, :, None])).astype(jnp.bfloat16)
            query_add = (
                jnp.einsum(
                    "hqk,khd->qhd", score_grad, key_split, preferred_element_type=jnp.float32
                )
                * score_scale
            )
            key_add = (
                jnp.einsum(
                    "hqk,qhd->khd", score_grad, query_split_mine, preferred_element_type=jnp.float32
                )
                * score_scale
            )
            value_add = jnp.einsum(
                "hqk,qhd->khd",
                weights.astype(jnp.bfloat16),
                grad_split_mine,
                preferred_element_type=jnp.float32,
            )
            pair_add = jnp.concatenate(
                [
                    key_add.reshape(key_block_rows, feature),
                    value_add.reshape(key_block_rows, feature),
                ],
                axis=1,
            )
            return (query_add.reshape(tokens, feature), pair_add)

        def skipped(unused_arg):
            return (
                jnp.zeros((tokens, feature), jnp.float32),
                jnp.zeros((key_block_rows, 2 * feature), jnp.float32),
            )

        active_block = (block_start <= last_pos) & (block_start + key_block_rows > lowest_first)
        query_add, pair_add = lax.cond(active_block, differentiate, skipped, 0)
        updated = lax.dynamic_update_slice(inner[1], pair_add, (block_start, jnp.int32(0)))
        return ((inner[0] + query_add, updated), None)

    carried, unused_out = lax.scan(key_visit, carried, blocks)
    query_grad, pair_buffer = carried
    pair_grad = lax.psum_scatter(pair_buffer, "seq", scatter_dimension=0, tiled=True)
    projected_grad = jnp.concatenate([query_grad, pair_grad], axis=1).astype(jnp.bfloat16)
    grad_w_qkv = inner_rows(normed_low, projected_grad)
    column_sums = jnp.sum(projected_grad, axis=0, dtype=jnp.float32)
    grad_bias_qv = jnp.concatenate([column_sums[:feature], column_sums[2 * feature :]])
    stream_part, grad_ln1_gain, grad_ln1_bias = first_norm_back(
        times_transposed(projected_grad, w_qkv)
    )
    grad_frames = (residual_grad + stream_part).astype(jnp.bfloat16)
    shares = (
        lax.psum_scatter(grad_ln1_gain, "seq", scatter_dimension=0, tiled=True),
        lax.psum_scatter(grad_ln1_bias, "seq", scatter_dimension=0, tiled=True),
        lax.psum_scatter(grad_w_qkv, "seq", scatter_dimension=0, tiled=True),
        lax.psum_scatter(grad_bias_qv, "seq", scatter_dimension=0, tiled=True),
        lax.psum_scatter(grad_w_out, "seq", scatter_dimension=0, tiled=True),
        lax.psum_scatter(grad_bias_out, "seq", scatter_dimension=0, tiled=True),
        lax.psum_scatter(grad_ln2_gain, "seq", scatter_dimension=0, tiled=True),
        lax.psum_scatter(grad_ln2_bias, "seq", scatter_dimension=0, tiled=True),
        lax.psum_scatter(grad_w_up, "seq", scatter_dimension=0, tiled=True),
        lax.psum_scatter(grad_bias_up, "seq", scatter_dimension=0, tiled=True),
        lax.psum_scatter(grad_w_down, "seq", scatter_dimension=0, tiled=True),
        lax.psum_scatter(grad_bias_down, "seq", scatter_dimension=0, tiled=True),
    )
    totals = lax.psum(
        (
            shares[0],
            shares[1],
            shares[2],
            shares[3],
            shares[4],
            shares[5],
            shares[6],
            shares[7],
            shares[8],
            shares[9],
            shares[10],
            shares[11],
        ),
        "row",
    )
    return (
        out_frames[None],
        grad_frames[None],
        totals[0],
        totals[1],
        totals[2],
        totals[3],
        totals[4],
        totals[5],
        totals[6],
        totals[7],
        totals[8],
        totals[9],
        totals[10],
        totals[11],
    )


def solution(mesh):
    return jax.shard_map(
        per_device,
        mesh=mesh,
        in_specs=(
            P("row", "seq", None),
            P("row", None),
            P(),
            P(),
            P(),
            P(),
            P(),
            P(),
            P(),
            P(),
            P(),
            P(),
            P(),
            P(),
            P("row", "seq", None),
        ),
        out_specs=(
            P("row", "seq", None),
            P("row", "seq", None),
            P("seq"),
            P("seq"),
            P("seq", None),
            P("seq"),
            P("seq", None),
            P("seq"),
            P("seq"),
            P("seq"),
            P("seq", None),
            P("seq"),
            P("seq", None),
            P("seq"),
        ),
        check_vma=False,
    )
```

profile of v0, /device:TPU:16, one launch (start us, length us, event | category | flops | bytes accessed | tf_op | source)
XLA Modules:
  0.0 1673.9 jit_solution(11242085232375992358)
XLA Ops:
  18.7 73.3 %all-gather.5.cloned.1.call-done = bf16[4096,1024]{1,0:T(8,128)(2,1)} async-done(((bf16[256,1024]{1,0:T(8,128)(2,1)}), bf16[4096,1024]{1,0:T(8,128)(2,1)}) %all-gather.5.cloned.1.call-update) | async-done | bytes 8388624 | tf_op jit(solution)/shard_map/all_gather | solution.py:111
  92.0 11.5 copy.78
  103.6 64.4 %all-gather.3.cloned.1.call-done = bf16[4096,1024]{1,0:T(8,128)(2,1)} async-done(((bf16[256,1024]{1,0:T(8,128)(2,1)}), bf16[4096,1024]{1,0:T(8,128)(2,1)}) %all-gather.3.cloned.1.call-update) | async-done | bytes 8388624 | tf_op jit(solution)/shard_map/all_gather | solution.py:110
  167.9 11.4 copy.76
  180.4 65.7 %while.28 = (s32[]{:T(128)}, f32[256,1024]{0,1:T(8,128)}, f32[256,16]{0,1:T(8,128)S(1)}, f32[256,16]{0,1:T(8,128)S(1)}, s32[8]{0:T(128)S(1)}, /*index=5*/s32[]{:...) while((s32[]{:T(128)}, f32[256,1024]{0,1:T(8,128)}, ...), condition=%wide.region_10.11_spmd.clone, body=%wide.region_5.10_spmd.clone.sunk | while | flops 560866048 | bytes 43267480 | solution.py:143
  183.0 9.0 conditional.6
  254.2 15.6 multiply_convert_fusion
  269.8 12.0 convert_reduce_fusion
  297.6 11.2 broadcast_in_dim.108
  308.8 293.5 %while.29 = (s32[]{:T(128)}, f32[256,1024]{0,1:T(8,128)}, f32[4096,2048]{0,1:T(8,128)}, s32[8]{0:T(128)S(1)}, s32[]{:T(128)}, /*index=5*/s32[]{:T(128)}, s32[256...) while((s32[]{:T(128)}, f32[256,1024]{0,1:T(8,128)}, ...), condition=%wide.region_19.20_spmd.clone, body=%wide.region_16.19_spmd.clone.sunk | while | flops 1365902080 | bytes 74905008 | solution.py:245
  313.2 13.5 conditional.7
  327.9 20.7 %dynamic_update_slice.5 = f32[4096,2048]{0,1:T(8,128)} dynamic-update-slice(f32[4096,2048]{0,1:T(8,128)} %get-tuple-element.916, f32[512,2048]{0,1:T(8,128)} %get-tuple-element.842, s32[]{:T(128)S(6)} %select_n.44, s32[]{:T(128)} %constant.76.clone.1..sunk) | dynamic-update-slice | bytes 8388612 | tf_op jit(solution)/shard_map/while/body/eval_jaxpr/dynamic_update_slice | solution.py:242
  353.0 13.5 conditional.7
  368.9 20.6 %dynamic_update_slice.5 = f32[4096,2048]{0,1:T(8,128)} dynamic-update-slice(f32[4096,2048]{0,1:T(8,128)} %get-tuple-element.916, f32[512,2048]{0,1:T(8,128)} %get-tuple-element.842, s32[]{:T(128)S(6)} %select_n.44, s32[]{:T(128)} %constant.76.clone.1..sunk) | dynamic-update-slice | bytes 8388612 | tf_op jit(solution)/shard_map/while/body/eval_jaxpr/dynamic_update_slice | solution.py:242
  394.0 13.5 conditional.7
  409.9 20.7 %dynamic_update_slice.5 = f32[4096,2048]{0,1:T(8,128)} dynamic-update-slice(f32[4096,2048]{0,1:T(8,128)} %get-tuple-element.916, f32[512,2048]{0,1:T(8,128)} %get-tuple-element.842, s32[]{:T(128)S(6)} %select_n.44, s32[]{:T(128)} %constant.76.clone.1..sunk) | dynamic-update-slice | bytes 8388612 | tf_op jit(solution)/shard_map/while/body/eval_jaxpr/dynamic_update_slice | solution.py:242
  435.0 13.5 conditional.7
  450.9 20.7 %dynamic_update_slice.5 = f32[4096,2048]{0,1:T(8,128)} dynamic-update-slice(f32[4096,2048]{0,1:T(8,128)} %get-tuple-element.916, f32[512,2048]{0,1:T(8,128)} %get-tuple-element.842, s32[]{:T(128)S(6)} %select_n.44, s32[]{:T(128)} %constant.76.clone.1..sunk) | dynamic-update-slice | bytes 8388612 | tf_op jit(solution)/shard_map/while/body/eval_jaxpr/dynamic_update_slice | solution.py:242
  476.1 13.5 conditional.7
  491.9 20.7 %dynamic_update_slice.5 = f32[4096,2048]{0,1:T(8,128)} dynamic-update-slice(f32[4096,2048]{0,1:T(8,128)} %get-tuple-element.916, f32[512,2048]{0,1:T(8,128)} %get-tuple-element.842, s32[]{:T(128)S(6)} %select_n.44, s32[]{:T(128)} %constant.76.clone.1..sunk) | dynamic-update-slice | bytes 8388612 | tf_op jit(solution)/shard_map/while/body/eval_jaxpr/dynamic_update_slice | solution.py:242
  522.1 20.6 %dynamic_update_slice.5 = f32[4096,2048]{0,1:T(8,128)} dynamic-update-slice(f32[4096,2048]{0,1:T(8,128)} %get-tuple-element.916, f32[512,2048]{0,1:T(8,128)} %get-tuple-element.842, s32[]{:T(128)S(6)} %select_n.44, s32[]{:T(128)} %constant.76.clone.1..sunk) | dynamic-update-slice | bytes 8388612 | tf_op jit(solution)/shard_map/while/body/eval_jaxpr/dynamic_update_slice | solution.py:242
  552.3 20.7 %dynamic_update_slice.5 = f32[4096,2048]{0,1:T(8,128)} dynamic-update-slice(f32[4096,2048]{0,1:T(8,128)} %get-tuple-element.916, f32[512,2048]{0,1:T(8,128)} %get-tuple-element.842, s32[]{:T(128)S(6)} %select_n.44, s32[]{:T(128)} %constant.76.clone.1..sunk) | dynamic-update-slice | bytes 8388612 | tf_op jit(solution)/shard_map/while/body/eval_jaxpr/dynamic_update_slice | solution.py:242
  582.5 19.8 %dynamic_update_slice.5 = f32[4096,2048]{0,1:T(8,128)} dynamic-update-slice(f32[4096,2048]{0,1:T(8,128)} %get-tuple-element.916, f32[512,2048]{0,1:T(8,128)} %get-tuple-element.842, s32[]{:T(128)S(6)} %select_n.44, s32[]{:T(128)} %constant.76.clone.1..sunk) | dynamic-update-slice | bytes 8388612 | tf_op jit(solution)/shard_map/while/body/eval_jaxpr/dynamic_update_slice | solution.py:242
  607.2 9.8 fusion.70
  618.0 9.7 fusion.55
  629.0 363.2 %reduce-scatter.6.cloned.1.call-done = f32[256,2048]{0,1:T(8,128)} async-done(((f32[4096,2048]{0,1:T(8,128)}), f32[256,2048]{0,1:T(8,128)}) %reduce-scatter.6.cloned.1.call-update) | async-done | bytes 2097168 | tf_op jit(solution)/shard_map/reduce_scatter | solution.py:247
  1000.9 66.8 %reduce-scatter.10.cloned.1.call-done = f32[64,1024]{1,0:T(8,128)} async-done(((f32[1024,1024]{1,0:T(8,128)}), f32[64,1024]{1,0:T(8,128)}) %reduce-scatter.10.cloned.1.call-update) | async-done | bytes 262160 | tf_op jit(solution)/shard_map/reduce_scatter | solution.py:261
  1067.7 182.1 %reduce-scatter.12.cloned.1.call-done = f32[64,4096]{1,0:T(8,128)} async-done(((f32[1024,4096]{1,0:T(8,128)}), f32[64,4096]{1,0:T(8,128)}) %reduce-scatter.12.cloned.1.call-update) | async-done | bytes 1048592 | tf_op jit(solution)/shard_map/reduce_scatter | solution.py:265
  1249.8 182.1 %reduce-scatter.14.cloned.1.call-done = f32[256,1024]{1,0:T(8,128)} async-done(((f32[4096,1024]{1,0:T(8,128)}), f32[256,1024]{1,0:T(8,128)}) %reduce-scatter.14.cloned.1.call-update) | async-done | bytes 1048592 | tf_op jit(solution)/shard_map/reduce_scatter | solution.py:267
  1432.0 138.7 %reduce-scatter.8.cloned.1.call-done = f32[64,3072]{1,0:T(8,128)} async-done(((f32[1024,3072]{1,0:T(8,128)}), f32[64,3072]{1,0:T(8,128)}) %reduce-scatter.8.cloned.1.call-update) | async-done | bytes 786448 | tf_op jit(solution)/shard_map/reduce_scatter | solution.py:259
  1587.8 44.8 %all-reduce.8 = (f32[1024]{0:T(1024)S(1)}, f32[1024]{0:T(1024)S(1)}, f32[2048]{0:T(1024)S(1)}, f32[1024]{0:T(1024)S(1)}, f32[1024]{0:T(1024)S(1)}, /*index=5*/f3...) all-reduce(f32[1024]{0:T(1024)S(1)} %get-tuple-element.558, ...), channel_id=3, replica_groups=mesh['row'=2,'seq'=16] {'seq'}, use_global_device_ids=true, to_apply=%region_24.25.clone | all-reduce | flops 12288 | bytes 98304
  1639.0 20.8 %all-reduce.13.cloned.1.call-done = (f32[64,3072]{1,0:T(8,128)}, f32[64,1024]{1,0:T(8,128)}, f32[64,4096]{1,0:T(8,128)}, f32[256,1024]{1,0:T(8,128)}) async-done(((f32[64,3072]{1,0:T(8,128)}, f32[64,1024]{1,0:T(8,128)}, f32[64,4096]{1,0:T(8,128)}, f32[256,1024]{1,0:T(8,128)}), (f32[64,3072]{1,0:T(8,128)}, f32[64,1024]{1,0:T(8,128)}, f32[64,4096]{1,0:T(8,128)}, ...) | async-done | bytes 3145744 | tf_op jit(solution)/shard_map/psum | solution.py:270
  (358 shorter events, 271.1 us)
Async XLA Ops:
  7.2 244.8 %copy-start = (bf16[1024,1024]{1,0:T(8,128)(2,1)S(1)}, bf16[1024,1024]{1,0:T(8,128)(2,1)}, u32[]{:S(2)}) copy-start(bf16[1024,1024]{1,0:T(8,128)(2,1)} %param.29) | copy-start | bytes 6291460
  7.2 84.8 %all-gather.5.cloned.1.call-start = ((), (), s32[]{:S(2)}) async-start(), calls=%async_computation.6 | async-start | bytes 8912896 | tf_op jit(solution)/shard_map/all_gather | solution.py:111
  8.6 7.0 copy-start.24
  9.9 5.7 copy-start.26
  16.8 151.2 %all-gather.3.cloned.1.call-start = ((), (), s32[]{:S(2)}) async-start(), calls=%async_computation.5 | async-start | bytes 8912896 | tf_op jit(solution)/shard_map/all_gather | solution.py:110
  17.5 974.7 %reduce-scatter.6.cloned.1.call-start = ((), (), s32[]{:S(2)}) async-start(), calls=%async_computation.7 | async-start | bytes 35651584 | tf_op jit(solution)/shard_map/reduce_scatter | solution.py:247
  246.2 5.8 copy-start.3
  246.2 5.8 copy-start.28
  248.4 5.8 copy-start.19
  248.4 5.8 copy-start.20
  248.4 5.8 copy-start.37
  253.8 35.4 %copy-start.5 = (f32[256,1024]{1,0:T(8,128)}, f32[256,1024]{1,0:T(8,128)S(1)}, u32[]{:S(2)}) copy-start(f32[256,1024]{1,0:T(8,128)S(1)} %get-tuple-element.661) | copy-start | bytes 3145732
  254.2 15.6 copy-start.12
  281.8 7.4 copy-start.15
  602.3 465.5 %reduce-scatter.10.cloned.1.call-start = ((), (), s32[]{:S(2)}) async-start(), calls=%async_computation.9 | async-start | bytes 4456448 | tf_op jit(solution)/shard_map/reduce_scatter | solution.py:261
  606.0 643.8 %reduce-scatter.12.cloned.1.call-start = ((), (), s32[]{:S(2)}) async-start(), calls=%async_computation.10 | async-start | bytes 17825792 | tf_op jit(solution)/shard_map/reduce_scatter | solution.py:265
  617.0 814.9 %reduce-scatter.14.cloned.1.call-start = ((), (), s32[]{:S(2)}) async-start(), calls=%async_computation.11 | async-start | bytes 17825792 | tf_op jit(solution)/shard_map/reduce_scatter | solution.py:267
  627.8 366.2 %copy-start.4 = (bf16[1,256,1024]{2,1,0:T(8,128)(2,1)S(1)}, bf16[1,256,1024]{2,1,0:T(8,128)(2,1)}, u32[]{:S(2)}) copy-start(bf16[1,256,1024]{2,1,0:T(8,128)(2,1)} %param.23) | copy-start | bytes 1572868
  627.8 366.2 %copy-start.22 = (f32[1024]{0:T(1024)S(1)}, f32[1024]{0:T(1024)}, u32[]{:S(2)}) copy-start(f32[1024]{0:T(1024)} %param.25) | copy-start | bytes 12292
  627.8 366.2 %copy-start.23 = (f32[1024]{0:T(1024)S(1)}, f32[1024]{0:T(1024)}, u32[]{:S(2)}) copy-start(f32[1024]{0:T(1024)} %param.26) | copy-start | bytes 12292
  627.8 366.2 %copy-start.25 = (f32[256]{0:T(256)S(1)}, f32[256]{0:T(256)}, u32[]{:S(2)}) copy-start(f32[256]{0:T(256)} %copy-done.24) | copy-start | bytes 3076
  627.8 366.2 %copy-start.27 = (f32[256]{0:T(256)S(1)}, f32[256]{0:T(256)}, u32[]{:S(2)}) copy-start(f32[256]{0:T(256)} %copy-done.26) | copy-start | bytes 3076
  627.8 942.8 %reduce-scatter.8.cloned.1.call-start = ((), (), s32[]{:S(2)}) async-start(), calls=%async_computation.8 | async-start | bytes 13369344 | tf_op jit(solution)/shard_map/reduce_scatter | solution.py:259
  1000.6 570.1 %copy-start.40 = (u32[32]{0:T(128)S(1)}, u32[32]{0:T(128)}, u32[]{:S(2)}) copy-start(u32[32]{0:T(128)} %constant.173) | copy-start | bytes 388
  1000.6 572.6 %copy-start.38 = (f32[1024]{0:T(1024)S(1)}, f32[1024]{0:T(1024)}, u32[]{:S(2)}) copy-start(f32[1024]{0:T(1024)} %param.36) | copy-start | bytes 12292
  1000.6 659.1 %all-reduce.13.cloned.1.call-start = ((), (), s32[]{:S(2)}) async-start(), calls=%async_computation.12 | async-start | bytes 6291456 | tf_op jit(solution)/shard_map/psum | solution.py:270
  1580.9 5.0 copy-start.34
  1580.9 5.6 copy-start.8
  1580.9 5.6 copy-start.14
  1580.9 5.6 copy-start.32
  1586.4 80.4 %copy-start.1 = (bf16[1024,1024]{1,0:T(8,128)(2,1)S(1)}, bf16[1024,1024]{1,0:T(8,128)(2,1)}, u32[]{:S(2)}) copy-start(bf16[1024,1024]{1,0:T(8,128)(2,1)} %param.29) | copy-start | bytes 6291460
  1659.8 6.1 copy-start.16
  (29 other events, 43.8 us)
Sparse Core Ops, SparseCore 0:
  16.9 75.1 all-gather.4
  94.8 73.1 all-gather.2
  602.4 389.8 reduce-scatter.5
  995.9 71.7 reduce-scatter.9
  1072.2 177.5 reduce-scatter.11
  1254.3 177.5 reduce-scatter.13
  1436.5 134.0 reduce-scatter.7
  1573.2 86.4 all-reduce.12
where the time goes:
time: 1690 us; the launch traced here: 1670 us
  waiting for transfers between devices  1090 us (64%)
  local copies, waits for them, and re-layouts  260 us (15%)
  matrix products  145 us (9%)
  other arithmetic  60.4 us (4%)
  blocking collectives  50.5 us (3%)
  loops' own time  48.1 us (3%)
  between operations  16.9 us (1%)
    reduce_scatter x1, waiting for transfers between devices, per_device(): lax.psum_scatter(pair_buffer, 'seq', scatter_dimension=0, tiled=True)  363 us
    reduce_scatter x1, waiting for transfers between devices, per_device(): lax.psum_scatter(grad_w_down, 'seq', scatter_dimension=0, tiled=True)  182 us
    reduce_scatter x1, waiting for transfers between devices, per_device(): lax.psum_scatter(grad_w_up, 'seq', scatter_dimension=0, tiled=True)  182 us
    dynamic_update_slice x8, local copies, waits for them, and re-layouts, key_visit(): lax.dynamic_update_slice(inner[1], pair_add, (block_start, jnp.int32(0)))  164 us
    reduce_scatter x1, waiting for transfers between devices, per_device(): lax.psum_scatter(grad_w_qkv, 'seq', scatter_dimension=0, tiled=True)  139 us
    all_gather x1, waiting for transfers between devices, per_device(): lax.all_gather(value_rows, 'seq', axis=0, tiled=True)  73.3 us
    reduce_scatter x1, waiting for transfers between devices, per_device(): lax.psum_scatter(grad_w_out, 'seq', scatter_dimension=0, tiled=True)  66.8 us
    all_gather x1, waiting for transfers between devices, per_device(): lax.all_gather(key_rows, 'seq', axis=0, tiled=True)  64.4 us
  transfers between devices with their start and end apart: 8, of which 8 were waited for; matrix products, arithmetic and copies ran while one was open for 4% of the time, Pallas kernels for 0%

commit v1 on v0

v1 whole, which is shorter than its diff:
```python
import functools
import math

import jax
import jax.numpy as jnp
from jax import lax
from jax.experimental import pallas as pl
from jax.experimental.pallas import tpu as pltpu
from jax.sharding import PartitionSpec as P

EPSILON = 1e-05
HEADS=16; HEAD_DIM=64; NEGATIVE=-1e30
FWD_TILE=(512,1024); BWD_TILE=(1024,1024)
LOG2E=math.log2(math.e); LN2=math.log(2.0)
BF=jnp.bfloat16; F32=jnp.float32
NT=(((1,),(1,)),((),())); TN=(((0,),(0,)),((),())); NN=(((1,),(0,)),((),()))

def dotf(a,b,dims):
    return lax.dot_general(a,b,dims,preferred_element_type=F32)

def split3(v):
    hi=v.astype(BF); r=v-hi.astype(F32); mid=r.astype(BF); lo=(r-mid.astype(F32)).astype(BF)
    return hi.astype(F32),mid.astype(F32),lo.astype(F32)

def with_tail(base, stat):
    lane=lax.broadcasted_iota(jnp.int32, base.shape, 1)
    hi,mid,lo=split3(stat)
    tail=jnp.where(lane==HEAD_DIM,hi,jnp.where(lane==HEAD_DIM+1,mid,jnp.where(lane==HEAD_DIM+2,lo,0.0)))
    return jnp.where(lane<HEAD_DIM,base,tail).astype(BF)

def seg_start(starts, p, segs):
    best=jnp.int32(0)
    for k in range(segs):
        s=starts[k]
        best=jnp.where(s<=p, jnp.maximum(best,s), best)
    return best

def seg_end(starts, p, segs, full):
    best=jnp.int32(full)
    for k in range(segs):
        s=starts[k]
        best=jnp.where(s>p, jnp.minimum(best,s), best)
    return best

def fwd_kernel(starts, part, x_ref, low_ref, out_ref, qa_ref, ka_ref, va_ref, s_ref, *, bq, bk, segs, group):
    i=pl.program_id(0); full=x_ref.shape[0]
    @pl.when(i==0)
    def _():
        step=512
        def build(t,_):
            rows=pl.ds(pl.multiple_of(t*step,step),step)
            head=x_ref[rows,:128].astype(F32)
            tail=x_ref[rows,128:192].astype(F32)
            lane=lax.broadcasted_iota(jnp.int32,(step,128),1)
            mark=jnp.where(lane<HEAD_DIM+3,-1.0,0.0)
            ka_ref[rows,:]=jnp.where(lane<HEAD_DIM,pltpu.roll(head,64,1),mark).astype(BF)
            va_ref[rows,:]=jnp.where(lane<HEAD_DIM,jnp.concatenate([tail,tail],axis=1),mark).astype(BF)
            return 0
        lax.fori_loop(0,full//step,build,0)
    def skip():
        low_ref[...]=jnp.zeros_like(low_ref); out_ref[...]=jnp.zeros_like(out_ref)
        qa_ref[...]=with_tail(jnp.zeros((bq,128),F32),jnp.full((bq,1),1e30,F32))
    def work():
        a=i*bq; last=a+bq-1
        f0=seg_start(starts,a,segs); f1=seg_start(starts,last,segs)
        lo=f0//bk; hi=last//bk+1
        u0=jnp.minimum((f1+bk-1)//bk,hi); u1=jnp.maximum(u0,(a+1)//bk)
        lane=lax.broadcasted_iota(jnp.int32,(bq,128),1)
        qf=x_ref[pl.ds(pl.multiple_of(a,bq),bq),:128].astype(F32)
        q=jnp.where(lane<HEAD_DIM,qf,0.0)
        qb=q.astype(BF)
        row=a+lax.broadcasted_iota(jnp.int32,(bq,1),0)
        first=jnp.zeros((bq,1),jnp.int32)
        for k in range(segs):
            s=starts[k]; first=jnp.where(s<=row,jnp.maximum(first,s),first)
        def score(j,top,masked):
            s=dotf(qb,ka_ref[pl.ds(pl.multiple_of(j*bk,bk),bk),:],NT)
            if masked:
                key=j*bk+lax.broadcasted_iota(jnp.int32,(bq,bk),1)
                s=jnp.where((key<=row)&(key>=first),s,NEGATIVE)
            s_ref[j]=s
            for c in range(bk//128):
                top=jnp.maximum(top,s[:,c*128:(c+1)*128])
            return top
        top=jnp.full((bq,128),NEGATIVE,F32)
        top=lax.fori_loop(lo,u0,lambda j,t:score(j,t,True),top)
        top=lax.fori_loop(u0,u1,lambda j,t:score(j,t,False),top)
        top=lax.fori_loop(u1,hi,lambda j,t:score(j,t,True),top)
        peak=jnp.max(top,axis=1,keepdims=True)
        def gather(j,acc):
            p=jnp.exp2(s_ref[j]-peak).astype(BF)
            return acc+dotf(p,va_ref[pl.ds(pl.multiple_of(j*bk,bk),bk),:],NN)
        acc=lax.fori_loop(lo,hi,gather,jnp.zeros((bq,128),F32))
        total=-acc[:,HEAD_DIM:HEAD_DIM+1]
        out=acc/total
        out_ref[...]=out[:,:HEAD_DIM]
        low_ref[...]=out[:,:HEAD_DIM].astype(BF)
        qa_ref[...]=with_tail(q,peak+jnp.log2(total))
    if group==1: work()
    else:
        own=(i%group)==part[0]
        pl.when(own)(work); pl.when(jnp.logical_not(own))(skip)

def attend(starts, part, x, *, bq, bk, group):
    full=x.shape[0]; segs=starts.shape[0]
    whole=lambda w: pl.BlockSpec((full,w),lambda i,*_:(0,0))
    blk=lambda w: pl.BlockSpec((bq,w),lambda i,*_:(i,0))
    return pl.pallas_call(
        functools.partial(fwd_kernel,bq=bq,bk=bk,segs=segs,group=group),
        grid_spec=pltpu.PrefetchScalarGridSpec(num_scalar_prefetch=2,grid=(full//bq,),
            in_specs=[whole(192)],
            out_specs=[blk(64),blk(64),blk(128),whole(128),whole(128)],
            scratch_shapes=[pltpu.VMEM((full//bk,bq,bk),F32)]),
        out_shape=[jax.ShapeDtypeStruct((full,64),BF),jax.ShapeDtypeStruct((full,64),F32)]+[jax.ShapeDtypeStruct((full,128),BF)]*3,
        compiler_params=pltpu.CompilerParams(vmem_limit_bytes=50<<20),
        cost_estimate=pl.CostEstimate(flops=full*full*512,bytes_accessed=full*1600,transcendentals=full*full//2),
        name="attend")(starts,part,x)

def bwd_kernel(starts, qa_ref, ka_ref, va_ref, do_ref, out_ref, dx_ref, da_ref, dq_ref, kt_ref, *, bq, bk, segs, variant):
    j=pl.program_id(0); full=qa_ref.shape[0]; nq=full//bq
    @pl.when(j==0)
    def _():
        step=512
        def build(t,_):
            rows=pl.ds(pl.multiple_of(t*step,step),step)
            g=do_ref[rows,:].astype(F32)
            delta=jnp.sum(g*out_ref[rows,:],axis=1,keepdims=True)
            da_ref[rows,:]=with_tail(jnp.concatenate([g,g],axis=1),delta)
            return 0
        lax.fori_loop(0,full//step,build,0)
        def trans(t,_):
            if variant==0:
                kt_ref[t]=ka_ref[pl.ds(pl.multiple_of(t*bk,bk),bk),:].astype(F32).T[:HEAD_DIM].astype(BF)
            return 0
        lax.fori_loop(0,full//bk,trans,0)
        def clear(t,_):
            dq_ref[t]=jnp.zeros(dq_ref.shape[1:],F32)
            return 0
        lax.fori_loop(0,nq,clear,0)
    c=j*bk; d=c+bk
    e0=seg_end(starts,c,segs,full); e1=seg_end(starts,d-1,segs,full)
    lo=c//bq; hi=(e1+bq-1)//bq
    u0=jnp.minimum((d-1+bq-1)//bq,hi); u1=jnp.maximum(u0,e0//bq)
    rows=pl.ds(pl.multiple_of(c,bk),bk)
    ka=ka_ref[rows,:]; va=va_ref[rows,:]
    if variant==0: kt=kt_ref[j]
    def step(i,carry,masked):
        dk,dv=carry
        qrows=pl.ds(pl.multiple_of(i*bq,bq),bq)
        qa=qa_ref[qrows,:]; da=da_ref[qrows,:]
        p=jnp.exp2(dotf(ka,qa,NT))
        if masked:
            row=i*bq+lax.broadcasted_iota(jnp.int32,(1,bq),1)
            first=jnp.zeros((1,bq),jnp.int32)
            for k in range(segs):
                s=starts[k]; first=jnp.where(s<=row,jnp.maximum(first,s),first)
            key=c+lax.broadcasted_iota(jnp.int32,(bk,bq),0)
            p=jnp.where((key<=row)&(key>=first),p,0.0)
        dp=dotf(va,da,NT)
        pb=p.astype(BF); ds=(p*dp).astype(BF)
        dv=dv+dotf(pb,da,NN); dk=dk+dotf(ds,qa,NN)
        if variant==0:
            dq_ref[i]+=dotf(kt,ds,NN)
        else:
            dq_ref[i]+=dotf(ds,ka,TN)
        return dk,dv
    z=jnp.zeros((bk,128),F32)
    carry=lax.fori_loop(lo,u0,lambda i,t:step(i,t,True),(z,z))
    carry=lax.fori_loop(u0,u1,lambda i,t:step(i,t,False),carry)
    dk,dv=lax.fori_loop(u1,hi,lambda i,t:step(i,t,True),carry)
    dx_ref[rows,64:128]=(dk[:,:HEAD_DIM]*LN2).astype(BF)
    dx_ref[rows,128:192]=dv[:,:HEAD_DIM].astype(BF)
    @pl.when(j==pl.num_programs(0)-1)
    def _():
        def fin(t,_):
            r=pl.ds(pl.multiple_of(t*bq,bq),bq)
            g=dq_ref[t]
            if variant==0: g=g.T
            dx_ref[r,0:64]=(g[:,:HEAD_DIM]*HEAD_DIM**-0.5).astype(BF)
            return 0
        lax.fori_loop(0,nq,fin,0)

def attend_back(starts, qa, ka, va, do, out, *, bq, bk, variant=0):
    full=qa.shape[0]; segs=starts.shape[0]
    whole=lambda w: pl.BlockSpec((full,w),lambda i,*_:(0,0))
    return pl.pallas_call(
        functools.partial(bwd_kernel,bq=bq,bk=bk,segs=segs,variant=variant),
        grid_spec=pltpu.PrefetchScalarGridSpec(num_scalar_prefetch=1,grid=(full//bk,),
            in_specs=[whole(128)]*3+[whole(64)]*2, out_specs=whole(192),
            scratch_shapes=[pltpu.VMEM((full,128),BF),
              pltpu.VMEM((full//bq,64,bq) if variant==0 else (full//bq,bq,128),F32),pltpu.VMEM((full//bk,64,bk),BF)]),
        out_shape=jax.ShapeDtypeStruct((full,192),BF),
        compiler_params=pltpu.CompilerParams(vmem_limit_bytes=50<<20),
        cost_estimate=pl.CostEstimate(flops=full*full*1280,bytes_accessed=full*2000,transcendentals=full*full//2),
        name="attend_back")(starts,qa,ka,va,do,out)

def statistics(values):
    centre = jnp.mean(values, axis=-1, keepdims=True)
    centred = values - centre
    second = jnp.mean(centred * centred, axis=-1, keepdims=True)
    scale = lax.rsqrt(second + EPSILON)
    return centred * scale, scale


def norm_back(unit, scale, gain, grad):
    scaled = grad * gain
    first = jnp.mean(scaled, axis=-1, keepdims=True)
    second = jnp.mean(scaled * unit, axis=-1, keepdims=True)
    return (scaled - first - unit * second) * scale


def row_sum(value):
    low = lax.optimization_barrier(value.astype(BF))
    if lax.axis_size("row") == 2:
        return low.astype(F32) + lax.ppermute(low, "row", [(0, 1), (1, 0)]).astype(F32)
    return lax.psum(low.astype(F32), "row")


def exchange(value):
    return lax.all_to_all(value, "seq", 0, 0, tiled=True)


def scatter_sum(value):
    return row_sum(lax.psum_scatter(value.astype(BF), "seq", scatter_dimension=0, tiled=True).astype(F32))


def per_device(
    frames,
    seg_lengths,
    ln1_gain,
    ln1_bias,
    w_qkv,
    bias_qv,
    w_out,
    bias_out,
    ln2_gain,
    ln2_bias,
    w_up,
    bias_up,
    w_down,
    bias_down,
    grad_out,
):
    tokens, feature = frames.shape[1:]
    ranks = lax.axis_size("seq")
    me = lax.axis_index("seq")
    group = max(1, ranks // HEADS)
    full = ranks * tokens
    share = feature // ranks
    lengths = seg_lengths[0]
    starts = jnp.cumsum(lengths, dtype=jnp.int32) - lengths
    part = (me % group).astype(jnp.int32)[None]

    def to_heads(value):
        value = value.reshape(tokens, -1, HEADS, HEAD_DIM).transpose(2, 0, 1, 3)
        value = value.reshape(HEADS, tokens, -1)
        return jnp.repeat(value, group, axis=0) if group > 1 else value

    def fold(value):
        if group == 1:
            return value
        value = value.reshape((HEADS, group) + value.shape[1:])
        return jnp.sum(value.astype(F32), axis=1).astype(value.dtype)

    def from_heads(value):
        rows = value.shape[1]
        value = value.reshape(HEADS, rows, -1, HEAD_DIM).transpose(1, 2, 0, 3)
        return value.reshape(rows, -1)

    stream = frames[0].astype(F32)
    unit_one, scale_one = statistics(stream)
    normed_low = (unit_one * ln1_gain + ln1_bias).astype(BF)
    normed_all = lax.all_gather(normed_low, "seq", axis=0, tiled=True)
    bias_full = jnp.concatenate(
        [bias_qv[:feature], jnp.zeros((feature,), F32), bias_qv[feature:]]
    )
    column_scale = jnp.where(lax.iota(jnp.int32, 3 * feature) < feature, LOG2E * HEAD_DIM**-0.5, 1.0)
    projected = ((dotf(normed_low, w_qkv, NN) + bias_full) * column_scale).astype(BF)
    packed = exchange(to_heads(projected)).reshape(full, 3 * HEAD_DIM)
    low, out, qa, ka, va = attend(starts, part, packed, bq=FWD_TILE[0], bk=FWD_TILE[1], group=group)
    attended_low = from_heads(fold(exchange(low.reshape(ranks, tokens, HEAD_DIM))))

    residual = stream + (dotf(attended_low, w_out, NN) + bias_out)
    unit_two, scale_two = statistics(residual)
    normed_two_low = (unit_two * ln2_gain + ln2_bias).astype(BF)
    up_proj = dotf(normed_two_low, w_up, NN) + bias_up
    phi = 0.5 * (1.0 + lax.erf(up_proj * (0.5**0.5)))
    hidden = (up_proj * phi).astype(BF)
    slope = phi + up_proj * jnp.exp(-0.5 * up_proj * up_proj) * (1.0 / math.sqrt(2.0 * math.pi))
    out_frames = (residual + (dotf(hidden, w_down, NN) + bias_down)).astype(BF)
    cot_low = grad_out[0]
    cot = cot_low.astype(F32)
    up_grad = (dotf(cot_low, w_down, NT) * slope).astype(BF)
    normed_two_grad = dotf(up_grad, w_up, NT)
    residual_grad = cot + norm_back(unit_two, scale_two, ln2_gain, normed_two_grad)
    branch_grad = residual_grad.astype(BF)
    attended_grad = dotf(branch_grad, w_out, NT).astype(BF)

    def piece(value):
        return value.reshape(ranks, -1)

    smalls = jnp.concatenate(
        [
            piece(jnp.sum(normed_two_grad * unit_two, axis=0)),
            piece(jnp.sum(normed_two_grad, axis=0)),
            piece(jnp.sum(branch_grad, axis=0, dtype=F32)),
            piece(jnp.sum(up_grad, axis=0, dtype=F32)),
            piece(jnp.sum(cot, axis=0)),
        ],
        axis=1,
    ).astype(BF)
    extra = smalls.shape[1] // HEAD_DIM
    sent = jnp.concatenate([to_heads(attended_grad), smalls.reshape(ranks, extra, HEAD_DIM)], axis=1)
    got = exchange(sent)
    small_total = row_sum(jnp.sum(got[:, tokens:].astype(F32), axis=0).reshape(-1))
    grad_heads = got[:, :tokens].reshape(full, HEAD_DIM)

    total_down = scatter_sum(dotf(hidden, cot_low, TN))
    total_up = scatter_sum(dotf(normed_two_low, up_grad, TN))
    total_out = scatter_sum(dotf(attended_low, branch_grad, TN))

    dx = attend_back(starts, qa, ka, va, grad_heads, out, bq=BWD_TILE[0], bk=BWD_TILE[1])
    projected_grad = from_heads(fold(exchange(dx.reshape(ranks, tokens, 3 * HEAD_DIM))))
    normed_grad = dotf(projected_grad, w_qkv, NT)
    grad_frames = (residual_grad + norm_back(unit_one, scale_one, ln1_gain, normed_grad)).astype(BF)

    columns = jnp.sum(dx, axis=0, dtype=F32)
    columns_high = lax.reduce_precision(columns, 8, 7)
    marks = jnp.stack([columns_high, columns - columns_high] + [jnp.zeros_like(columns)] * 6)
    weight_part = dotf(normed_all, dx, TN).reshape(ranks, share, 3 * HEAD_DIM)
    message = jnp.concatenate(
        [weight_part, jnp.broadcast_to(marks[None], (ranks, 8, 3 * HEAD_DIM))], axis=1
    ).astype(BF)
    mine = from_heads(fold(exchange(message)))
    mine_total = row_sum(mine.astype(F32))
    grad_w_qkv = mine_total[:share]
    column_total = mine_total[share] + mine_total[share + 1]
    grad_bias_qv = jnp.concatenate([column_total[:feature], column_total[2 * feature :]])
    grad_bias_qv = lax.dynamic_slice(grad_bias_qv, (me * 2 * share,), (2 * share,))
    my_rows = lax.dynamic_slice(w_qkv, (me * share, 0), (share, 3 * feature)).astype(F32)
    my_gain = lax.dynamic_slice(ln1_gain, (me * share,), (share,))
    my_bias = lax.dynamic_slice(ln1_bias, (me * share,), (share,))
    grad_ln1_bias = jnp.sum(my_rows * column_total, axis=1)
    grad_ln1_gain = (jnp.sum(my_rows * grad_w_qkv, axis=1) - my_bias * grad_ln1_bias) / my_gain

    wide = w_up.shape[1] // ranks
    ends = [share, 2 * share, 3 * share, 3 * share + wide]
    grad_ln2_gain, grad_ln2_bias, grad_bias_out, grad_bias_up, grad_bias_down = jnp.split(small_total, ends)
    return (
        out_frames[None],
        grad_frames[None],
        grad_ln1_gain,
        grad_ln1_bias,
        grad_w_qkv,
        grad_bias_qv,
        total_out,
        grad_bias_out,
        grad_ln2_gain,
        grad_ln2_bias,
        total_up,
        grad_bias_up,
        total_down,
        grad_bias_down,
    )


def solution(mesh):
    frames_spec = P("row", "seq", None)
    vector, matrix = P("seq"), P("seq", None)
    return jax.shard_map(
        per_device,
        mesh=mesh,
        in_specs=(frames_spec, P("row", None)) + (P(),) * 12 + (frames_spec,),
        out_specs=(
            frames_spec,
            frames_spec,
            vector,
            vector,
            matrix,
            vector,
            matrix,
            vector,
            vector,
            vector,
            matrix,
            vector,
            matrix,
            vector,
        ),
        check_vma=False,
    )
```

time: 1690 us -> 564 us (0.33)
  waiting for transfers between devices: 1090 us -> 279 us
  local copies, waits for them, and re-layouts: 260 us -> 34 us
  matrix products: 145 us -> 59.9 us
  Pallas kernels: 0 us -> 68.8 us
  loops' own time: 48.1 us -> 0 us
  other arithmetic: 60.4 us -> 24.2 us
  starting transfers between devices: 0.71 us -> 24.1 us
    reduce_scatter x5 -> x3, waiting for transfers between devices: 933 us -> 179 us  [scatter_sum(): lax.psum_scatter(value.astype(BF), 'seq', scatter_dimension=0, tiled=True)]
    dynamic_update_slice x8 -> x0, local copies, waits for them, and re-layouts: 164 us -> none  [key_visit(): lax.dynamic_update_slice(inner[1], pair_add, (block_start, jnp.int32(0)))]
    all_gather x2 -> x1, waiting for transfers between devices: 138 us -> 0.01 us  [per_device(): normed_all = lax.all_gather(normed_low, 'seq', axis=0, tiled=True)]
    all_to_all x0 -> x3, waiting for transfers between devices: none -> 90.9 us  [exchange(): return lax.all_to_all(value, 'seq', 0, 0, tiled=True)]
    dot_general x47 -> x12, matrix products: 145 us -> 59.9 us  [dotf(): return lax.dot_general(a, b, dims, preferred_element_type=F32)]
    pallas_call x0 -> x2, Pallas kernels: none -> 68.8 us  [the longest x1 39.6 us: attend_back(): pl.pallas_call(functools.partial(bwd_kernel, bq=bq, bk=bk, segs=segs, var...]
    all_to_all x0 -> x2, blocking collectives: none -> 50.3 us  [exchange(): return lax.all_to_all(value, 'seq', 0, 0, tiled=True)]
    another operation x18 -> x0, loops' own time: 48.1 us -> none  [the longest x1 31.2 us: per_device(): carried, unused_out = lax.scan(key_visit, carried, blocks)]
  transfers between devices with their start and end apart: 8 -> 12, of which waited for: 8 -> 8; matrix products, arithmetic and copies ran while one was open for 4% -> 13% of each run, Pallas kernels for 0% -> 7%
where the time goes in v1:
time: 564 us; the launch traced here: 555 us
  waiting for transfers between devices  279 us (49%)
  Pallas kernels  68.8 us (12%)
  matrix products  59.9 us (11%)
  blocking collectives  50.3 us (9%)
  local copies, waits for them, and re-layouts  34 us (6%)
  other arithmetic  24.2 us (4%)
  starting transfers between devices  24.1 us (4%)
  between operations  14.6 us (3%)
    reduce_scatter x3, waiting for transfers between devices, scatter_sum(): lax.psum_scatter(value.astype(BF), 'seq', scatter_dimension=0, tiled=True)  179 us
    all_to_all x3, waiting for transfers between devices, exchange(): return lax.all_to_all(value, 'seq', 0, 0, tiled=True)  90.9 us
    dot_general x12, matrix products, dotf(): return lax.dot_general(a, b, dims, preferred_element_type=F32)  59.9 us
    all_to_all x2, blocking collectives, exchange(): return lax.all_to_all(value, 'seq', 0, 0, tiled=True)  50.3 us
    pallas_call x1, Pallas kernels, attend_back(): pl.pallas_call(functools.partial(bwd_kernel, bq=bq, bk=bk, segs=segs, var...  39.6 us
    pallas_call x1, Pallas kernels, attend(): pl.pallas_call(functools.partial(fwd_kernel, bq=bq, bk=bk, segs=segs, gro...  29.1 us
    all_to_all x3, starting transfers between devices, exchange(): return lax.all_to_all(value, 'seq', 0, 0, tiled=True)  16.7 us
  transfers between devices with their start and end apart: 12, of which 8 were waited for; matrix products, arithmetic and copies ran while one was open for 13% of the time, Pallas kernels for 7%

profile of v1, /device:TPU:16, one launch (start us, length us, event | category | flops | bytes accessed | tf_op | source)
XLA Modules:
  0.0 555.3 jit_solution(10272306654414178261)
XLA Ops:
  12.0 5.9 %fusion.6 = bf16[256,3072]{1,0:T(8,128)(2,1)} fusion(bf16[256,1024]{1,0:T(8,128)(2,1)S(1)} %fusion.18, bf16[1024,3072]{1,0:T(8,128)(2,1)} %param.19, f32[3072]{0:T(1024)S(1)} %get-tuple-element.54, f32[3072]{0:T(1024)S(1)} %get-tuple-element.53), kind=kOutput, calls=%fused_computation.15 | convolution fusion | flops 1612972032 | bytes 8413184 | tf_op jit(solution)/shard_map/dot_general | solution.py:19
  17.9 2.6 copy.66
  20.5 2.7 copy.67
  23.2 6.2 %all-to-all-start = ((bf16[16,256,192]{1,2,0:T(8,128)(2,1)}), bf16[16,256,192]{1,2,0:T(8,128)(2,1)}, u32[]{:S(2)}, u32[]{:S(2)}) async-start(bf16[16,256,192]{1,2,0:T(8,128)(2,1)} %bitcast.104), calls=%async_computation | async-start | bytes 3145728 | tf_op jit(solution)/shard_map/all_to_all | solution.py:220
  29.6 36.3 %all-to-all-done = bf16[16,256,192]{1,2,0:T(8,128)(2,1)} async-done(((bf16[16,256,192]{1,2,0:T(8,128)(2,1)}), bf16[16,256,192]{1,2,0:T(8,128)(2,1)}, u32[]{:S(2)}, u32[]{:S(2)}) %all-to-all-start) | async-done | bytes 1572896 | tf_op jit(solution)/shard_map/all_to_all | solution.py:220
  65.9 3.7 copy.68
  69.6 29.1 %attend.1 = (bf16[4096,64]{1,0:T(8,128)(2,1)S(1)}, f32[4096,64]{1,0:T(8,128)}, bf16[4096,128]{1,0:T(8,128)(2,1)S(1)}, bf16[4096,128]{1,0:T(8,128)(2,1)S(1)}, bf16[4096,128]{1,0:T(8,128)(2,1)}) custom-call(s32[4]{0:T(128)S(1)} %bitcast_subtract_fusion.starts, s32[1]{0:T(128)} %constant.24.clone.1.part, bf16[4096,192]{1,0:T(8,128)(2,1)} %bitcast.109), custom_call_target="tpu_custom_call" | custom-call | flops 8589934592 | bytes 6553600 | tf_op jit(solution)/shard_map/attend/pallas_call | solution.py:108
  101.8 18.7 %all_to_all.25 = bf16[16,256,64]{1,2,0:T(8,128)(2,1)S(1)} all-to-all(bf16[16,256,64]{1,2,0:T(8,128)(2,1)} %copy.69), channel_id=1, replica_groups=mesh['row'=2,'seq'=16] {'seq'}, dimensions={0} | all-to-all | bytes 1048576 | tf_op jit(solution)/shard_map/all_to_all | solution.py:220
  122.8 7.0 %multiply_convert_fusion = (bf16[256,4096]{1,0:T(8,128)(2,1)}, f32[256,4096]{1,0:T(8,128)S(1)}) fusion(f32[4096]{0:T(1024)S(1)} %copy-done.24, bf16[1024,4096]{1,0:T(8,128)(2,1)} %param.25, f32[256,1024]{1,0:T(8,128)S(1)} %get-tuple-element.46, f32[1024]{0:T(1024)S(1)} %copy-done.20, f32[1024]{0:T(1024)S(1)} %copy-done.19, f32[256]{0:T(256)S(1)} %add_rsqrt_fusion, ...), kind=kOutput, calls=%fused_computation.11 | convolution fusion | flops 2155085824 | bytes 15755264 | tf_op jit(solution)/shard_map/dot_general | solution.py:19
  129.8 4.2 fusion.40
  134.1 2.7 multiply_reduce_fusion
  141.1 7.4 %convolution_convert_fusion.1 = bf16[1024,4096]{1,0:T(8,128)(2,1)} fusion(bf16[256,4096]{1,0:T(8,128)(2,1)} %copy-done.16, f32[256,1024]{1,0:T(8,128)S(1)} %get-tuple-element.46, f32[1024]{0:T(1024)S(1)} %copy-done.20, f32[1024]{0:T(1024)S(1)} %copy-done.19, f32[256]{0:T(256)S(1)} %add_rsqrt_fusion, f32[256]{0:T(256)S(1)} %broadcast_multiply_fusion.4), kind=kOutput, calls=%fused_computation.1 | convolution fusion | flops 2152988672 | bytes 11544576 | tf_op jit(solution)/shard_map/dot_general | solution.py:19
  149.6 7.3 %convolution_convert_fusion = bf16[4096,1024]{1,0:T(8,128)(2,1)} fusion(bf16[256,4096]{1,0:T(8,128)(2,1)} %get-tuple-element.47, bf16[1,256,1024]{2,1,0:T(8,128)(2,1)S(1)} %copy-done.14), kind=kOutput, calls=%fused_computation | convolution fusion | flops 2151677952 | bytes 11010048 | tf_op jit(solution)/shard_map/dot_general | solution.py:19
  160.4 2.2 copy.70
  163.7 31.6 %all_to_all.26 = bf16[16,264,64]{1,2,0:T(8,128)(2,1)S(1)} all-to-all(bf16[16,264,64]{1,2,0:T(8,128)(2,1)S(1)} %pad_maximum_fusion), channel_id=1, replica_groups=mesh['row'=2,'seq'=16] {'seq'}, dimensions={0} | all-to-all | bytes 1081344 | tf_op jit(solution)/shard_map/all_to_all | solution.py:220
  197.1 2.4 copy.72
  199.5 39.6 %attend_back.1 = bf16[4096,192]{1,0:T(8,128)(2,1)} custom-call(s32[4]{0:T(128)S(1)} %bitcast_subtract_fusion.starts, bf16[4096,128]{1,0:T(8,128)(2,1)S(1)} %copy-done.3, bf16[4096,128]{1,0:T(8,128)(2,1)S(1)} %copy-done.5, bf16[4096,128]{1,0:T(8,128)(2,1)S(1)} %copy-done.6, bf16[4096,64]{1,0:T(8,128)(2,1)} %bitcast.113, f32[4096,64]{1,0:T(8,128)} %get-tuple-element.23.out_ref), custom_call_target="tpu_custom_call" | custom-call | flops 21474836480 | bytes 8192000 | tf_op jit(solution)/shard_map/attend_back/pallas_call | solution.py:186
  239.2 4.0 copy.73
  243.2 5.8 %all-to-all-start.3 = ((bf16[16,256,192]{1,2,0:T(8,128)(2,1)}), bf16[16,256,192]{1,2,0:T(8,128)(2,1)}, u32[]{:S(2)}, u32[]{:S(2)}) async-start(bf16[16,256,192]{1,2,0:T(8,128)(2,1)} %copy.73), calls=%async_computation.3 | async-start | bytes 3145728 | tf_op jit(solution)/shard_map/all_to_all | solution.py:220
  249.2 7.2 %fusion.16 = bf16[1,256,1024]{2,1,0:T(8,128)(2,1)} fusion(f32[256,1024]{1,0:T(8,128)S(1)} %copy-done.8, bf16[256,4096]{1,0:T(8,128)(2,1)} %get-tuple-element.47, bf16[4096,1024]{1,0:T(8,128)(2,1)} %param.27, f32[1024]{0:T(1024)S(1)} %copy-done.25), kind=kOutput, calls=%fused_computation.33 | convolution fusion | flops 2148270080 | bytes 12062720 | tf_op jit(solution)/shard_map/dot_general | solution.py:19
  258.8 2.1 convert_reduce_fusion
  263.6 3.5 collective-permute-done.1
  268.8 46.1 %all-to-all-done.3 = bf16[16,256,192]{1,2,0:T(8,128)(2,1)} async-done(((bf16[16,256,192]{1,2,0:T(8,128)(2,1)}), bf16[16,256,192]{1,2,0:T(8,128)(2,1)}, u32[]{:S(2)}, u32[]{:S(2)}) %all-to-all-start.3) | async-done | bytes 1572896 | tf_op jit(solution)/shard_map/all_to_all | solution.py:220
  314.9 2.7 copy.74
  317.7 5.9 %convolution_convert_fusion.4 = bf16[1024,192]{0,1:T(8,128)(2,1)S(1)} fusion(bf16[4096,1024]{1,0:T(8,128)(2,1)} %all-gather.2.cloned.1.call-done, bf16[4096,192]{1,0:T(8,128)(2,1)} %attend_back.1), kind=kOutput, calls=%fused_computation.27 | convolution fusion | flops 1610809344 | bytes 10354688 | tf_op jit(solution)/shard_map/dot_general | solution.py:19
  324.7 4.7 all-to-all-start.4
  329.4 6.9 %fusion.34 = (f32[256]{0:T(256)S(1)}, f32[256]{0:T(256)S(1)}, f32[256,1024]{1,0:T(8,128)}) fusion(f32[256]{0:T(256)S(1)} %add_rsqrt_fusion.1, f32[256]{0:T(256)S(1)} %broadcast_multiply_fusion.5, bf16[1,256,1024]{2,1,0:T(8,128)(2,1)S(1)} %copy-done.12, f32[1024]{0:T(1024)S(1)} %copy-done.22, bf16[256,3072]{0,1:T(8,128)(2,1)} %bitcast.112, ...), kind=kOutput, calls=%fused_computation.86 | convolution fusion | flops 1612447232 | bytes 9445376 | tf_op jit(solution)/shard_map/dot_general | solution.py:19
  336.3 8.5 %all-to-all-done.4 = bf16[16,72,192]{2,1,0:T(8,128)(2,1)} async-done(((bf16[16,72,192]{2,1,0:T(8,128)(2,1)}), bf16[16,72,192]{2,1,0:T(8,128)(2,1)}, u32[]{:S(2)}, u32[]{:S(2)}) %all-to-all-start.4) | async-done | bytes 442400 | tf_op jit(solution)/shard_map/all_to_all | solution.py:220
  350.1 2.7 fusion.27
  352.8 71.5 %reduce-scatter.6.cloned.1.call-done = bf16[64,4096]{1,0:T(8,128)(2,1)} async-done(((bf16[1024,4096]{1,0:T(8,128)(2,1)}), bf16[64,4096]{1,0:T(8,128)(2,1)}) %reduce-scatter.6.cloned.1.call-update) | async-done | bytes 524304 | tf_op jit(solution)/shard_map/reduce_scatter | solution.py:224
  425.8 107.5 %reduce-scatter.8.cloned.1.call-done = bf16[256,1024]{1,0:T(8,128)(2,1)} async-done(((bf16[4096,1024]{1,0:T(8,128)(2,1)}), bf16[256,1024]{1,0:T(8,128)(2,1)}) %reduce-scatter.8.cloned.1.call-update) | async-done | bytes 524304 | tf_op jit(solution)/shard_map/reduce_scatter | solution.py:224
  542.1 5.1 collective-permute-done.4
  (142 shorter events, 46.7 us)
Async XLA Ops:
  7.2 113.4 %copy-start = (bf16[1024,1024]{1,0:T(8,128)(2,1)S(1)}, bf16[1024,1024]{1,0:T(8,128)(2,1)}, u32[]{:S(2)}) copy-start(bf16[1024,1024]{1,0:T(8,128)(2,1)} %param.21) | copy-start | bytes 6291460
  17.9 11.5 %copy-start.26 = (s32[1,4]{1,0:T(1,128)S(1)}, s32[1,4]{1,0:T(1,128)}, u32[]{:S(2)}) copy-start(s32[1,4]{1,0:T(1,128)} %param.16) | copy-start | bytes 52
  23.2 42.7 %all-to-all-start = ((bf16[16,256,192]{1,2,0:T(8,128)(2,1)}), bf16[16,256,192]{1,2,0:T(8,128)(2,1)}, u32[]{:S(2)}, u32[]{:S(2)}) async-start(bf16[16,256,192]{1,2,0:T(8,128)(2,1)} %bitcast.104), calls=%async_computation | async-start | bytes 3145728 | tf_op jit(solution)/shard_map/all_to_all | solution.py:220
  29.4 232.4 %reduce-scatter.4.cloned.1.call-start = ((), (), s32[]{:S(2)}) async-start(), calls=%async_computation.9 | async-start | bytes 2228224 | tf_op jit(solution)/shard_map/reduce_scatter | solution.py:224
  69.6 51.0 %copy-start.21 = (f32[1024]{0:T(1024)S(1)}, f32[1024]{0:T(1024)}, u32[]{:S(2)}) copy-start(f32[1024]{0:T(1024)} %param.22) | copy-start | bytes 12292
  100.7 22.0 %copy-start.19 = (f32[1024]{0:T(1024)S(1)}, f32[1024]{0:T(1024)}, u32[]{:S(2)}) copy-start(f32[1024]{0:T(1024)} %param.23) | copy-start | bytes 12292
  100.7 22.0 %copy-start.20 = (f32[1024]{0:T(1024)S(1)}, f32[1024]{0:T(1024)}, u32[]{:S(2)}) copy-start(f32[1024]{0:T(1024)} %param.24) | copy-start | bytes 12292
  100.7 22.0 %copy-start.24 = (f32[4096]{0:T(1024)S(1)}, f32[4096]{0:T(1024)}, u32[]{:S(2)}) copy-start(f32[4096]{0:T(1024)} %param.26) | copy-start | bytes 49156
  122.4 18.7 %copy-start.7 = (f32[256,1024]{1,0:T(8,128)}, f32[256,1024]{1,0:T(8,128)S(1)}, u32[]{:S(2)}) copy-start(f32[256,1024]{1,0:T(8,128)S(1)} %get-tuple-element.46) | copy-start | bytes 3145732
  122.5 7.4 %slice-start.2 = ((s8[8388608]{0:T(1024)(128)(4,1)}), s8[4194304]{0:T(1024)(128)(4,1)S(1)}, s32[]{:S(2)}) async-start(s8[8388608]{0:T(1024)(128)(4,1)} %bitcast.120), calls=%async_computation.14 | async-start | bytes 8388608
  122.8 11.3 %slice-start = ((s8[8388608]{0:T(1024)(128)(4,1)}), s8[4194304]{0:T(1024)(128)(4,1)S(1)}, s32[]{:S(2)}) async-start(s8[8388608]{0:T(1024)(128)(4,1)} %bitcast.118), calls=%async_computation.12 | async-start | bytes 8388608
  140.3 177.3 %all-gather.2.cloned.1.call-start = ((), (), s32[]{:S(2)}) async-start(), calls=%async_computation.8 | async-start | bytes 8912896 | tf_op jit(solution)/shard_map/all_gather | solution.py:273
  141.1 283.2 %reduce-scatter.6.cloned.1.call-start = ((), (), s32[]{:S(2)}) async-start(), calls=%async_computation.10 | async-start | bytes 8912896 | tf_op jit(solution)/shard_map/reduce_scatter | solution.py:224
  148.5 384.7 %reduce-scatter.8.cloned.1.call-start = ((), (), s32[]{:S(2)}) async-start(), calls=%async_computation.11 | async-start | bytes 8912896 | tf_op jit(solution)/shard_map/reduce_scatter | solution.py:224
  160.4 39.1 %copy-start.3 = (bf16[4096,128]{1,0:T(8,128)(2,1)S(1)}, bf16[4096,128]{1,0:T(8,128)(2,1)}, u32[]{:S(2)}) copy-start(bf16[4096,128]{1,0:T(8,128)(2,1)} %copy-done.2) | copy-start | bytes 3145732
  160.4 39.1 %copy-start.5 = (bf16[4096,128]{1,0:T(8,128)(2,1)S(1)}, bf16[4096,128]{1,0:T(8,128)(2,1)}, u32[]{:S(2)}) copy-start(bf16[4096,128]{1,0:T(8,128)(2,1)} %copy-done.4) | copy-start | bytes 3145732
  160.4 39.1 %copy-start.6 = (bf16[4096,128]{1,0:T(8,128)(2,1)S(1)}, bf16[4096,128]{1,0:T(8,128)(2,1)}, u32[]{:S(2)}) copy-start(bf16[4096,128]{1,0:T(8,128)(2,1)} %get-tuple-element.22.va_ref) | copy-start | bytes 3145732
  239.2 10.0 %copy-start.8 = (f32[256,1024]{1,0:T(8,128)S(1)}, f32[256,1024]{1,0:T(8,128)}, u32[]{:S(2)}) copy-start(f32[256,1024]{1,0:T(8,128)} %copy-done.7) | copy-start | bytes 3145732
  239.2 10.0 %copy-start.25 = (f32[1024]{0:T(1024)S(1)}, f32[1024]{0:T(1024)}, u32[]{:S(2)}) copy-start(f32[1024]{0:T(1024)} %param.28) | copy-start | bytes 12292
  243.2 71.8 %all-to-all-start.3 = ((bf16[16,256,192]{1,2,0:T(8,128)(2,1)}), bf16[16,256,192]{1,2,0:T(8,128)(2,1)}, u32[]{:S(2)}, u32[]{:S(2)}) async-start(bf16[16,256,192]{1,2,0:T(8,128)(2,1)} %copy.73), calls=%async_computation.3 | async-start | bytes 3145728 | tf_op jit(solution)/shard_map/all_to_all | solution.py:220
  257.5 3.6 collective-permute-start.2
  261.7 5.4 collective-permute-start.1
  317.6 11.8 %copy-start.12 = (bf16[1,256,1024]{2,1,0:T(8,128)(2,1)S(1)}, bf16[1,256,1024]{2,1,0:T(8,128)(2,1)}, u32[]{:S(2)}) copy-start(bf16[1,256,1024]{2,1,0:T(8,128)(2,1)} %param.15) | copy-start | bytes 1572868
  317.7 11.8 %copy-start.22 = (f32[1024]{0:T(1024)S(1)}, f32[1024]{0:T(1024)}, u32[]{:S(2)}) copy-start(f32[1024]{0:T(1024)} %param.17) | copy-start | bytes 12292
  324.7 20.1 %all-to-all-start.4 = ((bf16[16,72,192]{2,1,0:T(8,128)(2,1)}), bf16[16,72,192]{2,1,0:T(8,128)(2,1)}, u32[]{:S(2)}, u32[]{:S(2)}) async-start(bf16[16,72,192]{2,1,0:T(8,128)(2,1)} %pad_maximum_fusion.1), calls=%async_computation.4 | async-start | bytes 1179648 | tf_op jit(solution)/shard_map/all_to_all | solution.py:220
  336.3 13.8 %copy-start.11 = (f32[256,1024]{1,0:T(8,128)S(1)}, f32[256,1024]{1,0:T(8,128)}, u32[]{:S(2)}) copy-start(f32[256,1024]{1,0:T(8,128)} %copy-done.9) | copy-start | bytes 3145732
  348.4 186.3 %collective-permute-start = (bf16[72,3072]{1,0:T(8,128)(2,1)}, bf16[72,3072]{1,0:T(8,128)(2,1)}, u32[]{:S(2)}, u32[]{:S(2)}) collective-permute-start(bf16[72,3072]{1,0:T(8,128)(2,1)} %reshape.219), channel_id=1, source_target_pairs={{0,16},{16,0},{1,17},{17,1},{2,18},{18,2},{3,19},{19,3},{4,20},{20... | collective-permute-start | bytes 1327112 | tf_op jit(solution)/shard_map/ppermute | solution.py:215
  350.1 198.2 %copy-start.1 = (bf16[1024,1024]{1,0:T(8,128)(2,1)S(1)}, bf16[1024,1024]{1,0:T(8,128)(2,1)}, u32[]{:S(2)}) copy-start(bf16[1024,1024]{1,0:T(8,128)(2,1)} %param.21) | copy-start | bytes 6291460
  424.3 115.7 %collective-permute-start.3 = (bf16[64,4096]{1,0:T(8,128)(2,1)}, bf16[64,4096]{1,0:T(8,128)(2,1)S(1)}, u32[]{:S(2)}, u32[]{:S(2)}) collective-permute-start(bf16[64,4096]{1,0:T(8,128)(2,1)} %reduce-scatter.6.cloned.1.call-done), channel_id=1, source_target_pairs={{0,16},{16,0},{1,17},{17,1},{2,18},{18,2},{3,19},{19,3},{4,20},{20... | collective-permute-start | bytes 1572872 | tf_op jit(solution)/shard_map/ppermute | solution.py:215
  533.2 13.9 %copy-start.18 = (bf16[256,1024]{1,0:T(8,128)(2,1)S(1)}, bf16[256,1024]{1,0:T(8,128)(2,1)}, u32[]{:S(2)}) copy-start(bf16[256,1024]{1,0:T(8,128)(2,1)} %reduce-scatter.8.cloned.1.call-done) | copy-start | bytes 1572868
  533.3 13.9 %collective-permute-start.4 = (bf16[256,1024]{1,0:T(8,128)(2,1)}, bf16[256,1024]{1,0:T(8,128)(2,1)S(1)}, u32[]{:S(2)}, u32[]{:S(2)}) collective-permute-start(bf16[256,1024]{1,0:T(8,128)(2,1)} %reduce-scatter.8.cloned.1.call-done), channel_id=1, source_target_pairs={{0,16},{16,0},{1,17},{17,1},{2,18},{18,2},{3,19},{19,3},{4,20},{20... | collective-permute-start | bytes 1572872 | tf_op jit(solution)/shard_map/ppermute | solution.py:215
  538.7 9.7 %copy-start.23 = (f32[64]{0:T(128)}, f32[64]{0:T(128)S(1)}, u32[]{:S(2)}) copy-start(f32[64]{0:T(128)S(1)} %get-tuple-element.24) | copy-start | bytes 772
  (11 other events, 34.0 us)
Sparse Core Ops, SparseCore 0:
  140.4 68.8 reduce-scatter.3
  211.7 99.2 all-gather.1
  315.6 108.6 reduce-scatter.5
  428.8 104.4 reduce-scatter.7

commit v2 on v1

v2 whole, which is shorter than its diff:
```python
import functools
import math

import jax
import jax.numpy as jnp
from jax import lax
from jax.experimental import pallas as pl
from jax.experimental.pallas import tpu as pltpu
from jax.sharding import PartitionSpec as P

EPSILON = 1e-05
HEADS=16; HEAD_DIM=64; NEGATIVE=-1e30
FWD_TILE=(512,1024); BWD_TILE=(1024,1024)
LOG2E=math.log2(math.e); LN2=math.log(2.0)
BF=jnp.bfloat16; F32=jnp.float32
NT=(((1,),(1,)),((),())); TN=(((0,),(0,)),((),())); NN=(((1,),(0,)),((),()))

def dotf(a,b,dims):
    return lax.dot_general(a,b,dims,preferred_element_type=F32)

def split3(v):
    hi=v.astype(BF); r=v-hi.astype(F32); mid=r.astype(BF); lo=(r-mid.astype(F32)).astype(BF)
    return hi.astype(F32),mid.astype(F32),lo.astype(F32)

def with_tail(base, stat):
    lane=lax.broadcasted_iota(jnp.int32, base.shape, 1)
    hi,mid,lo=split3(stat)
    tail=jnp.where(lane==HEAD_DIM,hi,jnp.where(lane==HEAD_DIM+1,mid,jnp.where(lane==HEAD_DIM+2,lo,0.0)))
    return jnp.where(lane<HEAD_DIM,base,tail).astype(BF)

def seg_start(starts, p, segs):
    best=jnp.int32(0)
    for k in range(segs):
        s=starts[k]
        best=jnp.where(s<=p, jnp.maximum(best,s), best)
    return best

def seg_end(starts, p, segs, full):
    best=jnp.int32(full)
    for k in range(segs):
        s=starts[k]
        best=jnp.where(s>p, jnp.minimum(best,s), best)
    return best

def lanes_low(shape):
    return lax.broadcasted_iota(jnp.int32,shape,1)<HEAD_DIM

def pair_up(one, two):
    return jnp.where(lanes_low(one.shape),one,pltpu.roll(two,HEAD_DIM,1))

def pair_down(one, two):
    return jnp.where(lanes_low(one.shape),pltpu.roll(one,HEAD_DIM,1),two)

def fwd_kernel(starts, part, x_ref, low_ref, out_ref, qa_ref, ka_ref, va_ref, s_ref, q_ref, *, bq, bk, segs, group, tokens):
    i=pl.program_id(0); full=q_ref.shape[0]; half=tokens//2
    @pl.when(i==0)
    def _():
        mark=jnp.where(lax.broadcasted_iota(jnp.int32,(tokens,128),1)<HEAD_DIM+3,-1.0,0.0)
        def build(t,_):
            pair=x_ref[t,:tokens,:].astype(F32); v=x_ref[t,tokens:,:].astype(F32)
            rows=pl.ds(pl.multiple_of(t*tokens,tokens),tokens)
            low=lanes_low((tokens,128))
            q_ref[rows,:]=jnp.where(low,pair,0.0).astype(BF)
            ka_ref[rows,:]=jnp.where(low,pltpu.roll(pair,HEAD_DIM,1),mark).astype(BF)
            values=jnp.concatenate([v,pltpu.roll(v,HEAD_DIM,1)],axis=0)
            va_ref[rows,:]=jnp.where(low,values,mark).astype(BF)
            return 0
        lax.fori_loop(0,full//tokens,build,0)
    def skip():
        low_ref[...]=jnp.zeros_like(low_ref); out_ref[...]=jnp.zeros_like(out_ref)
        qa_ref[...]=with_tail(jnp.zeros((bq,128),F32),jnp.full((bq,1),1e30,F32))
    def work():
        a=i*bq; last=a+bq-1
        f0=seg_start(starts,a,segs); f1=seg_start(starts,last,segs)
        lo=f0//bk; hi=last//bk+1
        u0=jnp.minimum((f1+bk-1)//bk,hi); u1=jnp.maximum(u0,(a+1)//bk)
        qb=q_ref[pl.ds(pl.multiple_of(a,bq),bq),:]
        row=a+lax.broadcasted_iota(jnp.int32,(bq,1),0)
        first=jnp.zeros((bq,1),jnp.int32)
        for k in range(segs):
            s=starts[k]; first=jnp.where(s<=row,jnp.maximum(first,s),first)
        def score(j,top,masked):
            s=dotf(qb,ka_ref[pl.ds(pl.multiple_of(j*bk,bk),bk),:],NT)
            if masked:
                key=j*bk+lax.broadcasted_iota(jnp.int32,(bq,bk),1)
                s=jnp.where((key<=row)&(key>=first),s,NEGATIVE)
            s_ref[j]=s
            for c in range(bk//128):
                top=jnp.maximum(top,s[:,c*128:(c+1)*128])
            return top
        top=jnp.full((bq,128),NEGATIVE,F32)
        top=lax.fori_loop(lo,u0,lambda j,t:score(j,t,True),top)
        top=lax.fori_loop(u0,u1,lambda j,t:score(j,t,False),top)
        top=lax.fori_loop(u1,hi,lambda j,t:score(j,t,True),top)
        peak=jnp.max(top,axis=1,keepdims=True)
        def gather(j,acc):
            p=jnp.exp2(s_ref[j]-peak).astype(BF)
            return acc+dotf(p,va_ref[pl.ds(pl.multiple_of(j*bk,bk),bk),:],NN)
        acc=lax.fori_loop(lo,hi,gather,jnp.zeros((bq,128),F32))
        total=-acc[:,HEAD_DIM:HEAD_DIM+1]
        out=jnp.where(lanes_low((bq,128)),acc/total,0.0)
        out_ref[...]=out
        for c in range(bq//tokens):
            mid=c*tokens+half
            low_ref[c]=pair_up(out[c*tokens:mid],out[mid:mid+half]).astype(BF)
        qa_ref[...]=with_tail(qb.astype(F32),peak+jnp.log2(total))
    if group==1: work()
    else:
        own=(i%group)==part[0]
        pl.when(own)(work); pl.when(jnp.logical_not(own))(skip)

def attend(starts, part, x, *, bq, bk, group):
    ranks,rows,_=x.shape; tokens=rows//3*2; full=ranks*tokens; segs=starts.shape[0]
    if group>1: bq=tokens
    whole=lambda w: pl.BlockSpec((full,w),lambda i,*_:(0,0))
    blk=lambda w: pl.BlockSpec((bq,w),lambda i,*_:(i,0))
    return pl.pallas_call(
        functools.partial(fwd_kernel,bq=bq,bk=bk,segs=segs,group=group,tokens=tokens),
        grid_spec=pltpu.PrefetchScalarGridSpec(num_scalar_prefetch=2,grid=(full//bq,),
            in_specs=[pl.BlockSpec(x.shape,lambda i,*_:(0,0,0))],
            out_specs=[pl.BlockSpec((bq//tokens,tokens//2,128),lambda i,*_:(i,0,0)),blk(128),blk(128),whole(128),whole(128)],
            scratch_shapes=[pltpu.VMEM((full//bk,bq,bk),F32),pltpu.VMEM((full,128),BF)]),
        out_shape=[jax.ShapeDtypeStruct((ranks,tokens//2,128),BF),jax.ShapeDtypeStruct((full,128),F32)]+[jax.ShapeDtypeStruct((full,128),BF)]*3,
        compiler_params=pltpu.CompilerParams(vmem_limit_bytes=50<<20),
        cost_estimate=pl.CostEstimate(flops=full*full*512,bytes_accessed=full*1600,transcendentals=full*full//2),
        name="attend")(starts,part,x)

def bwd_kernel(starts, *refs, bq, bk, segs, begin, count, first, last, tokens):
    half=tokens//2
    refs=list(refs)
    qa_ref,ka_ref,va_ref=refs[:3]; refs=refs[3:]
    full=qa_ref.shape[0]; nq=full//bq
    if first:
        do_ref,out_ref=refs[:2]; refs=refs[2:]
    else:
        da_ref,dq_in,early_ref=refs[:3]; refs=refs[3:]
    if last:
        dx_ref,dq_ref,kt_ref,kv_ref=refs[:4]; refs=refs[4:]
        if first: da_ref=refs[0]
    else:
        if first: da_ref,refs=refs[0],refs[1:]
        dq_ref,kv_ref,kt_ref=refs[:3]
    j=pl.program_id(0)
    @pl.when(j==0)
    def _():
        if first:
            def build(t,_):
                rows=pl.ds(pl.multiple_of(t*tokens,tokens),tokens)
                g=do_ref[t,:half,:].astype(F32)
                g=jnp.concatenate([g,pltpu.roll(g,HEAD_DIM,1)],axis=0)
                delta=jnp.sum(g*out_ref[rows,:],axis=1,keepdims=True)
                da_ref[rows,:]=with_tail(g,delta)
                return 0
            lax.fori_loop(0,full//tokens,build,0)
        def clear(t,_):
            dq_ref[t]=jnp.zeros(dq_ref.shape[1:],F32) if first else dq_in[t]
            return 0
        lax.fori_loop(0,nq,clear,0)
        def trans(t,_):
            kt_ref[t]=ka_ref[pl.ds(pl.multiple_of((begin+t)*bk,bk),bk),:].astype(F32).T[:HEAD_DIM].astype(BF)
            return 0
        lax.fori_loop(0,count,trans,0)
    c=(begin+j)*bk; d=c+bk
    e0=seg_end(starts,c,segs,full); e1=seg_end(starts,d-1,segs,full)
    lo=c//bq; hi=(e1+bq-1)//bq
    u0=jnp.minimum((d-1+bq-1)//bq,hi); u1=jnp.maximum(u0,e0//bq)
    rows=pl.ds(pl.multiple_of(c,bk),bk)
    ka=ka_ref[rows,:]; va=va_ref[rows,:]; kt=kt_ref[j]
    def step(i,carry,masked):
        dk,dv=carry
        qrows=pl.ds(pl.multiple_of(i*bq,bq),bq)
        qa=qa_ref[qrows,:]; da=da_ref[qrows,:]
        p=jnp.exp2(dotf(ka,qa,NT))
        if masked:
            row=i*bq+lax.broadcasted_iota(jnp.int32,(1,bq),1)
            first_key=jnp.zeros((1,bq),jnp.int32)
            for k in range(segs):
                s=starts[k]; first_key=jnp.where(s<=row,jnp.maximum(first_key,s),first_key)
            key=c+lax.broadcasted_iota(jnp.int32,(bk,bq),0)
            p=jnp.where((key<=row)&(key>=first_key),p,0.0)
        dp=dotf(va,da,NT)
        pb=p.astype(BF); ds=(p*dp).astype(BF)
        dv=dv+dotf(pb,da,NN); dk=dk+dotf(ds,qa,NN)
        dq_ref[i]+=dotf(kt,ds,NN)
        return dk,dv
    z=jnp.zeros((bk,128),F32)
    carry=lax.fori_loop(lo,u0,lambda i,t:step(i,t,True),(z,z))
    carry=lax.fori_loop(u0,u1,lambda i,t:step(i,t,False),carry)
    dk,dv=lax.fori_loop(u1,hi,lambda i,t:step(i,t,True),carry)
    mine=pair_up(dv,dk*LN2).astype(BF)
    kv_ref[pl.ds(pl.multiple_of(j*bk,bk),bk),:]=mine
    if last:
        @pl.when(j==count-1)
        def _():
            for t in range(nq):
                dq=dq_ref[t].T*HEAD_DIM**-0.5
                dq=jnp.concatenate([dq,dq],axis=1)
                for c in range(bq//tokens):
                    r=t*bq+c*tokens
                    kv=early_ref[r:r+tokens,:] if r<begin*bk else kv_ref[r-begin*bk:r-begin*bk+tokens,:]
                    kv=kv.astype(F32)
                    dx_ref[r//tokens,:tokens,:]=jnp.where(lanes_low(kv.shape),dq[c*tokens:(c+1)*tokens],kv).astype(BF)
                    dx_ref[r//tokens,tokens:,:]=pair_up(kv[:half],kv[half:]).astype(BF)

def attend_back(starts, qa, ka, va, rest, *, bq, bk, begin, count, tokens):
    full=qa.shape[0]; segs=starts.shape[0]
    first=begin==0; last=begin+count==full//bk
    fixed=lambda shape: pl.BlockSpec(shape,lambda i,*_:(0,)*len(shape))
    dq_shape=(full//bq,64,bq); kt=pltpu.VMEM((count,64,bk),BF)
    if last:
        outs=[jax.ShapeDtypeStruct((full//tokens,tokens//2*3,128),BF)]
        scratch=[pltpu.VMEM(dq_shape,F32),kt,pltpu.VMEM((count*bk,128),BF)]
        if first: scratch.append(pltpu.VMEM((full,128),BF))
    else:
        outs=[jax.ShapeDtypeStruct(dq_shape,F32),jax.ShapeDtypeStruct((count*bk,128),BF)]
        if first: outs.insert(0,jax.ShapeDtypeStruct((full,128),BF))
        scratch=[kt]
    area=full*full*(count/(full//bk))
    return pl.pallas_call(
        functools.partial(bwd_kernel,bq=bq,bk=bk,segs=segs,begin=begin,count=count,first=first,last=last,tokens=tokens),
        grid_spec=pltpu.PrefetchScalarGridSpec(num_scalar_prefetch=1,grid=(count,),
            in_specs=[fixed(v.shape) for v in (qa,ka,va)+tuple(rest)],
            out_specs=[fixed(o.shape) for o in outs],
            scratch_shapes=scratch),
        out_shape=outs,
        compiler_params=pltpu.CompilerParams(vmem_limit_bytes=50<<20),
        cost_estimate=pl.CostEstimate(flops=int(area*1280),bytes_accessed=full*2000,transcendentals=int(area/2)),
        name="attend_back")(starts,qa,ka,va,*rest)

def fixed_block(shape):
    return pl.BlockSpec(shape,lambda s,*_:(0,)*len(shape))

def run_kernel(kernel, ids, grid, ins, in_specs, outs, out_specs, scratch, name, flops):
    moved=sum(math.prod(v.shape)*2 for v in ins)+sum(math.prod(o.shape)*2 for o in outs)
    return pl.pallas_call(kernel,
        grid_spec=pltpu.PrefetchScalarGridSpec(num_scalar_prefetch=1,grid=grid,in_specs=in_specs,out_specs=out_specs,scratch_shapes=scratch),
        out_shape=outs,compiler_params=pltpu.CompilerParams(vmem_limit_bytes=50<<20),
        cost_estimate=pl.CostEstimate(flops=flops,bytes_accessed=moved,transcendentals=0),name=name)(ids,*ins)

def pick_kernel(ids, h_ref, *outs, wide):
    for k,out in enumerate(outs):
        other=lax.bitwise_xor(ids[1]*2+ids[0],jnp.int32(k+1))
        for z in range(out.shape[1]//wide):
            out[:,z*wide:(z+1)*wide]=h_ref[:,pl.ds(pl.multiple_of((4*z+other)*wide,wide),wide)]

def pick_blocks(ids, hidden, ranks):
    tokens,inner=hidden.shape; out=jax.ShapeDtypeStruct((tokens,inner//4),hidden.dtype)
    return run_kernel(functools.partial(pick_kernel,wide=inner//ranks),ids,(1,),[hidden],[fixed_block(hidden.shape)],
        [out]*3,[fixed_block(out.shape)]*3,[],"pick_blocks",0)

def down_kernel(ids, *refs):
    lefts,rights,(sent_ref,keep_ref)=refs[:4],refs[4:8],refs[8:]
    s=pl.program_id(0)
    v=dotf(lefts[0][...],rights[0][...],TN)
    for a,b in zip(lefts[1:],rights[1:]): v=v+dotf(a[...],b[...],TN)
    v=v.astype(BF)
    @pl.when(s<2)
    def _(): sent_ref[0]=v
    @pl.when(s>=2)
    def _(): keep_ref[0]=v

def grads_down(ids, hidden, others, cots, ranks):
    tokens,inner=hidden.shape; width=cots[0].shape[1]; wide=inner//ranks
    def level(s,ids): return 2*(s%2)+jnp.where(s<2,1-ids[3],ids[3])
    mine=pl.BlockSpec((tokens,wide),lambda s,ids:(0,4*level(s,ids)+2*ids[1]+ids[0]))
    got=pl.BlockSpec((tokens,wide),lambda s,ids:(0,level(s,ids)))
    shape=jax.ShapeDtypeStruct((2,wide,width),BF)
    return run_kernel(down_kernel,ids,(4,),[hidden,*others,*cots],[mine,got,got,got]+[fixed_block(cots[0].shape)]*4,[shape,shape],
        [pl.BlockSpec((1,wide,width),lambda s,ids:(jnp.minimum(s,1),0,0)),
         pl.BlockSpec((1,wide,width),lambda s,ids:(jnp.maximum(s-2,0),0,0))],[],"grads_down",2*tokens*inner*width)

def up_kernel(ids, n_ref, no_ref, a_ref, ao_ref, ua_ref, uao_ref, ub_ref, ubo_ref, ba_ref, bao_ref, bb_ref, bbo_ref,
              as_ref, ak_ref, bs_ref, bk_ref, ln_ref, la_ref, *, share):
    s=pl.program_id(0); tokens,width=n_ref.shape; tile=width//2
    @pl.when(s==0)
    def _():
        f=lax.broadcasted_iota(jnp.int32,(width,tile),0); j=lax.broadcasted_iota(jnp.int32,(width,tile),1)
        pick=jnp.where(f==(j//share*2+ids[0])*share+j%share,1.0,0.0).astype(BF)
        for ref,pair in ((ln_ref,(n_ref,no_ref)),(la_ref,(a_ref,ao_ref))):
            for e,src in enumerate(pair):
                ref[e*tokens:(e+1)*tokens,:]=dotf(src[...],pick,NN).astype(BF)
    def product(left,one,two):
        return (dotf(left[:tokens],one[...],TN)+dotf(left[tokens:],two[...],TN)).astype(BF)
    def put_a(v):
        v=v.reshape(as_ref.shape[0],2,share,tile)
        low,high=v[:,0],v[:,1]
        cols=pl.ds(pl.multiple_of(s*tile,tile),tile)
        ak_ref[:,:,cols]=jnp.where(ids[1]==0,low,high)
        as_ref[:,:,cols]=jnp.where(ids[1]==0,high,low)
    @pl.when(s<4)
    def _():
        put_a(product(ln_ref,ua_ref,uao_ref))
        v=product(ln_ref,ub_ref,ubo_ref)
        cols=pl.ds(pl.multiple_of(s%2*tile,tile),tile)
        @pl.when(s//2==ids[2])
        def _(): bk_ref[:,cols]=v
        @pl.when(s//2!=ids[2])
        def _(): bs_ref[:,cols]=v
    @pl.when(s==4)
    def _():
        put_a(product(la_ref,ba_ref,bao_ref))
        v=product(la_ref,bb_ref,bbo_ref)
        low,high=v[:,:tile//2],v[:,tile//2:]
        bk_ref[:,2*tile:]=jnp.where(ids[2]==0,low,high)
        bs_ref[:,2*tile:]=jnp.where(ids[2]==0,high,low)

def grads_up(ids, normed, normed_other, att, att_other, up, up_other, branch, branch_other, ranks):
    tokens,width=normed.shape; share=width//ranks; tile=width//2
    f=fixed_block(normed.shape)
    at=lambda base:pl.BlockSpec((tokens,tile),lambda s,ids:(0,base+jnp.minimum(s,3)))
    fix=lambda col:pl.BlockSpec((tokens,tile),lambda s,ids:(0,col))
    a=jax.ShapeDtypeStruct((ranks//4,share,5*tile),BF); b=jax.ShapeDtypeStruct((tile,5*tile//2),BF)
    return run_kernel(functools.partial(up_kernel,share=share),ids,(5,),
        [normed,normed_other,att,att_other,up,up_other,up,up_other,branch,branch_other,branch,branch_other],
        [f,f,f,f,at(0),at(0),at(4),at(4),fix(0),fix(0),fix(1),fix(1)],[a,a,b,b],[fixed_block(v.shape) for v in (a,a,b,b)],
        [pltpu.VMEM((2*tokens,tile),BF)]*2,"grads_up",2*tokens*width*(up.shape[1]+width))

def add_kernel(ids, *refs, plan, joined):
    n=len(plan); ins,outs=refs[:2*n],refs[2*n:]
    for p,(mode,which) in enumerate(plan):
        k_ref,r_ref=ins[2*p:2*p+2]
        def total(index): return (k_ref[index].astype(F32)+r_ref[index].astype(F32)).astype(BF)
        if mode=="sum":
            outs[p][...]=total(...); continue
        for o in range(2):
            half=ids[which] if o else 1-ids[which]
            out=outs[o] if joined else outs[2*p+o]
            for i in range(out.shape[0]):
                if mode=="columns":
                    width=k_ref.shape[2]//2
                    v=total((i,slice(None),pl.ds(pl.multiple_of(half*width,128),width)))
                else:
                    v=total((2*i+half,))
                rows=v.shape[0]
                if joined: out[i,p*rows:(p+1)*rows,:]=v
                else: out[i]=v

def add_split(ids, plan, arrays, name, joined=False):
    shapes=[]
    for p,(mode,_) in enumerate(plan):
        m,r,c=arrays[2*p].shape
        shapes.append((m,r,c) if mode=="sum" else (m,r,c//2) if mode=="columns" else (m//2,r,c))
    if joined: outs=[(shapes[0][0],shapes[0][1]*len(plan),shapes[0][2])]*2
    else: outs=[s for s,(mode,_) in zip(shapes,plan) for _ in range(1 if mode=="sum" else 2)]
    return run_kernel(functools.partial(add_kernel,plan=plan,joined=joined),ids,(1,),arrays,[fixed_block(a.shape) for a in arrays],
        [jax.ShapeDtypeStruct(s,BF) for s in outs],[fixed_block(s) for s in outs],[],name,sum(math.prod(s) for s in outs))

def project_kernel(ids, x_ref, gain_ref, shift_ref, wq_ref, wk_ref, wv_ref, bq_ref, bv_ref, packed_ref, normed_ref):
    tokens=x_ref.shape[0]; half=tokens//2
    @pl.when(pl.program_id(0)==0)
    def _():
        x=x_ref[...].astype(F32)
        x=x-jnp.mean(x,axis=1,keepdims=True)
        x=x*lax.rsqrt(jnp.mean(x*x,axis=1,keepdims=True)+EPSILON)
        normed_ref[...]=(x*gain_ref[...]+shift_ref[...]).astype(BF)
    n=normed_ref[...]
    q=(dotf(n,wq_ref[...],NN)+bq_ref[...])*(LOG2E*HEAD_DIM**-0.5)
    k=dotf(n,wk_ref[...],NN)
    v=dotf(n,wv_ref[...],NN)+bv_ref[...]
    for h in range(q.shape[1]//HEAD_DIM):
        join=pair_down if h%2 else pair_up
        cols=slice(h//2*128,h//2*128+128)
        packed_ref[h,:tokens,:]=join(q[:,cols],k[:,cols]).astype(BF)
        packed_ref[h,tokens:,:]=join(v[:half,cols],v[half:,cols]).astype(BF)

def project(ids, x, gain, shift, w_qkv, bias_qv):
    tokens,width=x.shape; tile=256; steps=width//tile
    w=lambda base:pl.BlockSpec((width,tile),lambda s,ids:(0,base+s))
    c=lambda base:pl.BlockSpec((1,tile),lambda s,ids:(0,base+s))
    outs=[jax.ShapeDtypeStruct((HEADS,tokens//2*3,128),BF),jax.ShapeDtypeStruct((tokens,width),BF)]
    return run_kernel(project_kernel,ids,(steps,),[x,gain[None],shift[None],w_qkv,w_qkv,w_qkv,bias_qv[None],bias_qv[None]],
        [fixed_block(x.shape)]+[fixed_block((1,width))]*2+[w(0),w(steps),w(2*steps),c(0),c(steps)],outs,
        [pl.BlockSpec((tile//HEAD_DIM,tokens//2*3,128),lambda s,ids:(s,0,0)),fixed_block((tokens,width))],[],"project",6*tokens*width*width)

def unpack_tile(one, two):
    return jnp.concatenate([pair_up(one,two),pair_down(one,two)],axis=0)

def mix_kernel(ids, got_ref, w_ref, x_ref, bias_ref, gain_ref, shift_ref, left_ref, res_ref):
    s=pl.program_id(0); width=x_ref.shape[1]
    tiles=[unpack_tile(got_ref[2*p].astype(F32),got_ref[2*p+1].astype(F32)).astype(BF) for p in range(2)]
    att=jnp.concatenate(tiles,axis=1)
    left_ref[:,pl.ds(pl.multiple_of(width+s*256,256),256)]=att
    @pl.when(s==0)
    def _(): res_ref[...]=x_ref[...].astype(F32)+bias_ref[...]
    res_ref[...]+=dotf(att,w_ref[...],NN)
    @pl.when(s==pl.num_programs(0)-1)
    def _():
        x=res_ref[...]
        x=x-jnp.mean(x,axis=1,keepdims=True)
        x=x*lax.rsqrt(jnp.mean(x*x,axis=1,keepdims=True)+EPSILON)
        left_ref[:,:width]=(x*gain_ref[...]+shift_ref[...]).astype(BF)

def mix(ids, got, w_out, x, bias, gain, shift):
    tokens,width=x.shape; row=fixed_block((1,width))
    return run_kernel(mix_kernel,ids,(width//256,),[got,w_out,x,bias[None],gain[None],shift[None]],
        [pl.BlockSpec((4,tokens//2,128),lambda s,ids:(s,0,0)),pl.BlockSpec((256,width),lambda s,ids:(s,0)),fixed_block(x.shape),row,row,row],
        [jax.ShapeDtypeStruct((tokens,2*width),BF),jax.ShapeDtypeStruct((tokens,width),F32)],
        [fixed_block((tokens,2*width)),fixed_block((tokens,width))],[],"mix",2*tokens*width*width)

def grad_pack_kernel(ids, g_ref, w_ref, small_ref, out_ref):
    half=g_ref.shape[0]//2
    g=dotf(g_ref[...],w_ref[...],NT)
    for h in range(4):
        join=pair_down if h%2 else pair_up
        cols=slice(h//2*128,h//2*128+128)
        out_ref[h,:half,:]=join(g[:half,cols],g[half:,cols]).astype(BF)
    out_ref[:,half:,:]=small_ref[...]

def grad_pack(ids, g, w_out, smalls):
    tokens,width=g.shape; rows=tokens//2+smalls.shape[1]
    return run_kernel(grad_pack_kernel,ids,(width//256,),[g,w_out,smalls],
        [fixed_block(g.shape),pl.BlockSpec((256,width),lambda s,ids:(s,0)),pl.BlockSpec((4,)+smalls.shape[1:],lambda s,ids:(s,0,0))],
        [jax.ShapeDtypeStruct((HEADS,rows,128),BF)],[pl.BlockSpec((4,rows,128),lambda s,ids:(s,0,0))],[],"grad_pack",2*tokens*width*width)[0]

def message_kernel(ids, n_ref, dx_ref, out_ref, acc_ref, sum_ref, *, tokens, share):
    s=pl.program_id(0); half=tokens//2
    sides=[]
    for c in range(dx_ref.shape[0]):
        v=dx_ref[c,tokens:,:].astype(F32)
        v=jnp.concatenate([v,pltpu.roll(v,HEAD_DIM,1)],axis=0)
        v=jnp.where(lanes_low(v.shape),v,0.0).astype(BF)
        sides.append(jnp.concatenate([dx_ref[c,:tokens,:],v],axis=1))
    side=jnp.concatenate(sides,axis=0)
    @pl.when(s==0)
    def _():
        acc_ref[...]=jnp.zeros_like(acc_ref); sum_ref[...]=jnp.zeros_like(sum_ref)
    acc_ref[...]+=dotf(n_ref[...],side,TN)
    sum_ref[...]+=jnp.sum(side.astype(F32).reshape(-1,8,256),axis=0)
    @pl.when(s==pl.num_programs(0)-1)
    def _():
        total=jnp.sum(sum_ref[...],axis=0,keepdims=True)
        high=total.astype(BF).astype(F32); rest=total-high
        line=lax.broadcasted_iota(jnp.int32,(16,128),0)
        extra=jnp.where(line==0,high[:,:128],jnp.where(line==1,rest[:,:128],jnp.where(line==2,high[:,128:],jnp.where(line==3,rest[:,128:],0.0))))
        for r in range(out_ref.shape[0]):
            rows=slice(r*share,(r+1)*share)
            out_ref[r,:share,:]=acc_ref[rows,:128].astype(BF)
            v=acc_ref[rows,128:]
            out_ref[r,share:share+share//2,:]=pair_up(v[:share//2],v[share//2:]).astype(BF)
            out_ref[r,share+share//2:,:]=extra.astype(BF)

def weight_message(ids, normed_all, dx):
    ranks,rows,_=dx.shape; tokens=rows//3*2; full,width=normed_all.shape; share=width//ranks
    step=4; shape=(ranks,share//2*3+16,128)
    return run_kernel(functools.partial(message_kernel,tokens=tokens,share=share),ids,(ranks//step,),[normed_all,dx],
        [pl.BlockSpec((step*tokens,width),lambda s,ids:(s,0)),pl.BlockSpec((step,rows,128),lambda s,ids:(s,0,0))],
        [jax.ShapeDtypeStruct(shape,BF)],[fixed_block(shape)],
        [pltpu.VMEM((width,256),F32),pltpu.VMEM((8,256),F32)],"weight_message",2*full*width*192)[0]

def finish_kernel(ids, one_ref, two_ref, w_ref, gain_ref, shift_ref, grad_ref, cols_ref, lg_ref, lb_ref):
    share=grad_ref.shape[0]; width=grad_ref.shape[1]//3
    first=jnp.zeros((share,128),F32); second=jnp.zeros((share,128),F32)
    def both(h): return one_ref[h].astype(F32)+two_ref[h].astype(F32)
    for p in range(HEADS//2):
        a,b=both(2*p),both(2*p+1)
        end=share+share//2
        q=pair_up(a[:share],b[:share]); k=pair_down(a[:share],b[:share])
        v=unpack_tile(a[share:end],b[share:end])
        la=a[end:end+8],b[end:end+8]
        cq=pair_up(*la); ck=pair_down(*la)
        for base,tile,col in ((0,q,cq[0:1]+cq[1:2]),(width,k,ck[0:1]+ck[1:2]),(2*width,v,cq[2:3]+cq[3:4])):
            at=slice(base+p*128,base+p*128+128)
            w=w_ref[:,at].astype(F32)
            grad_ref[:,at]=tile; cols_ref[:,at]=col
            first=first+w*tile; second=second+w*col
    bias=jnp.sum(second,axis=1,keepdims=True)
    lb_ref[...]=bias
    lg_ref[...]=(jnp.sum(first,axis=1,keepdims=True)-shift_ref[...]*bias)/gain_ref[...]

def finish(ids, one, two, w_qkv, gain, shift, ranks):
    width=w_qkv.shape[0]; share=width//ranks
    mine=lambda c:pl.BlockSpec((share,c),lambda s,ids:(ids[5],0))
    outs=[jax.ShapeDtypeStruct(s,F32) for s in ((share,3*width),(1,3*width),(share,1),(share,1))]
    return run_kernel(finish_kernel,ids,(1,),[one,two,w_qkv,gain[:,None],shift[:,None]],
        [fixed_block(one.shape)]*2+[mine(3*width),mine(1),mine(1)],outs,[fixed_block(o.shape) for o in outs],[],"finish",share*width*12)

def input_kernel(ids, got_ref, wq_ref, wk_ref, wv_ref, x_ref, gain_ref, res_ref, out_ref, acc_ref):
    s=pl.program_id(0); tokens=x_ref.shape[0]
    @pl.when(s==0)
    def _(): acc_ref[...]=jnp.zeros_like(acc_ref)
    q,k,v=[],[],[]
    for p in range(2):
        a,b=got_ref[2*p].astype(F32),got_ref[2*p+1].astype(F32)
        q.append(pair_up(a[:tokens],b[:tokens])); k.append(pair_down(a[:tokens],b[:tokens]))
        v.append(unpack_tile(a[tokens:],b[tokens:]))
    total=acc_ref[...]
    for tiles,w_ref in ((q,wq_ref),(k,wk_ref),(v,wv_ref)):
        total=total+dotf(jnp.concatenate(tiles,axis=1).astype(BF),w_ref[...],NT)
    acc_ref[...]=total
    @pl.when(s==pl.num_programs(0)-1)
    def _():
        x=x_ref[...].astype(F32)
        x=x-jnp.mean(x,axis=1,keepdims=True)
        scale=lax.rsqrt(jnp.mean(x*x,axis=1,keepdims=True)+EPSILON)
        x=x*scale
        g=acc_ref[...]*gain_ref[...]
        g=(g-jnp.mean(g,axis=1,keepdims=True)-x*jnp.mean(g*x,axis=1,keepdims=True))*scale
        out_ref[...]=(res_ref[...]+g).astype(BF)

def input_grad(ids, got, w_qkv, x, gain, residual_grad):
    tokens,width=x.shape; steps=width//256
    w=lambda base:pl.BlockSpec((width,256),lambda s,ids:(0,base+s))
    return run_kernel(input_kernel,ids,(steps,),[got,w_qkv,w_qkv,w_qkv,x,gain[None],residual_grad],
        [pl.BlockSpec((4,)+got.shape[1:],lambda s,ids:(s,0,0)),w(0),w(steps),w(2*steps),fixed_block(x.shape),fixed_block((1,width)),fixed_block(x.shape)],
        [jax.ShapeDtypeStruct((tokens,width),BF)],[fixed_block((tokens,width))],[pltpu.VMEM((tokens,width),F32)],"input_grad",6*tokens*width*width)[0]

def statistics(values):
    centre = jnp.mean(values, axis=-1, keepdims=True)
    centred = values - centre
    second = jnp.mean(centred * centred, axis=-1, keepdims=True)
    scale = lax.rsqrt(second + EPSILON)
    return centred * scale, scale


def norm_back(unit, scale, gain, grad):
    scaled = grad * gain
    first = jnp.mean(scaled, axis=-1, keepdims=True)
    second = jnp.mean(scaled * unit, axis=-1, keepdims=True)
    return (scaled - first - unit * second) * scale


def row_sum(value):
    low = lax.optimization_barrier(value.astype(BF))
    if lax.axis_size("row") == 2:
        return low.astype(F32) + lax.ppermute(low, "row", [(0, 1), (1, 0)]).astype(F32)
    return lax.psum(low.astype(F32), "row")


def exchange(value):
    return lax.all_to_all(value, "seq", 0, 0, tiled=True)


def swap(value, bit):
    return lax.ppermute(value, "seq", [(i, i ^ bit) for i in range(lax.axis_size("seq"))])


def swap_row(value):
    return lax.ppermute(value, "row", [(0, 1), (1, 0)])


def half_step(value, axis, mine, move):
    keep = lax.dynamic_index_in_dim(value, mine, axis, keepdims=False)
    sent = lax.dynamic_index_in_dim(value, 1 - mine, axis, keepdims=False)
    return (keep.astype(F32) + move(sent).astype(F32)).astype(BF)


def outer_steps(value):
    me, bit = lax.axis_index("seq"), 4
    while value.shape[0] > 1:
        value = value.reshape((value.shape[0] // 2, 2) + value.shape[1:])
        value = half_step(value, 1, me // bit % 2, lambda v, bit=bit: swap(v, bit))
        bit *= 2
    return value[0]


def row_join(value):
    other = swap_row(value)
    first = lax.axis_index("row") == 0
    return jnp.where(first, value, other).astype(F32), jnp.where(first, other, value).astype(F32)


def per_device(
    frames,
    seg_lengths,
    ln1_gain,
    ln1_bias,
    w_qkv,
    bias_qv,
    w_out,
    bias_out,
    ln2_gain,
    ln2_bias,
    w_up,
    bias_up,
    w_down,
    bias_down,
    grad_out,
):
    tokens, feature = frames.shape[1:]
    ranks = lax.axis_size("seq")
    me = lax.axis_index("seq")
    group = max(1, ranks // HEADS)
    full = ranks * tokens
    share = feature // ranks
    lengths = seg_lengths[0]
    starts = jnp.cumsum(lengths, dtype=jnp.int32) - lengths
    part = (me % group).astype(jnp.int32)[None]

    def spread(value):
        return jnp.repeat(value, group, axis=0) if group > 1 else value

    def fold(value):
        if group == 1:
            return value
        value = value.reshape((HEADS, group) + value.shape[1:])
        return jnp.sum(value.astype(F32), axis=1).astype(value.dtype)

    place = [me % 2, me // 2 % 2, lax.axis_index("row"), me // 4 % 2, me // 8 % 2, me]
    ids = jnp.stack(place).astype(jnp.int32)
    packed, normed_low = project(ids, frames[0], ln1_gain, ln1_bias, w_qkv, bias_qv)
    packed = exchange(spread(packed))
    cot_low = grad_out[0]
    fast = ranks == 16 and lax.axis_size("row") == 2
    if fast:
        cot_two = swap(cot_low, 2)
        cots = [cot_low, swap(cot_low, 1), cot_two, swap(cot_two, 1)]
        cots, packed = lax.optimization_barrier((cots, packed))
    gather = lambda v: lax.all_gather(v, "seq", axis=0, tiled=True)
    normed_low, packed = lax.optimization_barrier((normed_low, packed))
    normed_all = gather(normed_low)
    low, out, qa, ka, va = attend(starts, part, packed, bq=FWD_TILE[0], bk=FWD_TILE[1], group=group)
    left, residual = mix(ids, fold(exchange(low)), w_out, frames[0], bias_out, ln2_gain, ln2_bias)
    normed_two_low, attended_low = left[:, :feature], left[:, feature:]
    unit_two, scale_two = statistics(residual)
    up_proj = dotf(normed_two_low, w_up, NN) + bias_up
    phi = 0.5 * (1.0 + lax.erf(up_proj * (0.5**0.5)))
    hidden = (up_proj * phi).astype(BF)
    slope = phi + up_proj * jnp.exp(-0.5 * up_proj * up_proj) * (1.0 / math.sqrt(2.0 * math.pi))
    out_frames = (residual + (dotf(hidden, w_down, NN) + bias_down)).astype(BF)
    cot = cot_low.astype(F32)
    if fast:
        picked, cot_low = lax.optimization_barrier((pick_blocks(ids, hidden, ranks), cot_low))
    up_grad = (dotf(cot_low, w_down, NT) * slope).astype(BF)
    normed_two_grad = dotf(up_grad, w_up, NT)
    residual_grad = cot + norm_back(unit_two, scale_two, ln2_gain, normed_two_grad)
    branch_grad = residual_grad.astype(BF)

    def piece(value):
        return value.reshape(ranks, -1)

    smalls = jnp.concatenate(
        [
            piece(jnp.sum(normed_two_grad * unit_two, axis=0)),
            piece(jnp.sum(normed_two_grad, axis=0)),
            piece(jnp.sum(branch_grad, axis=0, dtype=F32)),
            piece(jnp.sum(up_grad, axis=0, dtype=F32)),
            piece(jnp.sum(cot, axis=0)),
        ],
        axis=1,
    ).astype(BF)
    smalls = smalls.reshape(ranks, -1, 128)
    lines = smalls.shape[1]
    smalls = jnp.pad(smalls, ((0, 0), (0, 16 - lines), (0, 0)))
    if group == 1:
        sent = grad_pack(ids, branch_grad, w_out, smalls)
    else:
        sent = grad_pack(ids, branch_grad, w_out, jnp.zeros((HEADS, 16, 128), BF))
        sent = jnp.concatenate([spread(sent[:, : tokens // 2]), smalls], axis=1)
    sent, normed_all = lax.optimization_barrier((sent, normed_all))
    got = exchange(sent)
    small_total = row_sum(jnp.sum(got[:, tokens // 2 : tokens // 2 + lines].astype(F32), axis=0).reshape(-1))

    back = functools.partial(attend_back, starts, qa, ka, va, bq=BWD_TILE[0], bk=BWD_TILE[1], tokens=tokens)
    tiles = full // BWD_TILE[1]
    if fast:
        others = [swap(v, k + 1) for k, v in enumerate(picked)]
        others, up_grad, _ = lax.optimization_barrier((others, up_grad, sent))
        down_sent, down_keep = grads_down(ids, hidden, others, cots, ranks)
        down_got = swap(down_sent, 4)
        a_sent, a_keep, b_sent, b_keep = grads_up(
            ids,
            normed_two_low,
            swap(normed_two_low, 1),
            attended_low,
            swap(attended_low, 1),
            up_grad,
            swap(up_grad, 1),
            branch_grad,
            swap(branch_grad, 1),
            ranks,
        )
        a_got, b_got = swap(a_sent, 2), swap_row(b_sent)
        one = back((got, out), begin=0, count=tiles // 4)
        a_got, b_got, down_got, one = lax.optimization_barrier((a_got, b_got, down_got, one))
        blocks = lambda v: v.reshape(ranks // 2, share, -1)
        a_sent, a_keep, b_sent, b_keep, down_sent, down_keep = add_split(
            ids,
            (("columns", 2), ("blocks", 1), ("blocks", 4)),
            [a_keep, a_got, blocks(b_keep), blocks(b_got), down_keep, down_got],
            "add_one",
        )
        one, a_sent, b_sent, down_sent = lax.optimization_barrier((one, a_sent, b_sent, down_sent))
        a_got, b_got, down_got = swap_row(a_sent), swap(b_sent, 2), swap(down_sent, 8)
        two = back(one, begin=tiles // 4, count=tiles // 4)
        two = [one[0], two[0], jnp.concatenate([one[2], two[1]], axis=0)]
        a_got, b_got, two = lax.optimization_barrier((a_got, b_got, two))
        up_sent, up_keep = add_split(
            ids, (("blocks", 3), ("blocks", 3)), [a_keep, a_got, b_keep, b_got], "add_two", joined=True
        )
        two, up_sent = lax.optimization_barrier((two, up_sent))
        up_got = swap(up_sent, 4)
        (dx,) = back(two, begin=tiles // 2, count=tiles // 2)
        up_got, down_got, dx = lax.optimization_barrier((up_got, down_got, dx))
        message = weight_message(ids, normed_all, dx)
        up_got, down_got, message = lax.optimization_barrier((up_got, down_got, message))
        up_sent, up_keep, down_sent, down_keep = add_split(
            ids, (("blocks", 4), ("columns", 2)), [up_keep, up_got, down_keep, down_got], "add_three"
        )
        down_got = swap_row(down_sent)
        dx_got = exchange(dx)
        up_sent, dx_got = lax.optimization_barrier((up_sent, dx_got))
        up_got = swap(up_sent, 8)
        up_part, down_part = add_split(
            ids, (("sum", 0), ("sum", 0)), [up_keep, up_got, down_keep, down_got], "add_four"
        )
        total_down = jnp.concatenate(row_join(down_part[0]), axis=1)
        one_half, other_half = row_join(up_part[0])
        width = feature
        rows_a, rows_b = slice(0, share), slice(share, 2 * share)
        total_up = jnp.concatenate(
            [
                one_half[rows_a],
                other_half[rows_a, : 3 * width // 4],
                one_half[rows_b, :width],
                other_half[rows_b, :width],
            ],
            axis=1,
        )
        total_out = jnp.concatenate(
            [other_half[rows_a, 3 * width // 4 :], one_half[rows_b, width:], other_half[rows_b, width:]], axis=1
        )
    else:
        core, across = me % 2, me // 2 % 2

        def halves(value):
            parts = value.reshape(tokens, ranks // 2, 2, -1)
            keep = lax.dynamic_index_in_dim(parts, core, 2, keepdims=False).reshape(tokens, -1)
            sent = lax.dynamic_index_in_dim(parts, 1 - core, 2, keepdims=False).reshape(tokens, -1)
            return jnp.concatenate([keep, swap(sent, 1)], axis=0)

        def both(value):
            return jnp.concatenate([value, swap(value, 1)], axis=0)

        def reduced(value):
            value = value.astype(BF).reshape(ranks // 4, 2, -1, value.shape[-1])
            return row_sum(outer_steps(half_step(value, 1, across, lambda v: swap(v, 2))))

        total_down = reduced(dotf(halves(hidden), both(cot_low), TN))
        total_up = reduced(dotf(halves(normed_two_low), both(up_grad), TN))
        total_out = reduced(dotf(halves(attended_low), both(branch_grad), TN))
        (dx,) = back((got, out), begin=0, count=tiles)
        dx_got = exchange(dx)
        message = weight_message(ids, normed_all, dx)
    message, dx_got = lax.optimization_barrier((message, dx_got))
    grad_frames = input_grad(ids, fold(dx_got), w_qkv, frames[0], ln1_gain, residual_grad)
    mine = fold(exchange(message))
    if lax.axis_size("row") == 2:
        theirs = swap_row(mine)
    else:
        mine = lax.psum(mine.astype(F32), "row")
        theirs = jnp.zeros_like(mine)
    grad_w_qkv, column_total, grad_ln1_gain, grad_ln1_bias = finish(ids, mine, theirs, w_qkv, ln1_gain, ln1_bias, ranks)
    grad_ln1_gain, grad_ln1_bias = grad_ln1_gain[:, 0], grad_ln1_bias[:, 0]
    grad_bias_qv = jnp.concatenate([column_total[0, :feature], column_total[0, 2 * feature :]])
    grad_bias_qv = lax.dynamic_slice(grad_bias_qv, (me * 2 * share,), (2 * share,))

    wide = w_up.shape[1] // ranks
    ends = [share, 2 * share, 3 * share, 3 * share + wide]
    grad_ln2_gain, grad_ln2_bias, grad_bias_out, grad_bias_up, grad_bias_down = jnp.split(small_total, ends)
    return (
        out_frames[None],
        grad_frames[None],
        grad_ln1_gain,
        grad_ln1_bias,
        grad_w_qkv,
        grad_bias_qv,
        total_out,
        grad_bias_out,
        grad_ln2_gain,
        grad_ln2_bias,
        total_up,
        grad_bias_up,
        total_down,
        grad_bias_down,
    )


def solution(mesh):
    frames_spec = P("row", "seq", None)
    vector, matrix = P("seq"), P("seq", None)
    return jax.shard_map(
        per_device,
        mesh=mesh,
        in_specs=(frames_spec, P("row", None)) + (P(),) * 12 + (frames_spec,),
        out_specs=(
            frames_spec,
            frames_spec,
            vector,
            vector,
            matrix,
            vector,
            matrix,
            vector,
            vector,
            vector,
            matrix,
            vector,
            matrix,
            vector,
        ),
        check_vma=False,
    )
```

time: 564 us -> 385 us (0.68)
  waiting for transfers between devices: 279 us -> 119 us
  Pallas kernels: 68.8 us -> 133 us
  blocking collectives: 50.3 us -> 0 us
  matrix products: 59.9 us -> 27.3 us
  starting transfers between devices: 24.1 us -> 48.8 us
  other arithmetic: 24.2 us -> 9.4 us
  local copies, waits for them, and re-layouts: 34 us -> 25.9 us
    reduce_scatter x3 -> x0, waiting for transfers between devices: 179 us -> none  [scatter_sum(): lax.psum_scatter(value.astype(BF), 'seq', scatter_dimension=0, tiled=True)]
    ppermute x0 -> x22, waiting for transfers between devices: none -> 65.3 us  [the longest x16 47.4 us: swap(): lax.ppermute(value, 'seq', [(i, i ^ bit) for i in range(lax.axis_size('se...]
    pallas_call x1 -> x16, Pallas kernels: 39.6 us -> 103 us  [the longest x13 56.3 us: run_kernel(): pl.pallas_call(kernel, grid_spec=pltpu.PrefetchScalarGridSpec(num_scalar_...]
    all_to_all x2 -> x0, blocking collectives: 50.3 us -> none  [exchange(): return lax.all_to_all(value, 'seq', 0, 0, tiled=True)]
    all_to_all x3 -> x5, waiting for transfers between devices: 90.9 us -> 53.7 us  [exchange(): return lax.all_to_all(value, 'seq', 0, 0, tiled=True)]
    dot_general x12 -> x4, matrix products: 59.9 us -> 27.3 us  [dotf(): return lax.dot_general(a, b, dims, preferred_element_type=F32)]
    ppermute x0 -> x22, starting transfers between devices: none -> 17.4 us  [the longest x16 9.94 us: swap(): lax.ppermute(value, 'seq', [(i, i ^ bit) for i in range(lax.axis_size('se...]
    unnamed x62 -> x116, local copies, waits for them, and re-layouts: 4.94 us -> 21.5 us
  transfers between devices with their start and end apart: 12 -> 29, of which waited for: 8 -> 12; matrix products, arithmetic and copies ran while one was open for 13% -> 10% of each run, Pallas kernels for 7% -> 31%
where the time goes in v2:
time: 385 us; the launch traced here: 378 us
  Pallas kernels  133 us (35%)
  waiting for transfers between devices  119 us (31%)
  starting transfers between devices  48.8 us (13%)
  matrix products  27.3 us (7%)
  local copies, waits for them, and re-layouts  25.9 us (7%)
  between operations  15.1 us (4%)
  other arithmetic  9.4 us (2%)
    pallas_call x13, Pallas kernels, run_kernel(): pl.pallas_call(kernel, grid_spec=pltpu.PrefetchScalarGridSpec(num_scalar_...  56.3 us
    all_to_all x5, waiting for transfers between devices, exchange(): return lax.all_to_all(value, 'seq', 0, 0, tiled=True)  53.7 us
    ppermute x16, waiting for transfers between devices, swap(): lax.ppermute(value, 'seq', [(i, i ^ bit) for i in range(lax.axis_size('se...  47.4 us
    pallas_call x3, Pallas kernels, attend_back(): pl.pallas_call(functools.partial(bwd_kernel, bq=bq, bk=bk, segs=segs, beg...  46.9 us
    all_to_all x5, starting transfers between devices, exchange(): return lax.all_to_all(value, 'seq', 0, 0, tiled=True)  30.9 us
    pallas_call x1, Pallas kernels, attend(): pl.pallas_call(functools.partial(fwd_kernel, bq=bq, bk=bk, segs=segs, gro...  29.5 us
    dot_general x4, matrix products, dotf(): return lax.dot_general(a, b, dims, preferred_element_type=F32)  27.3 us
    unnamed x116, local copies, waits for them, and re-layouts  21.5 us
  transfers between devices with their start and end apart: 29, of which 12 were waited for; matrix products, arithmetic and copies ran while one was open for 10% of the time, Pallas kernels for 31%

profile of v2, /device:TPU:16, one launch (start us, length us, event | category | flops | bytes accessed | tf_op | source)
XLA Modules:
  0.0 378.3 jit_solution(17427426506712482464)
XLA Ops:
  10.5 6.8 %project.1 = (bf16[16,384,128]{2,1,0:T(8,128)(2,1)}, bf16[256,1024]{1,0:T(8,128)(2,1)}) custom-call(s32[6]{0:T(128)S(1)} %stack.27.ids, bf16[256,1024]{1,0:T(8,128)(2,1)S(1)} %bitcast.44, f32[1,1024]{1,0:T(1,128)S(1)} %bitcast.53, f32[1,1024]{1,0:T(1,128)S(1)} %bitcast.58, bf16[1024,3072]{1,0:T(8,128)(2,1)} %w_ref.5, bf16[1024,3072]{1,0:T(8,128)(2,1)} %w_ref.5, ...), custom_call_target="tpu_custom_call" | custom-call | flops 1610612736 | bytes 21508096 | tf_op jit(solution)/shard_map/project/pallas_call | solution.py:235
  17.3 6.2 %all-to-all-start = ((bf16[16,384,128]{2,1,0:T(8,128)(2,1)}), bf16[16,384,128]{2,1,0:T(8,128)(2,1)S(1)}, u32[]{:S(2)}, u32[]{:S(2)}) async-start(bf16[16,384,128]{2,1,0:T(8,128)(2,1)} %get-tuple-element.104), calls=%async_computation | async-start | bytes 3145728 | tf_op jit(solution)/shard_map/all_to_all | solution.py:530
  25.0 27.1 %collective-permute-done.1.refs_6_ = bf16[256,1024]{1,0:T(8,128)(2,1)S(1)} collective-permute-done((bf16[256,1024]{1,0:T(8,128)(2,1)S(1)}, bf16[256,1024]{1,0:T(8,128)(2,1)S(1)}, u32[]{:S(2)}, u32[]{:S(2)}) %collective-permute-start.1) | collective-permute-done | bytes 524320 | tf_op jit(solution)/shard_map/ppermute | solution.py:534
  54.8 5.0 %all-to-all-done.x_ref = bf16[16,384,128]{2,1,0:T(8,128)(2,1)S(1)} async-done(((bf16[16,384,128]{2,1,0:T(8,128)(2,1)}), bf16[16,384,128]{2,1,0:T(8,128)(2,1)S(1)}, u32[]{:S(2)}, u32[]{:S(2)}) %all-to-all-start) | async-done | bytes 1572896 | tf_op jit(solution)/shard_map/all_to_all | solution.py:530
  61.0 29.5 %attend.1 = (bf16[16,128,128]{2,1,0:T(8,128)(2,1)}, f32[4096,128]{1,0:T(8,128)}, bf16[4096,128]{1,0:T(8,128)(2,1)S(1)}, bf16[4096,128]{1,0:T(8,128)(2,1)S(1)}, bf16[4096,128]{1,0:T(8,128)(2,1)S(1)}) custom-call(s32[4]{0:T(128)S(1)} %bitcast_subtract_fusion.starts, s32[1]{0:T(128)} %constant.96.clone.1.part, bf16[16,384,128]{2,1,0:T(8,128)(2,1)} %copy-done.54), custom_call_target="tpu_custom_call" | custom-call | flops 8589934592 | bytes 6553600 | tf_op jit(solution)/shard_map/attend/pallas_call | solution.py:117
  93.4 5.2 %all-to-all-start.1 = ((bf16[16,128,128]{2,1,0:T(8,128)(2,1)}), bf16[16,128,128]{2,1,0:T(8,128)(2,1)S(1)}, u32[]{:S(2)}, u32[]{:S(2)}) async-start(bf16[16,128,128]{2,1,0:T(8,128)(2,1)} %get-tuple-element.107), calls=%async_computation.1 | async-start | bytes 1048576 | tf_op jit(solution)/shard_map/all_to_all | solution.py:530
  98.8 27.8 %all-to-all-done.1.got_ref = bf16[16,128,128]{2,1,0:T(8,128)(2,1)S(1)} async-done(((bf16[16,128,128]{2,1,0:T(8,128)(2,1)}), bf16[16,128,128]{2,1,0:T(8,128)(2,1)S(1)}, u32[]{:S(2)}, u32[]{:S(2)}) %all-to-all-start.1) | async-done | bytes 524320 | tf_op jit(solution)/shard_map/all_to_all | solution.py:530
  126.6 4.4 %mix.1 = (bf16[256,2048]{1,0:T(8,128)(2,1)S(1)}, f32[256,1024]{1,0:T(8,128)S(1)}) custom-call(s32[6]{0:T(128)S(1)} %stack.27.ids, bf16[16,128,128]{2,1,0:T(8,128)(2,1)S(1)} %all-to-all-done.1.got_ref, bf16[1024,1024]{1,0:T(8,128)(2,1)} %w_ref.4, bf16[256,1024]{1,0:T(8,128)(2,1)S(1)} %bitcast.45, f32[1,1024]{1,0:T(1,128)S(1)} %bitcast.61, ...), custom_call_target="tpu_custom_call" | custom-call | flops 536870912 | bytes 4724736 | tf_op jit(solution)/shard_map/mix/pallas_call | solution.py:235
  131.0 5.6 %multiply_convert_fusion = (bf16[256,4096]{1,0:T(8,128)(2,1)S(1)}, f32[256,4096]{1,0:T(8,128)S(1)}) fusion(f32[4096]{0:T(1024)S(1)} %copy-done.55, bf16[1024,4096]{1,0:T(8,128)(2,1)} %param.25, bf16[256,2048]{1,0:T(8,128)(2,1)S(1)} %get-tuple-element.109), kind=kOutput, calls=%fused_computation.8 | convolution fusion | flops 2153775104 | bytes 15220736 | tf_op jit(solution)/shard_map/dot_general | solution.py:19
  138.6 6.9 %fusion.14 = (bf16[4096]{0:T(1024)(128)(2,1)S(1)}, bf16[256,4096]{1,0:T(8,128)(2,1)}) fusion(f32[256,4096]{1,0:T(8,128)S(1)} %get-tuple-element.212, bf16[256,1024]{1,0:T(8,128)(2,1)S(1)} %bitcast.49, bf16[4096,1024]{1,0:T(8,128)(2,1)} %param.27), kind=kOutput, calls=%fused_computation.43 | convolution fusion | flops 2159013888 | bytes 15212544 | tf_op jit(solution)/shard_map/dot_general | solution.py:19
  147.8 7.6 %multiply_reduce_fusion = (bf16[1024]{0:T(1024)(128)(2,1)S(1)}, f32[256]{0:T(256)S(1)}, f32[256]{0:T(256)S(1)}, bf16[1024]{0:T(1024)(128)(2,1)S(1)}, f32[256,1024]{1,0:T(8,128)}) fusion(f32[256,1024]{1,0:T(8,128)S(1)} %get-tuple-element.108, f32[256]{0:T(256)S(1)} %add_rsqrt_fusion, f32[256]{0:T(256)S(1)} %broadcast_multiply_fusion.1, ...), kind=kOutput, calls=%fused_computation.15 | convolution fusion | flops 2149840384 | bytes 12595200 | tf_op jit(solution)/shard_map/dot_general | solution.py:19
  155.5 3.1 fusion.10
  159.9 2.2 grad_pack.1
  163.0 8.0 %collective-permute-done.7.refs_3_ = bf16[256,1024]{1,0:T(8,128)(2,1)} collective-permute-done((bf16[256,1024]{1,0:T(8,128)(2,1)}, bf16[256,1024]{1,0:T(8,128)(2,1)}, u32[]{:S(2)}, u32[]{:S(2)}) %collective-permute-start.7) | collective-permute-done | bytes 524320 | tf_op jit(solution)/shard_map/ppermute | solution.py:534
  173.4 5.9 %all-to-all-start.2 = ((bf16[16,144,128]{2,1,0:T(8,128)(2,1)}), bf16[16,144,128]{2,1,0:T(8,128)(2,1)}, u32[]{:S(2)}, u32[]{:S(2)}) async-start(bf16[16,144,128]{2,1,0:T(8,128)(2,1)} %copy-done.8), calls=%async_computation.2 | async-start | bytes 1179648 | tf_op jit(solution)/shard_map/all_to_all | solution.py:530
  180.4 10.3 %grads_up.1 = (bf16[4,64,2560]{2,1,0:T(8,128)(2,1)}, bf16[4,64,2560]{2,1,0:T(8,128)(2,1)}, bf16[512,1280]{1,0:T(8,128)(2,1)}, bf16[512,1280]{1,0:T(8,128)(2,1)}) custom-call(s32[6]{0:T(128)S(1)} %stack.27.ids, bf16[256,1024]{1,0:T(8,128)(2,1)S(1)} %get-tuple-element.200.n_ref, bf16[256,1024]{1,0:T(8,128)(2,1)} %collective-permute-done.3.no_ref, ...), custom_call_target="tpu_custom_call" | custom-call | flops 2684354560 | bytes 17825792 | tf_op jit(solution)/shard_map/grads_up/pallas_call | solution.py:235
  193.9 6.4 %grads_down.1 = (bf16[2,256,1024]{2,1,0:T(8,128)(2,1)}, bf16[2,256,1024]{2,1,0:T(8,128)(2,1)}) custom-call(s32[6]{0:T(128)S(1)} %stack.27.ids, bf16[256,4096]{1,0:T(8,128)(2,1)} %copy-done.10, bf16[256,1024]{1,0:T(8,128)(2,1)} %collective-permute-done.5.refs_1_, bf16[256,1024]{1,0:T(8,128)(2,1)} %collective-permute-done.6.refs_2_, ...), custom_call_target="tpu_custom_call" | custom-call | flops 2147483648 | bytes 7864320 | tf_op jit(solution)/shard_map/grads_down/pallas_call | solution.py:235
  201.7 19.4 %attend_back.3 = (bf16[4096,128]{1,0:T(8,128)(2,1)S(1)}, f32[4,64,1024]{2,1,0:T(8,128)S(1)}, bf16[1024,128]{1,0:T(8,128)(2,1)S(1)}) custom-call(s32[4]{0:T(128)S(1)} %bitcast_subtract_fusion.starts, bf16[4096,128]{1,0:T(8,128)(2,1)S(1)} %copy-done.45, bf16[4096,128]{1,0:T(8,128)(2,1)} %copy-done.47, bf16[4096,128]{1,0:T(8,128)(2,1)} %copy-done.49, ...), custom_call_target="tpu_custom_call" | custom-call | flops 5368709120 | bytes 8192000 | tf_op jit(solution)/shard_map/attend_back/pallas_call | solution.py:219
  225.2 4.5 %add_one.1 = (bf16[4,64,1280]{2,1,0:T(8,128)(2,1)S(1)}, bf16[4,64,1280]{2,1,0:T(8,128)(2,1)S(1)}, bf16[4,64,1280]{2,1,0:T(8,128)(2,1)S(1)}, bf16[4,64,1280]{2,1,...) custom-call(s32[6]{0:T(128)S(1)} %stack.27.ids, ...), custom_call_target="tpu_custom_call" | custom-call | flops 1835008 | bytes 11010048 | tf_op jit(solution)/shard_map/add_one/pallas_call | solution.py:235
  231.8 12.3 %attend_back.4 = (f32[4,64,1024]{2,1,0:T(8,128)S(1)}, bf16[1024,128]{1,0:T(8,128)(2,1)S(1)}) custom-call(s32[4]{0:T(128)S(1)} %bitcast_subtract_fusion.starts, bf16[4096,128]{1,0:T(8,128)(2,1)S(1)} %copy-done.46, bf16[4096,128]{1,0:T(8,128)(2,1)S(1)} %copy-done.48, bf16[4096,128]{1,0:T(8,128)(2,1)} %copy-done.49, bf16[4096,128]{1,0:T(8,128)(2,1)} %copy-done.51, ...), custom_call_target="tpu_custom_call" | custom-call | flops 5368709120 | bytes 8192000 | tf_op jit(solution)/shard_map/attend_back/pallas_call | solution.py:219
  249.3 15.2 %attend_back.5.dx_ref = bf16[16,384,128]{2,1,0:T(8,128)(2,1)} custom-call(s32[4]{0:T(128)S(1)} %bitcast_subtract_fusion.starts, bf16[4096,128]{1,0:T(8,128)(2,1)S(1)} %copy-done.46, bf16[4096,128]{1,0:T(8,128)(2,1)S(1)} %copy-done.48, bf16[4096,128]{1,0:T(8,128)(2,1)S(1)} %copy-done.50, bf16[4096,128]{1,0:T(8,128)(2,1)} %copy-done.51, ...), custom_call_target="tpu_custom_call" | custom-call | flops 10737418240 | bytes 8192000 | tf_op jit(solution)/shard_map/attend_back/pallas_call | solution.py:219
  265.4 2.8 collective-permute-done.15.refs_1_
  269.0 6.5 %all-to-all-start.3 = ((bf16[16,384,128]{2,1,0:T(8,128)(2,1)}), bf16[16,384,128]{2,1,0:T(8,128)(2,1)}, u32[]{:S(2)}, u32[]{:S(2)}) async-start(bf16[16,384,128]{2,1,0:T(8,128)(2,1)} %attend_back.5.dx_ref), calls=%async_computation.3 | async-start | bytes 3145728 | tf_op jit(solution)/shard_map/all_to_all | solution.py:530
  278.1 6.9 %weight_message.1 = bf16[16,112,128]{2,1,0:T(8,128)(2,1)S(1)} custom-call(s32[6]{0:T(128)S(1)} %stack.27.ids, bf16[4096,1024]{1,0:T(8,128)(2,1)} %all-gather.2.cloned.1.call-done.n_ref, bf16[16,384,128]{2,1,0:T(8,128)(2,1)S(1)} %copy-done.3), custom_call_target="tpu_custom_call" | custom-call | flops 1610612736 | bytes 10420224 | tf_op jit(solution)/shard_map/weight_message/pallas_call | solution.py:235
  291.0 20.9 %all-to-all-done.3.got_ref = bf16[16,384,128]{2,1,0:T(8,128)(2,1)} async-done(((bf16[16,384,128]{2,1,0:T(8,128)(2,1)}), bf16[16,384,128]{2,1,0:T(8,128)(2,1)}, u32[]{:S(2)}, u32[]{:S(2)}) %all-to-all-start.3) | async-done | bytes 1572896 | tf_op jit(solution)/shard_map/all_to_all | solution.py:530
  312.0 7.3 %fusion.7 = bf16[1,256,1024]{2,1,0:T(8,128)(2,1)} fusion(f32[256,1024]{1,0:T(8,128)S(1)} %get-tuple-element.108, bf16[256,4096]{1,0:T(8,128)(2,1)} %copy-done.10, bf16[4096,1024]{1,0:T(8,128)(2,1)} %param.27, f32[1024]{0:T(1024)S(1)} %copy-done.56), kind=kOutput, calls=%fused_computation.13 | convolution fusion | flops 2148270080 | bytes 12062720 | tf_op jit(solution)/shard_map/dot_general | solution.py:19
  320.0 6.4 %collective-permute-done.18.refs_1_ = bf16[1,128,1280]{2,1,0:T(8,128)(2,1)S(1)} collective-permute-done((bf16[1,128,1280]{2,1,0:T(8,128)(2,1)}, bf16[1,128,1280]{2,1,0:T(8,128)(2,1)S(1)}, u32[]{:S(2)}, u32[]{:S(2)}) %collective-permute-start.18) | collective-permute-done | bytes 327712 | tf_op jit(solution)/shard_map/ppermute | solution.py:534
  329.6 7.2 %all-to-all-start.4 = ((bf16[16,112,128]{2,1,0:T(8,128)(2,1)}), bf16[16,112,128]{2,1,0:T(8,128)(2,1)S(1)}, u32[]{:S(2)}, u32[]{:S(2)}) async-start(bf16[16,112,128]{2,1,0:T(8,128)(2,1)} %copy-done.13), calls=%async_computation.4 | async-start | bytes 917504 | tf_op jit(solution)/shard_map/all_to_all | solution.py:530
  336.8 7.1 %input_grad.1 = bf16[256,1024]{1,0:T(8,128)(2,1)} custom-call(s32[6]{0:T(128)S(1)} %stack.27.ids, bf16[16,384,128]{2,1,0:T(8,128)(2,1)} %all-to-all-done.3.got_ref, bf16[1024,3072]{1,0:T(8,128)(2,1)} %w_ref.5, bf16[1024,3072]{1,0:T(8,128)(2,1)} %w_ref.5, bf16[1024,3072]{1,0:T(8,128)(2,1)} %w_ref.5, bf16[256,1024]{1,0:T(8,128)(2,1)S(1)} %bitcast.46, ...), custom_call_target="tpu_custom_call" | custom-call | flops 1610612736 | bytes 22022144 | tf_op jit(solution)/shard_map/input_grad/pallas_call | solution.py:235
  346.8 6.9 %collective-permute-done.20 = bf16[128,1280]{1,0:T(8,128)(2,1)S(1)} collective-permute-done((bf16[128,1280]{1,0:T(8,128)(2,1)S(1)}, bf16[128,1280]{1,0:T(8,128)(2,1)S(1)}, u32[]{:S(2)}, u32[]{:S(2)}) %collective-permute-start.20) | collective-permute-done | bytes 327712 | tf_op jit(solution)/shard_map/ppermute | solution.py:538
  357.4 9.0 %collective-permute-done.17.two_ref = bf16[16,112,128]{2,1,0:T(8,128)(2,1)S(1)} collective-permute-done((bf16[16,112,128]{2,1,0:T(8,128)(2,1)S(1)}, bf16[16,112,128]{2,1,0:T(8,128)(2,1)S(1)}, u32[]{:S(2)}, u32[]{:S(2)}) %collective-permute-start.17) | collective-permute-done | bytes 458784 | tf_op jit(solution)/shard_map/ppermute | solution.py:538
  366.5 2.8 finish.1
  (206 shorter events, 60.2 us)
Async XLA Ops:
  17.3 42.6 %all-to-all-start = ((bf16[16,384,128]{2,1,0:T(8,128)(2,1)}), bf16[16,384,128]{2,1,0:T(8,128)(2,1)S(1)}, u32[]{:S(2)}, u32[]{:S(2)}) async-start(bf16[16,384,128]{2,1,0:T(8,128)(2,1)} %get-tuple-element.104), calls=%async_computation | async-start | bytes 3145728 | tf_op jit(solution)/shard_map/all_to_all | solution.py:530
  23.4 139.5 %all-gather.2.cloned.1.call-start = ((), (), s32[]{:S(2)}) async-start(), calls=%async_computation.5 | async-start | bytes 8912896 | tf_op jit(solution)/shard_map/all_gather | solution.py:608
  23.5 28.6 %collective-permute-start.1 = (bf16[256,1024]{1,0:T(8,128)(2,1)S(1)}, bf16[256,1024]{1,0:T(8,128)(2,1)S(1)}, u32[]{:S(2)}, u32[]{:S(2)}) collective-permute-start(bf16[256,1024]{1,0:T(8,128)(2,1)S(1)} %bitcast.47), channel_id=1, source_target_pairs={{0,2},{1,3},{2,0},{3,1},{4,6},{5,7},{6,4},{7,5},{8,10},{9,11},{10,... | collective-permute-start | bytes 1572872 | tf_op jit(solution)/shard_map/ppermute | solution.py:534
  25.0 27.1 %collective-permute-start = (bf16[256,1024]{1,0:T(8,128)(2,1)S(1)}, bf16[256,1024]{1,0:T(8,128)(2,1)S(1)}, u32[]{:S(2)}, u32[]{:S(2)}) collective-permute-start(bf16[256,1024]{1,0:T(8,128)(2,1)S(1)} %bitcast.48), channel_id=1, source_target_pairs={{0,1},{1,0},{2,3},{3,2},{4,5},{5,4},{6,7},{7,6},{8,9},{9,8},{10,11... | collective-permute-start | bytes 1572872 | tf_op jit(solution)/shard_map/ppermute | solution.py:534
  52.1 1.9 collective-permute-start.2
  61.0 65.6 %copy-start.5 = (bf16[1,256,1024]{2,1,0:T(8,128)(2,1)S(1)}, bf16[1,256,1024]{2,1,0:T(8,128)(2,1)}, u32[]{:S(2)}) copy-start(bf16[1,256,1024]{2,1,0:T(8,128)(2,1)} %param.15) | copy-start | bytes 1572868
  61.0 65.6 %copy-start.34 = (f32[1024]{0:T(1024)S(1)}, f32[1024]{0:T(1024)}, u32[]{:S(2)}) copy-start(f32[1024]{0:T(1024)} %param.23) | copy-start | bytes 12292
  61.0 65.6 %copy-start.35 = (f32[1024]{0:T(1024)S(1)}, f32[1024]{0:T(1024)}, u32[]{:S(2)}) copy-start(f32[1024]{0:T(1024)} %param.22) | copy-start | bytes 12292
  93.4 33.1 %all-to-all-start.1 = ((bf16[16,128,128]{2,1,0:T(8,128)(2,1)}), bf16[16,128,128]{2,1,0:T(8,128)(2,1)S(1)}, u32[]{:S(2)}, u32[]{:S(2)}) async-start(bf16[16,128,128]{2,1,0:T(8,128)(2,1)} %get-tuple-element.107), calls=%async_computation.1 | async-start | bytes 1048576 | tf_op jit(solution)/shard_map/all_to_all | solution.py:530
  145.5 17.5 %collective-permute-start.5 = (bf16[256,1024]{1,0:T(8,128)(2,1)}, bf16[256,1024]{1,0:T(8,128)(2,1)}, u32[]{:S(2)}, u32[]{:S(2)}) collective-permute-start(bf16[256,1024]{1,0:T(8,128)(2,1)} %get-tuple-element.113), channel_id=1, source_target_pairs={{0,1},{1,0},{2,3},{3,2},{4,5},{5,4},{6,7},{7,6},{8,9},{9,8},{10,11... | collective-permute-start | bytes 1572872 | tf_op jit(solution)/shard_map/ppermute | solution.py:534
  145.6 17.4 %collective-permute-start.6 = (bf16[256,1024]{1,0:T(8,128)(2,1)}, bf16[256,1024]{1,0:T(8,128)(2,1)}, u32[]{:S(2)}, u32[]{:S(2)}) collective-permute-start(bf16[256,1024]{1,0:T(8,128)(2,1)} %get-tuple-element.114), channel_id=1, source_target_pairs={{0,2},{1,3},{2,0},{3,1},{4,6},{5,7},{6,4},{7,5},{8,10},{9,11},{10,... | collective-permute-start | bytes 1572872 | tf_op jit(solution)/shard_map/ppermute | solution.py:534
  145.7 25.4 %collective-permute-start.7 = (bf16[256,1024]{1,0:T(8,128)(2,1)}, bf16[256,1024]{1,0:T(8,128)(2,1)}, u32[]{:S(2)}, u32[]{:S(2)}) collective-permute-start(bf16[256,1024]{1,0:T(8,128)(2,1)} %get-tuple-element.115), channel_id=1, source_target_pairs={{0,3},{1,2},{2,1},{3,0},{4,7},{5,6},{6,5},{7,4},{8,11},{9,10},{10,... | collective-permute-start | bytes 1572872 | tf_op jit(solution)/shard_map/ppermute | solution.py:534
  171.0 8.3 %collective-permute-start.8 = (bf16[256,4096]{1,0:T(8,128)(2,1)}, bf16[256,4096]{1,0:T(8,128)(2,1)}, u32[]{:S(2)}, u32[]{:S(2)}) collective-permute-start(bf16[256,4096]{1,0:T(8,128)(2,1)} %get-tuple-element.119.ua_ref.ub_ref), channel_id=1, source_target_pairs={{0,1},{1,0},{2,3},{3,2},{4,5},{5,4},{6,7},{7,6},{8,9},{9,8},{10,11... | collective-permute-start | bytes 6291464 | tf_op jit(solution)/shard_map/ppermute | solution.py:534
  172.6 6.7 %collective-permute-start.4 = (bf16[256,1024]{1,0:T(8,128)(2,1)S(1)}, bf16[256,1024]{1,0:T(8,128)(2,1)}, u32[]{:S(2)}, u32[]{:S(2)}) collective-permute-start(bf16[256,1024]{1,0:T(8,128)(2,1)S(1)} %get-tuple-element.199.a_ref), channel_id=1, source_target_pairs={{0,1},{1,0},{2,3},{3,2},{4,5},{5,4},{6,7},{7,6},{8,9},{9,8},{10,11... | collective-permute-start | bytes 1572872 | tf_op jit(solution)/shard_map/ppermute | solution.py:534
  172.9 6.5 %collective-permute-start.3 = (bf16[256,1024]{1,0:T(8,128)(2,1)S(1)}, bf16[256,1024]{1,0:T(8,128)(2,1)}, u32[]{:S(2)}, u32[]{:S(2)}) collective-permute-start(bf16[256,1024]{1,0:T(8,128)(2,1)S(1)} %get-tuple-element.200.n_ref), channel_id=1, source_target_pairs={{0,1},{1,0},{2,3},{3,2},{4,5},{5,4},{6,7},{7,6},{8,9},{9,8},{10,11... | collective-permute-start | bytes 1572872 | tf_op jit(solution)/shard_map/ppermute | solution.py:534
  173.1 6.2 %collective-permute-start.9 = (bf16[256,1024]{1,0:T(8,128)(2,1)}, bf16[256,1024]{1,0:T(8,128)(2,1)S(1)}, u32[]{:S(2)}, u32[]{:S(2)}) collective-permute-start(bf16[256,1024]{1,0:T(8,128)(2,1)} %get-tuple-element.197.g_ref.ba_ref.bb_ref), channel_id=1, source_target_pairs={{0,1},{1,0},{2,3},{3,2},{4,5},{5,4},{6,7},{7,6},{8,9},{9,8},{10,11... | collective-permute-start | bytes 1572872 | tf_op jit(solution)/shard_map/ppermute | solution.py:534
  173.4 28.4 %all-to-all-start.2 = ((bf16[16,144,128]{2,1,0:T(8,128)(2,1)}), bf16[16,144,128]{2,1,0:T(8,128)(2,1)}, u32[]{:S(2)}, u32[]{:S(2)}) async-start(bf16[16,144,128]{2,1,0:T(8,128)(2,1)} %copy-done.8), calls=%async_computation.2 | async-start | bytes 1179648 | tf_op jit(solution)/shard_map/all_to_all | solution.py:530
  190.7 34.5 %collective-permute-start.10 = (bf16[4,64,2560]{2,1,0:T(8,128)(2,1)}, bf16[4,64,2560]{2,1,0:T(8,128)(2,1)}, u32[]{:S(2)}, u32[]{:S(2)}) collective-permute-start(bf16[4,64,2560]{2,1,0:T(8,128)(2,1)} %get-tuple-element.120), channel_id=1, source_target_pairs={{0,2},{1,3},{2,0},{3,1},{4,6},{5,7},{6,4},{7,5},{8,10},{9,11},{10,... | collective-permute-start | bytes 3932168 | tf_op jit(solution)/shard_map/ppermute | solution.py:534
  192.1 33.1 %collective-permute-start.11 = (bf16[512,1280]{1,0:T(8,128)(2,1)}, bf16[512,1280]{1,0:T(8,128)(2,1)}, u32[]{:S(2)}, u32[]{:S(2)}) collective-permute-start(bf16[512,1280]{1,0:T(8,128)(2,1)} %get-tuple-element.121), channel_id=1, source_target_pairs={{0,16},{16,0},{1,17},{17,1},{2,18},{18,2},{3,19},{19,3},{4,20},{20... | collective-permute-start | bytes 3932168 | tf_op jit(solution)/shard_map/ppermute | solution.py:538
  200.3 25.0 %collective-permute-start.12 = (bf16[2,256,1024]{2,1,0:T(8,128)(2,1)}, bf16[2,256,1024]{2,1,0:T(8,128)(2,1)}, u32[]{:S(2)}, u32[]{:S(2)}) collective-permute-start(bf16[2,256,1024]{2,1,0:T(8,128)(2,1)} %get-tuple-element.129), channel_id=1, source_target_pairs={{0,4},{1,5},{2,6},{3,7},{4,0},{5,1},{6,2},{7,3},{8,12},{9,13},{10,... | collective-permute-start | bytes 3145736 | tf_op jit(solution)/shard_map/ppermute | solution.py:534
  230.5 34.1 %collective-permute-start.16 = (bf16[1,256,1024]{2,1,0:T(8,128)(2,1)S(1)}, bf16[1,256,1024]{2,1,0:T(8,128)(2,1)S(1)}, u32[]{:S(2)}, u32[]{:S(2)}) collective-permute-start(bf16[1,256,1024]{2,1,0:T(8,128)(2,1)S(1)} %get-tuple-element.165), channel_id=1, source_target_pairs={{0,8},{1,9},{2,10},{3,11},{4,12},{5,13},{6,14},{7,15},{8,0},{9,1},... | collective-permute-start | bytes 1572872 | tf_op jit(solution)/shard_map/ppermute | solution.py:534
  231.1 15.0 %collective-permute-start.13 = (bf16[4,64,1280]{2,1,0:T(8,128)(2,1)S(1)}, bf16[4,64,1280]{2,1,0:T(8,128)(2,1)S(1)}, u32[]{:S(2)}, u32[]{:S(2)}) collective-permute-start(bf16[4,64,1280]{2,1,0:T(8,128)(2,1)S(1)} %get-tuple-element.149), channel_id=1, source_target_pairs={{0,16},{16,0},{1,17},{17,1},{2,18},{18,2},{3,19},{19,3},{4,20},{20... | collective-permute-start | bytes 1966088 | tf_op jit(solution)/shard_map/ppermute | solution.py:538
  231.4 14.8 %collective-permute-start.14 = (bf16[4,64,1280]{2,1,0:T(8,128)(2,1)S(1)}, bf16[4,64,1280]{2,1,0:T(8,128)(2,1)S(1)}, u32[]{:S(2)}, u32[]{:S(2)}) collective-permute-start(bf16[4,64,1280]{2,1,0:T(8,128)(2,1)S(1)} %get-tuple-element.150), channel_id=1, source_target_pairs={{0,2},{1,3},{2,0},{3,1},{4,6},{5,7},{6,4},{7,5},{8,10},{9,11},{10,... | collective-permute-start | bytes 1966088 | tf_op jit(solution)/shard_map/ppermute | solution.py:534
  247.9 20.3 %collective-permute-start.15 = (bf16[2,128,1280]{2,1,0:T(8,128)(2,1)S(1)}, bf16[2,128,1280]{2,1,0:T(8,128)(2,1)S(1)}, u32[]{:S(2)}, u32[]{:S(2)}) collective-permute-start(bf16[2,128,1280]{2,1,0:T(8,128)(2,1)S(1)} %get-tuple-element.164), channel_id=1, source_target_pairs={{0,4},{1,5},{2,6},{3,7},{4,0},{5,1},{6,2},{7,3},{8,12},{9,13},{10,... | collective-permute-start | bytes 1966088 | tf_op jit(solution)/shard_map/ppermute | solution.py:534
  269.0 42.9 %all-to-all-start.3 = ((bf16[16,384,128]{2,1,0:T(8,128)(2,1)}), bf16[16,384,128]{2,1,0:T(8,128)(2,1)}, u32[]{:S(2)}, u32[]{:S(2)}) async-start(bf16[16,384,128]{2,1,0:T(8,128)(2,1)} %attend_back.5.dx_ref), calls=%async_computation.3 | async-start | bytes 3145728 | tf_op jit(solution)/shard_map/all_to_all | solution.py:530
  277.7 41.6 %collective-permute-start.21 = (bf16[512]{0:T(512)(128)(2,1)S(1)}, bf16[512]{0:T(512)(128)(2,1)S(1)}, u32[]{:S(2)}, u32[]{:S(2)}) collective-permute-start(bf16[512]{0:T(512)(128)(2,1)S(1)} %bitcast.67), channel_id=1, source_target_pairs={{0,16},{16,0},{1,17},{17,1},{2,18},{18,2},{3,19},{19,3},{4,20},{20... | collective-permute-start | bytes 3080 | tf_op jit(solution)/shard_map/ppermute | solution.py:525
  289.3 29.9 %collective-permute-start.19 = (bf16[1,256,512]{2,1,0:T(8,128)(2,1)}, bf16[1,256,512]{2,1,0:T(8,128)(2,1)S(1)}, u32[]{:S(2)}, u32[]{:S(2)}) collective-permute-start(bf16[1,256,512]{2,1,0:T(8,128)(2,1)} %get-tuple-element.189), channel_id=1, source_target_pairs={{0,16},{16,0},{1,17},{17,1},{2,18},{18,2},{3,19},{19,3},{4,20},{20... | collective-permute-start | bytes 786440 | tf_op jit(solution)/shard_map/ppermute | solution.py:538
  311.9 14.5 %collective-permute-start.18 = (bf16[1,128,1280]{2,1,0:T(8,128)(2,1)}, bf16[1,128,1280]{2,1,0:T(8,128)(2,1)S(1)}, u32[]{:S(2)}, u32[]{:S(2)}) collective-permute-start(bf16[1,128,1280]{2,1,0:T(8,128)(2,1)} %copy-done.43), channel_id=1, source_target_pairs={{0,8},{1,9},{2,10},{3,11},{4,12},{5,13},{6,14},{7,15},{8,0},{9,1},... | collective-permute-start | bytes 983048 | tf_op jit(solution)/shard_map/ppermute | solution.py:534
  328.0 17.7 %collective-permute-start.22 = (bf16[256,512]{1,0:T(8,128)(2,1)S(1)}, bf16[256,512]{1,0:T(8,128)(2,1)S(1)}, u32[]{:S(2)}, u32[]{:S(2)}) collective-permute-start(bf16[256,512]{1,0:T(8,128)(2,1)S(1)} %bitcast.52), channel_id=1, source_target_pairs={{0,16},{16,0},{1,17},{17,1},{2,18},{18,2},{3,19},{19,3},{4,20},{20... | collective-permute-start | bytes 786440 | tf_op jit(solution)/shard_map/ppermute | solution.py:538
  329.6 25.1 %all-to-all-start.4 = ((bf16[16,112,128]{2,1,0:T(8,128)(2,1)}), bf16[16,112,128]{2,1,0:T(8,128)(2,1)S(1)}, u32[]{:S(2)}, u32[]{:S(2)}) async-start(bf16[16,112,128]{2,1,0:T(8,128)(2,1)} %copy-done.13), calls=%async_computation.4 | async-start | bytes 917504 | tf_op jit(solution)/shard_map/all_to_all | solution.py:530
  344.0 9.8 %collective-permute-start.20 = (bf16[128,1280]{1,0:T(8,128)(2,1)S(1)}, bf16[128,1280]{1,0:T(8,128)(2,1)S(1)}, u32[]{:S(2)}, u32[]{:S(2)}) collective-permute-start(bf16[128,1280]{1,0:T(8,128)(2,1)S(1)} %bitcast.51), channel_id=1, source_target_pairs={{0,16},{16,0},{1,17},{17,1},{2,18},{18,2},{3,19},{19,3},{4,20},{20... | collective-permute-start | bytes 983048 | tf_op jit(solution)/shard_map/ppermute | solution.py:538
  354.7 11.7 %collective-permute-start.17 = (bf16[16,112,128]{2,1,0:T(8,128)(2,1)S(1)}, bf16[16,112,128]{2,1,0:T(8,128)(2,1)S(1)}, u32[]{:S(2)}, u32[]{:S(2)}) collective-permute-start(bf16[16,112,128]{2,1,0:T(8,128)(2,1)S(1)} %all-to-all-done.4.one_ref), channel_id=1, source_target_pairs={{0,16},{16,0},{1,17},{17,1},{2,18},{18,2},{3,19},{19,3},{4,20},{20... | collective-permute-start | bytes 1376264 | tf_op jit(solution)/shard_map/ppermute | solution.py:538
  (55 other events, 592.2 us)
Sparse Core Ops, SparseCore 0:
  60.0 79.5 all-gather.1

commit v3 on v2

--- a/solution.py
+++ b/solution.py
@@ -121,7 +121,7 @@
             out_specs=[pl.BlockSpec((bq//tokens,tokens//2,128),lambda i,*_:(i,0,0)),blk(128),blk(128),whole(128),whole(128)],
             scratch_shapes=[pltpu.VMEM((full//bk,bq,bk),F32),pltpu.VMEM((full,128),BF)]),
         out_shape=[jax.ShapeDtypeStruct((ranks,tokens//2,128),BF),jax.ShapeDtypeStruct((full,128),F32)]+[jax.ShapeDtypeStruct((full,128),BF)]*3,
-        compiler_params=pltpu.CompilerParams(vmem_limit_bytes=50<<20),
+        compiler_params=pltpu.CompilerParams(vmem_limit_bytes=full//1024*(22<<18)),
         cost_estimate=pl.CostEstimate(flops=full*full*512,bytes_accessed=full*1600,transcendentals=full*full//2),
         name="attend")(starts,part,x)
 
@@ -202,9 +202,8 @@
                     dx_ref[r//tokens,:tokens,:]=jnp.where(lanes_low(kv.shape),dq[c*tokens:(c+1)*tokens],kv).astype(BF)
                     dx_ref[r//tokens,tokens:,:]=pair_up(kv[:half],kv[half:]).astype(BF)
 
-def attend_back(starts, qa, ka, va, rest, *, bq, bk, begin, count, tokens):
+def attend_back(starts, qa, ka, va, rest, *, bq, bk, begin, count, tokens, first, last):
     full=qa.shape[0]; segs=starts.shape[0]
-    first=begin==0; last=begin+count==full//bk
     fixed=lambda shape: pl.BlockSpec(shape,lambda i,*_:(0,)*len(shape))
     dq_shape=(full//bq,64,bq); kt=pltpu.VMEM((count,64,bk),BF)
     if last:
@@ -223,18 +222,20 @@
             out_specs=[fixed(o.shape) for o in outs],
             scratch_shapes=scratch),
         out_shape=outs,
-        compiler_params=pltpu.CompilerParams(vmem_limit_bytes=50<<20),
+        compiler_params=pltpu.CompilerParams(vmem_limit_bytes=full//1024*((48 if first else 24)<<18)),
         cost_estimate=pl.CostEstimate(flops=int(area*1280),bytes_accessed=full*2000,transcendentals=int(area/2)),
         name="attend_back")(starts,qa,ka,va,*rest)
 
 def fixed_block(shape):
     return pl.BlockSpec(shape,lambda s,*_:(0,)*len(shape))
+
+ROOM={"project": 48}
 
 def run_kernel(kernel, ids, grid, ins, in_specs, outs, out_specs, scratch, name, flops):
     moved=sum(math.prod(v.shape)*2 for v in ins)+sum(math.prod(o.shape)*2 for o in outs)
     return pl.pallas_call(kernel,
         grid_spec=pltpu.PrefetchScalarGridSpec(num_scalar_prefetch=1,grid=grid,in_specs=in_specs,out_specs=out_specs,scratch_shapes=scratch),
-        out_shape=outs,compiler_params=pltpu.CompilerParams(vmem_limit_bytes=50<<20),
+        out_shape=outs,compiler_params=pltpu.CompilerParams(vmem_limit_bytes=ROOM.get(name,20)<<20),
         cost_estimate=pl.CostEstimate(flops=flops,bytes_accessed=moved,transcendentals=0),name=name)(ids,*ins)
 
 def pick_kernel(ids, h_ref, *outs, wide):
@@ -315,34 +316,33 @@
         [f,f,f,f,at(0),at(0),at(4),at(4),fix(0),fix(0),fix(1),fix(1)],[a,a,b,b],[fixed_block(v.shape) for v in (a,a,b,b)],
         [pltpu.VMEM((2*tokens,tile),BF)]*2,"grads_up",2*tokens*width*(up.shape[1]+width))
 
-def add_kernel(ids, *refs, plan, joined):
-    n=len(plan); ins,outs=refs[:2*n],refs[2*n:]
-    for p,(mode,which) in enumerate(plan):
-        k_ref,r_ref=ins[2*p:2*p+2]
-        def total(index): return (k_ref[index].astype(F32)+r_ref[index].astype(F32)).astype(BF)
-        if mode=="sum":
-            outs[p][...]=total(...); continue
-        for o in range(2):
-            half=ids[which] if o else 1-ids[which]
-            out=outs[o] if joined else outs[2*p+o]
-            for i in range(out.shape[0]):
-                if mode=="columns":
-                    width=k_ref.shape[2]//2
-                    v=total((i,slice(None),pl.ds(pl.multiple_of(half*width,128),width)))
-                else:
-                    v=total((2*i+half,))
-                rows=v.shape[0]
-                if joined: out[i,p*rows:(p+1)*rows,:]=v
-                else: out[i]=v
-
-def add_split(ids, plan, arrays, name, joined=False):
-    shapes=[]
-    for p,(mode,_) in enumerate(plan):
-        m,r,c=arrays[2*p].shape
-        shapes.append((m,r,c) if mode=="sum" else (m,r,c//2) if mode=="columns" else (m//2,r,c))
-    if joined: outs=[(shapes[0][0],shapes[0][1]*len(plan),shapes[0][2])]*2
-    else: outs=[s for s,(mode,_) in zip(shapes,plan) for _ in range(1 if mode=="sum" else 2)]
-    return run_kernel(functools.partial(add_kernel,plan=plan,joined=joined),ids,(1,),arrays,[fixed_block(a.shape) for a in arrays],
+def add_kernel(ids, *refs, plan):
+    n=sum(len(parts) for _,_,parts in plan)
+    ins,outs=list(refs[:2*n]),list(refs[2*n:])
+    for mode,which,parts in plan:
+        made=[outs.pop(0) for _ in range(1 if mode=="sum" else 2)]
+        base=0
+        for part in parts:
+            k_ref,r_ref=ins.pop(0),ins.pop(0)
+            def total(index): return (k_ref[index].astype(F32)+r_ref[index].astype(F32)).astype(BF)
+            for o,out in enumerate(made):
+                half=ids[which] if o else 1-ids[which]
+                for i in range(out.shape[0]):
+                    if mode=="sum": v=total((i,))
+                    elif mode=="columns":
+                        width=k_ref.shape[2]//2
+                        v=total((i,slice(None),pl.ds(pl.multiple_of(half*width,128),width)))
+                    else: v=total((2*i+half,))
+                    out[i,base:base+v.shape[0],:]=v
+            base+=k_ref.shape[1]
+
+def add_split(ids, plan, arrays, name):
+    outs=[]; at=0
+    for mode,_,parts in plan:
+        m,_,c=arrays[at].shape
+        r=sum(arrays[at+2*i].shape[1] for i in range(len(parts))); at+=2*len(parts)
+        outs+=[(m,r,c)] if mode=="sum" else [(m,r,c//2) if mode=="columns" else (m//2,r,c)]*2
+    return run_kernel(functools.partial(add_kernel,plan=plan),ids,(1,),arrays,[fixed_block(a.shape) for a in arrays],
         [jax.ShapeDtypeStruct(s,BF) for s in outs],[fixed_block(s) for s in outs],[],name,sum(math.prod(s) for s in outs))
 
 def project_kernel(ids, x_ref, gain_ref, shift_ref, wq_ref, wk_ref, wv_ref, bq_ref, bv_ref, packed_ref, normed_ref):
@@ -375,11 +375,11 @@
 def unpack_tile(one, two):
     return jnp.concatenate([pair_up(one,two),pair_down(one,two)],axis=0)
 
-def mix_kernel(ids, got_ref, w_ref, x_ref, bias_ref, gain_ref, shift_ref, left_ref, res_ref):
+def mix_kernel(ids, got_ref, w_ref, x_ref, bias_ref, gain_ref, shift_ref, two_ref, att_ref, res_ref):
     s=pl.program_id(0); width=x_ref.shape[1]
     tiles=[unpack_tile(got_ref[2*p].astype(F32),got_ref[2*p+1].astype(F32)).astype(BF) for p in range(2)]
     att=jnp.concatenate(tiles,axis=1)
-    left_ref[:,pl.ds(pl.multiple_of(width+s*256,256),256)]=att
+    att_ref[:,pl.ds(pl.multiple_of(s*256,256),256)]=att
     @pl.when(s==0)
     def _(): res_ref[...]=x_ref[...].astype(F32)+bias_ref[...]
     res_ref[...]+=dotf(att,w_ref[...],NN)
@@ -388,14 +388,13 @@
         x=res_ref[...]
         x=x-jnp.mean(x,axis=1,keepdims=True)
         x=x*lax.rsqrt(jnp.mean(x*x,axis=1,keepdims=True)+EPSILON)
-        left_ref[:,:width]=(x*gain_ref[...]+shift_ref[...]).astype(BF)
+        two_ref[...]=(x*gain_ref[...]+shift_ref[...]).astype(BF)
 
 def mix(ids, got, w_out, x, bias, gain, shift):
     tokens,width=x.shape; row=fixed_block((1,width))
     return run_kernel(mix_kernel,ids,(width//256,),[got,w_out,x,bias[None],gain[None],shift[None]],
         [pl.BlockSpec((4,tokens//2,128),lambda s,ids:(s,0,0)),pl.BlockSpec((256,width),lambda s,ids:(s,0)),fixed_block(x.shape),row,row,row],
-        [jax.ShapeDtypeStruct((tokens,2*width),BF),jax.ShapeDtypeStruct((tokens,width),F32)],
-        [fixed_block((tokens,2*width)),fixed_block((tokens,width))],[],"mix",2*tokens*width*width)
+        [jax.ShapeDtypeStruct((tokens,width),t) for t in (BF,BF,F32)],[fixed_block((tokens,width))]*3,[],"mix",2*tokens*width*width)
 
 def grad_pack_kernel(ids, g_ref, w_ref, small_ref, out_ref):
     half=g_ref.shape[0]//2
@@ -419,6 +418,7 @@
         v=dx_ref[c,tokens:,:].astype(F32)
         v=jnp.concatenate([v,pltpu.roll(v,HEAD_DIM,1)],axis=0)
         v=jnp.where(lanes_low(v.shape),v,0.0).astype(BF)
+        out_ref[s*dx_ref.shape[0]+c,:tokens+half,:]=dx_ref[c]
         sides.append(jnp.concatenate([dx_ref[c,:tokens,:],v],axis=1))
     side=jnp.concatenate(sides,axis=0)
     @pl.when(s==0)
@@ -434,14 +434,15 @@
         extra=jnp.where(line==0,high[:,:128],jnp.where(line==1,rest[:,:128],jnp.where(line==2,high[:,128:],jnp.where(line==3,rest[:,128:],0.0))))
         for r in range(out_ref.shape[0]):
             rows=slice(r*share,(r+1)*share)
-            out_ref[r,:share,:]=acc_ref[rows,:128].astype(BF)
+            base=tokens+half
+            out_ref[r,base:base+share,:]=acc_ref[rows,:128].astype(BF)
             v=acc_ref[rows,128:]
-            out_ref[r,share:share+share//2,:]=pair_up(v[:share//2],v[share//2:]).astype(BF)
-            out_ref[r,share+share//2:,:]=extra.astype(BF)
+            out_ref[r,base+share:base+share+share//2,:]=pair_up(v[:share//2],v[share//2:]).astype(BF)
+            out_ref[r,base+share+share//2:,:]=extra.astype(BF)
 
 def weight_message(ids, normed_all, dx):
     ranks,rows,_=dx.shape; tokens=rows//3*2; full,width=normed_all.shape; share=width//ranks
-    step=4; shape=(ranks,share//2*3+16,128)
+    step=4; shape=(ranks,rows+share//2*3+16,128)
     return run_kernel(functools.partial(message_kernel,tokens=tokens,share=share),ids,(ranks//step,),[normed_all,dx],
         [pl.BlockSpec((step*tokens,width),lambda s,ids:(s,0)),pl.BlockSpec((step,rows,128),lambda s,ids:(s,0,0))],
         [jax.ShapeDtypeStruct(shape,BF)],[fixed_block(shape)],
@@ -482,7 +483,7 @@
     for p in range(2):
         a,b=got_ref[2*p].astype(F32),got_ref[2*p+1].astype(F32)
         q.append(pair_up(a[:tokens],b[:tokens])); k.append(pair_down(a[:tokens],b[:tokens]))
-        v.append(unpack_tile(a[tokens:],b[tokens:]))
+        v.append(unpack_tile(a[tokens:tokens//2*3],b[tokens:tokens//2*3]))
     total=acc_ref[...]
     for tiles,w_ref in ((q,wq_ref),(k,wk_ref),(v,wv_ref)):
         total=total+dotf(jnp.concatenate(tiles,axis=1).astype(BF),w_ref[...],NT)
@@ -582,6 +583,7 @@
     group = max(1, ranks // HEADS)
     full = ranks * tokens
     share = feature // ranks
+    wide = w_up.shape[1] // ranks
     lengths = seg_lengths[0]
     starts = jnp.cumsum(lengths, dtype=jnp.int32) - lengths
     part = (me % group).astype(jnp.int32)[None]
@@ -609,8 +611,7 @@
     normed_low, packed = lax.optimization_barrier((normed_low, packed))
     normed_all = gather(normed_low)
     low, out, qa, ka, va = attend(starts, part, packed, bq=FWD_TILE[0], bk=FWD_TILE[1], group=group)
-    left, residual = mix(ids, fold(exchange(low)), w_out, frames[0], bias_out, ln2_gain, ln2_bias)
-    normed_two_low, attended_low = left[:, :feature], left[:, feature:]
+    normed_two_low, attended_low, residual = mix(ids, fold(exchange(low)), w_out, frames[0], bias_out, ln2_gain, ln2_bias)
     unit_two, scale_two = statistics(residual)
     up_proj = dotf(normed_two_low, w_up, NN) + bias_up
     phi = 0.5 * (1.0 + lax.erf(up_proj * (0.5**0.5)))
@@ -624,6 +625,23 @@
     normed_two_grad = dotf(up_grad, w_up, NT)
     residual_grad = cot + norm_back(unit_two, scale_two, ln2_gain, normed_two_grad)
     branch_grad = residual_grad.astype(BF)
+    if fast:
+        a_sent, a_keep, b_sent, b_keep = grads_up(
+            ids,
+            normed_two_low,
+            swap(normed_two_low, 1),
+            attended_low,
+            swap(attended_low, 1),
+            up_grad,
+            swap(up_grad, 1),
+            branch_grad,
+            swap(branch_grad, 1),
+            ranks,
+        )
+        branch_grad, a_sent, b_sent = lax.optimization_barrier((branch_grad, a_sent, b_sent))
+        others = [swap(v, k + 1) for k, v in enumerate(picked)]
+        branch_grad, others = lax.optimization_barrier((branch_grad, others))
+        a_got, b_got = swap(a_sent, 2), swap_row(b_sent)
 
     def piece(value):
         return value.reshape(ranks, -1)
@@ -653,60 +671,42 @@
     back = functools.partial(attend_back, starts, qa, ka, va, bq=BWD_TILE[0], bk=BWD_TILE[1], tokens=tokens)
     tiles = full // BWD_TILE[1]
     if fast:
-        others = [swap(v, k + 1) for k, v in enumerate(picked)]
-        others, up_grad, _ = lax.optimization_barrier((others, up_grad, sent))
+        blocks = lambda v: v.reshape(ranks // 2, share, -1)
+        a_sent, a_keep, b_sent, b_keep = add_split(
+            ids, (("columns", 2, "a"), ("blocks", 1, "b")), [a_keep, a_got, blocks(b_keep), blocks(b_got)], "add_one"
+        )
+        got, a_sent, b_sent = lax.optimization_barrier((got, a_sent, b_sent))
+        a_got, b_got = swap_row(a_sent), swap(b_sent, 2)
         down_sent, down_keep = grads_down(ids, hidden, others, cots, ranks)
+        got, down_sent = lax.optimization_barrier((got, down_sent))
         down_got = swap(down_sent, 4)
-        a_sent, a_keep, b_sent, b_keep = grads_up(
+        one = back((got, out), begin=tiles // 4, count=tiles // 4, first=True, last=False)
+        a_got, b_got, down_got, one = lax.optimization_barrier((a_got, b_got, down_got, one))
+        up_sent, up_keep, down_sent, down_keep = add_split(
             ids,
-            normed_two_low,
-            swap(normed_two_low, 1),
-            attended_low,
-            swap(attended_low, 1),
-            up_grad,
-            swap(up_grad, 1),
-            branch_grad,
-            swap(branch_grad, 1),
-            ranks,
+            (("blocks", 3, "ab"), ("columns", 2, "d")),
+            [a_keep, a_got, b_keep, b_got, down_keep, down_got],
+            "add_two",
         )
-        a_got, b_got = swap(a_sent, 2), swap_row(b_sent)
-        one = back((got, out), begin=0, count=tiles // 4)
-        a_got, b_got, down_got, one = lax.optimization_barrier((a_got, b_got, down_got, one))
-        blocks = lambda v: v.reshape(ranks // 2, share, -1)
-        a_sent, a_keep, b_sent, b_keep, down_sent, down_keep = add_split(
-            ids,
-            (("columns", 2), ("blocks", 1), ("blocks", 4)),
-            [a_keep, a_got, blocks(b_keep), blocks(b_got), down_keep, down_got],
-            "add_one",
+        one, up_sent, down_sent = lax.optimization_barrier((one, up_sent, down_sent))
+        up_got, down_got = swap(up_sent, 4), swap_row(down_sent)
+        two = back(one, begin=0, count=tiles // 4, first=False, last=False)
+        two = [one[0], two[0], jnp.concatenate([two[1], one[2]], axis=0)]
+        up_got, down_got, two = lax.optimization_barrier((up_got, down_got, two))
+        up_sent, up_keep, down_sent, down_keep = add_split(
+            ids, (("blocks", 4, "u"), ("blocks", 4, "d")), [up_keep, up_got, down_keep, down_got], "add_three"
         )
-        one, a_sent, b_sent, down_sent = lax.optimization_barrier((one, a_sent, b_sent, down_sent))
-        a_got, b_got, down_got = swap_row(a_sent), swap(b_sent, 2), swap(down_sent, 8)
-        two = back(one, begin=tiles // 4, count=tiles // 4)
-        two = [one[0], two[0], jnp.concatenate([one[2], two[1]], axis=0)]
-        a_got, b_got, two = lax.optimization_barrier((a_got, b_got, two))
-        up_sent, up_keep = add_split(
-            ids, (("blocks", 3), ("blocks", 3)), [a_keep, a_got, b_keep, b_got], "add_two", joined=True
+        two, up_sent, down_sent = lax.optimization_barrier((two, up_sent, down_sent))
+        up_got, down_got = swap(up_sent, 8), swap(down_sent, 8)
+        (dx,) = back(two, begin=tiles // 2, count=tiles // 2, first=False, last=True)
+        everything = weight_message(ids, normed_all, dx)
+        up_got, down_got, everything = lax.optimization_barrier((up_got, down_got, everything))
+        up_part, down_part = add_split(
+            ids, (("sum", 0, "u"), ("sum", 0, "d")), [up_keep, up_got, down_keep, down_got], "add_four"
         )
-        two, up_sent = lax.optimization_barrier((two, up_sent))
-        up_got = swap(up_sent, 4)
-        (dx,) = back(two, begin=tiles // 2, count=tiles // 2)
-        up_got, down_got, dx = lax.optimization_barrier((up_got, down_got, dx))
-        message = weight_message(ids, normed_all, dx)
-        up_got, down_got, message = lax.optimization_barrier((up_got, down_got, message))
-        up_sent, up_keep, down_sent, down_keep = add_split(
-            ids, (("blocks", 4), ("columns", 2)), [up_keep, up_got, down_keep, down_got], "add_three"
-        )
-        down_got = swap_row(down_sent)
-        dx_got = exchange(dx)
-        up_sent, dx_got = lax.optimization_barrier((up_sent, dx_got))
-        up_got = swap(up_sent, 8)
-        up_part, down_part = add_split(
-            ids, (("sum", 0), ("sum", 0)), [up_keep, up_got, down_keep, down_got], "add_four"
-        )
-        total_down = jnp.concatenate(row_join(down_part[0]), axis=1)
         one_half, other_half = row_join(up_part[0])
+        rows_a, rows_b = slice(0, share), slice(share, 2 * share)
         width = feature
-        rows_a, rows_b = slice(0, share), slice(share, 2 * share)
         total_up = jnp.concatenate(
             [
                 one_half[rows_a],
@@ -719,6 +719,7 @@
         total_out = jnp.concatenate(
             [other_half[rows_a, 3 * width // 4 :], one_half[rows_b, width:], other_half[rows_b, width:]], axis=1
         )
+        total_down = jnp.concatenate(row_join(down_part[0]), axis=1)
     else:
         core, across = me % 2, me // 2 % 2
 
@@ -738,12 +739,11 @@
         total_down = reduced(dotf(halves(hidden), both(cot_low), TN))
         total_up = reduced(dotf(halves(normed_two_low), both(up_grad), TN))
         total_out = reduced(dotf(halves(attended_low), both(branch_grad), TN))
-        (dx,) = back((got, out), begin=0, count=tiles)
-        dx_got = exchange(dx)
-        message = weight_message(ids, normed_all, dx)
-    message, dx_got = lax.optimization_barrier((message, dx_got))
-    grad_frames = input_grad(ids, fold(dx_got), w_qkv, frames[0], ln1_gain, residual_grad)
-    mine = fold(exchange(message))
+        (dx,) = back((got, out), begin=0, count=tiles, first=True, last=True)
+        everything = weight_message(ids, normed_all, dx)
+    returned = fold(exchange(everything))
+    grad_frames = input_grad(ids, returned, w_qkv, frames[0], ln1_gain, residual_grad)
+    mine = returned[:, tokens // 2 * 3 :]
     if lax.axis_size("row") == 2:
         theirs = swap_row(mine)
     else:
@@ -754,7 +754,6 @@
     grad_bias_qv = jnp.concatenate([column_total[0, :feature], column_total[0, 2 * feature :]])
     grad_bias_qv = lax.dynamic_slice(grad_bias_qv, (me * 2 * share,), (2 * share,))
 
-    wide = w_up.shape[1] // ranks
     ends = [share, 2 * share, 3 * share, 3 * share + wide]
     grad_ln2_gain, grad_ln2_bias, grad_bias_out, grad_bias_up, grad_bias_down = jnp.split(small_total, ends)
     return (

time: 385 us -> 366 us (0.951)
  blocking collectives: 0 us -> 33.2 us
  waiting for transfers between devices: 119 us -> 90.1 us
  Pallas kernels: 133 us -> 118 us
  starting transfers between devices: 48.8 us -> 37.7 us
  local copies, waits for them, and re-layouts: 25.9 us -> 32.4 us
    all_to_all x0 -> x1, blocking collectives: none -> 33.2 us  [exchange(): return lax.all_to_all(value, 'seq', 0, 0, tiled=True)]
    all_to_all x5 -> x3, waiting for transfers between devices: 53.7 us -> 22.7 us  [exchange(): return lax.all_to_all(value, 'seq', 0, 0, tiled=True)]
    all_to_all x5 -> x3, starting transfers between devices: 30.9 us -> 20.2 us  [exchange(): return lax.all_to_all(value, 'seq', 0, 0, tiled=True)]
    ppermute x16, waiting for transfers between devices: 47.4 us -> 56.7 us  [swap(): lax.ppermute(value, 'seq', [(i, i ^ bit) for i in range(lax.axis_size('se...]
    pallas_call x13, Pallas kernels: 56.3 us -> 48.3 us  [run_kernel(): pl.pallas_call(kernel, grid_spec=pltpu.PrefetchScalarGridSpec(num_scalar_...]
    ppermute x6, waiting for transfers between devices: 17.9 us -> 10.7 us  [swap_row(): return lax.ppermute(value, 'row', [(0, 1), (1, 0)])]
    pallas_call x3, Pallas kernels: 46.9 us -> 41.9 us  [attend_back(): pl.pallas_call(functools.partial(bwd_kernel, bq=bq, bk=bk, segs=segs, beg...]
    unnamed x116 -> x108, local copies, waits for them, and re-layouts: 21.5 us -> 26.1 us
  transfers between devices with their start and end apart: 29 -> 27, of which waited for: 12 -> 13; matrix products, arithmetic and copies ran while one was open for 10% -> 10% of each run, Pallas kernels for 31% -> 30%
where the time goes in v3:
time: 366 us; the launch traced here: 360 us
  Pallas kernels  118 us (32%)
  waiting for transfers between devices  90.1 us (25%)
  starting transfers between devices  37.7 us (10%)
  blocking collectives  33.2 us (9%)
  local copies, waits for them, and re-layouts  32.4 us (9%)
  matrix products  25 us (7%)
  between operations  14.9 us (4%)
  other arithmetic  9.01 us (2%)
    ppermute x16, waiting for transfers between devices, swap(): lax.ppermute(value, 'seq', [(i, i ^ bit) for i in range(lax.axis_size('se...  56.7 us
    pallas_call x13, Pallas kernels, run_kernel(): pl.pallas_call(kernel, grid_spec=pltpu.PrefetchScalarGridSpec(num_scalar_...  48.3 us
    pallas_call x3, Pallas kernels, attend_back(): pl.pallas_call(functools.partial(bwd_kernel, bq=bq, bk=bk, segs=segs, beg...  41.9 us
    all_to_all x1, blocking collectives, exchange(): return lax.all_to_all(value, 'seq', 0, 0, tiled=True)  33.2 us
    pallas_call x1, Pallas kernels, attend(): pl.pallas_call(functools.partial(fwd_kernel, bq=bq, bk=bk, segs=segs, gro...  27.4 us
    unnamed x108, local copies, waits for them, and re-layouts  26.1 us
    dot_general x4, matrix products, dotf(): return lax.dot_general(a, b, dims, preferred_element_type=F32)  25 us
    all_to_all x3, waiting for transfers between devices, exchange(): return lax.all_to_all(value, 'seq', 0, 0, tiled=True)  22.7 us
  transfers between devices with their start and end apart: 27, of which 13 were waited for; matrix products, arithmetic and copies ran while one was open for 10% of the time, Pallas kernels for 30%

profile of v3, /device:TPU:16, one launch (start us, length us, event | category | flops | bytes accessed | tf_op | source)
XLA Modules:
  0.0 359.9 jit_solution(2277193727501168953)
XLA Ops:
  10.5 6.5 %project.1 = (bf16[16,384,128]{2,1,0:T(8,128)(2,1)S(1)}, bf16[256,1024]{1,0:T(8,128)(2,1)}) custom-call(s32[6]{0:T(128)S(1)} %stack.27.ids, bf16[256,1024]{1,0:T(8,128)(2,1)S(1)} %bitcast.49, f32[1,1024]{1,0:T(1,128)S(1)} %bitcast.59, f32[1,1024]{1,0:T(1,128)S(1)} %bitcast.64, bf16[1024,3072]{1,0:T(8,128)(2,1)} %w_ref.5, bf16[1024,3072]{1,0:T(8,128)(2,1)} %w_ref.5, ...), custom_call_target="tpu_custom_call" | custom-call | flops 1610612736 | bytes 21508096 | tf_op jit(solution)/shard_map/project/pallas_call | solution.py:236
  18.2 6.2 %all-to-all-start = ((bf16[16,384,128]{2,1,0:T(8,128)(2,1)}), bf16[16,384,128]{2,1,0:T(8,128)(2,1)S(1)}, u32[]{:S(2)}, u32[]{:S(2)}) async-start(bf16[16,384,128]{2,1,0:T(8,128)(2,1)} %copy-done.10), calls=%async_computation | async-start | bytes 3145728 | tf_op jit(solution)/shard_map/all_to_all | solution.py:531
  25.9 27.1 %collective-permute-done.1.refs_6_ = bf16[256,1024]{1,0:T(8,128)(2,1)S(1)} collective-permute-done((bf16[256,1024]{1,0:T(8,128)(2,1)S(1)}, bf16[256,1024]{1,0:T(8,128)(2,1)S(1)}, u32[]{:S(2)}, u32[]{:S(2)}) %collective-permute-start.1) | collective-permute-done | bytes 524320 | tf_op jit(solution)/shard_map/ppermute | solution.py:535
  55.7 5.1 %all-to-all-done.x_ref = bf16[16,384,128]{2,1,0:T(8,128)(2,1)S(1)} async-done(((bf16[16,384,128]{2,1,0:T(8,128)(2,1)}), bf16[16,384,128]{2,1,0:T(8,128)(2,1)S(1)}, u32[]{:S(2)}, u32[]{:S(2)}) %all-to-all-start) | async-done | bytes 1572896 | tf_op jit(solution)/shard_map/all_to_all | solution.py:531
  61.0 27.4 %attend.1 = (bf16[16,128,128]{2,1,0:T(8,128)(2,1)S(1)}, f32[4096,128]{1,0:T(8,128)S(1)}, bf16[4096,128]{1,0:T(8,128)(2,1)S(1)}, bf16[4096,128]{1,0:T(8,128)(2,1)S(1)}, bf16[4096,128]{1,0:T(8,128)(2,1)S(1)}) custom-call(s32[4]{0:T(128)S(1)} %bitcast_subtract_fusion.starts, s32[1]{0:T(128)} %constant.96.clone.1.part, bf16[16,384,128]{2,1,0:T(8,128)(2,1)S(1)} %all-to-all-done.x_ref), custom_call_target="tpu_custom_call" | custom-call | flops 8589934592 | bytes 6553600 | tf_op jit(solution)/shard_map/attend/pallas_call | solution.py:117
  88.4 33.2 %all_to_all.20.got_ref = bf16[16,128,128]{2,1,0:T(8,128)(2,1)S(1)} all-to-all(bf16[16,128,128]{2,1,0:T(8,128)(2,1)S(1)} %get-tuple-element.109), channel_id=1, replica_groups=mesh['row'=2,'seq'=16] {'seq'}, dimensions={0} | all-to-all | bytes 1048576 | tf_op jit(solution)/shard_map/all_to_all | solution.py:531
  121.7 2.7 mix.1
  124.4 5.9 %multiply_convert_fusion = (bf16[256,4096]{1,0:T(8,128)(2,1)S(1)}, f32[256,4096]{1,0:T(8,128)S(1)}) fusion(f32[4096]{0:T(1024)S(1)} %copy-done.45, bf16[256,1024]{1,0:T(8,128)(2,1)S(1)} %get-tuple-element.111.n_ref, bf16[1024,4096]{1,0:T(8,128)(2,1)} %param.25), kind=kOutput, calls=%fused_computation.8 | convolution fusion | flops 2153775104 | bytes 15220736 | tf_op jit(solution)/shard_map/dot_general | solution.py:19
  133.6 5.1 %fusion.12 = (bf16[4096]{0:T(1024)(128)(2,1)S(1)}, bf16[256,4096]{1,0:T(8,128)(2,1)}) fusion(f32[256,4096]{1,0:T(8,128)S(1)} %get-tuple-element.213, bf16[256,1024]{1,0:T(8,128)(2,1)S(1)} %bitcast.54, bf16[4096,1024]{1,0:T(8,128)(2,1)S(1)} %bitcast.75), kind=kOutput, calls=%fused_computation.41 | convolution fusion | flops 2159013888 | bytes 15212544 | tf_op jit(solution)/shard_map/dot_general | solution.py:19
  139.2 6.8 %multiply_reduce_fusion = (bf16[1024]{0:T(1024)(128)(2,1)S(1)}, f32[256]{0:T(256)S(1)}, f32[256]{0:T(256)S(1)}, bf16[1024]{0:T(1024)(128)(2,1)S(1)}, f32[256,1024]{1,0:T(8,128)S(1)}) fusion(f32[256,1024]{1,0:T(8,128)S(1)} %get-tuple-element.110, f32[256]{0:T(256)S(1)} %add_rsqrt_fusion, f32[256]{0:T(256)S(1)} %broadcast_multiply_fusion.1, ...), kind=kOutput, calls=%fused_computation.15 | convolution fusion | flops 2149840384 | bytes 12595200 | tf_op jit(solution)/shard_map/dot_general | solution.py:19
  151.6 9.1 %grads_up.1 = (bf16[4,64,2560]{2,1,0:T(8,128)(2,1)}, bf16[4,64,2560]{2,1,0:T(8,128)(2,1)S(1)}, bf16[512,1280]{1,0:T(8,128)(2,1)}, bf16[512,1280]{1,0:T(8,128)(2,1)S(1)}) custom-call(s32[6]{0:T(128)S(1)} %stack.27.ids, bf16[256,1024]{1,0:T(8,128)(2,1)S(1)} %copy-done.18, bf16[256,1024]{1,0:T(8,128)(2,1)S(1)} %collective-permute-done.3.no_ref, ...), custom_call_target="tpu_custom_call" | custom-call | flops 2684354560 | bytes 17825792 | tf_op jit(solution)/shard_map/grads_up/pallas_call | solution.py:236
  166.1 8.4 %collective-permute-done.9.refs_3_ = bf16[256,1024]{1,0:T(8,128)(2,1)} collective-permute-done((bf16[256,1024]{1,0:T(8,128)(2,1)}, bf16[256,1024]{1,0:T(8,128)(2,1)}, u32[]{:S(2)}, u32[]{:S(2)}) %collective-permute-start.9) | collective-permute-done | bytes 524320 | tf_op jit(solution)/shard_map/ppermute | solution.py:535
  176.4 3.1 grad_pack.1
  179.6 6.1 %all-to-all-start.2 = ((bf16[16,144,128]{2,1,0:T(8,128)(2,1)}), bf16[16,144,128]{2,1,0:T(8,128)(2,1)}, u32[]{:S(2)}, u32[]{:S(2)}) async-start(bf16[16,144,128]{2,1,0:T(8,128)(2,1)} %grad_pack.1), calls=%async_computation.2 | async-start | bytes 1179648 | tf_op jit(solution)/shard_map/all_to_all | solution.py:531
  190.4 5.4 %grads_down.1 = (bf16[2,256,1024]{2,1,0:T(8,128)(2,1)S(1)}, bf16[2,256,1024]{2,1,0:T(8,128)(2,1)S(1)}) custom-call(s32[6]{0:T(128)S(1)} %stack.27.ids, bf16[256,4096]{1,0:T(8,128)(2,1)S(1)} %copy-done.8, bf16[256,1024]{1,0:T(8,128)(2,1)} %collective-permute-done.7.refs_1_, bf16[256,1024]{1,0:T(8,128)(2,1)} %collective-permute-done.8.refs_2_, ...), custom_call_target="tpu_custom_call" | custom-call | flops 2147483648 | bytes 7864320 | tf_op jit(solution)/shard_map/grads_down/pallas_call | solution.py:236
  195.9 12.6 %collective-permute-done.10.refs_1_ = bf16[4,64,2560]{2,1,0:T(8,128)(2,1)} collective-permute-done((bf16[4,64,2560]{2,1,0:T(8,128)(2,1)}, bf16[4,64,2560]{2,1,0:T(8,128)(2,1)}, u32[]{:S(2)}, u32[]{:S(2)}) %collective-permute-start.10) | collective-permute-done | bytes 1310752 | tf_op jit(solution)/shard_map/ppermute | solution.py:535
  208.5 2.8 add_one.1
  215.5 2.0 collective-permute-start.13
  221.2 14.9 %attend_back.3 = (bf16[4096,128]{1,0:T(8,128)(2,1)S(1)}, f32[4,64,1024]{2,1,0:T(8,128)S(1)}, bf16[1024,128]{1,0:T(8,128)(2,1)S(1)}) custom-call(s32[4]{0:T(128)S(1)} %bitcast_subtract_fusion.starts, bf16[4096,128]{1,0:T(8,128)(2,1)S(1)} %copy-done.40, bf16[4096,128]{1,0:T(8,128)(2,1)S(1)} %copy-done.42, bf16[4096,128]{1,0:T(8,128)(2,1)S(1)} %copy-done.44, ...), custom_call_target="tpu_custom_call" | custom-call | flops 5368709120 | bytes 8192000 | tf_op jit(solution)/shard_map/attend_back/pallas_call | solution.py:218
  236.1 2.1 collective-permute-done.14.refs_5_
  241.5 14.1 %attend_back.4 = (f32[4,64,1024]{2,1,0:T(8,128)S(1)}, bf16[1024,128]{1,0:T(8,128)(2,1)S(1)}) custom-call(s32[4]{0:T(128)S(1)} %bitcast_subtract_fusion.starts, bf16[4096,128]{1,0:T(8,128)(2,1)S(1)} %copy-done.40, bf16[4096,128]{1,0:T(8,128)(2,1)S(1)} %copy-done.42, bf16[4096,128]{1,0:T(8,128)(2,1)S(1)} %copy-done.44, ...), custom_call_target="tpu_custom_call" | custom-call | flops 5368709120 | bytes 8192000 | tf_op jit(solution)/shard_map/attend_back/pallas_call | solution.py:218
  259.5 12.9 %attend_back.5.dx_ref = bf16[16,384,128]{2,1,0:T(8,128)(2,1)S(1)} custom-call(s32[4]{0:T(128)S(1)} %bitcast_subtract_fusion.starts, bf16[4096,128]{1,0:T(8,128)(2,1)S(1)} %copy-done.40, bf16[4096,128]{1,0:T(8,128)(2,1)S(1)} %copy-done.42, bf16[4096,128]{1,0:T(8,128)(2,1)S(1)} %copy-done.44, bf16[4096,128]{1,0:T(8,128)(2,1)S(1)} %get-tuple-element.182.refs_3_, ...), custom_call_target="tpu_custom_call" | custom-call | flops 10737418240 | bytes 8192000 | tf_op jit(solution)/shard_map/attend_back/pallas_call | solution.py:218
  272.5 5.8 %weight_message.1 = bf16[16,496,128]{2,1,0:T(8,128)(2,1)} custom-call(s32[6]{0:T(128)S(1)} %stack.27.ids, bf16[4096,1024]{1,0:T(8,128)(2,1)S(1)} %bitcast.48, bf16[16,384,128]{2,1,0:T(8,128)(2,1)S(1)} %attend_back.5.dx_ref), custom_call_target="tpu_custom_call" | custom-call | flops 1610612736 | bytes 11993088 | tf_op jit(solution)/shard_map/weight_message/pallas_call | solution.py:236
  278.2 2.6 collective-permute-done.18.refs_3_
  280.8 7.9 %all-to-all-start.3 = ((bf16[16,496,128]{2,1,0:T(8,128)(2,1)}), bf16[16,496,128]{2,1,0:T(8,128)(2,1)}, u32[]{:S(2)}, u32[]{:S(2)}) async-start(bf16[16,496,128]{2,1,0:T(8,128)(2,1)} %weight_message.1), calls=%async_computation.3 | async-start | bytes 4063232 | tf_op jit(solution)/shard_map/all_to_all | solution.py:531
  291.3 7.1 %fusion.7 = bf16[1,256,1024]{2,1,0:T(8,128)(2,1)} fusion(f32[256,1024]{1,0:T(8,128)S(1)} %get-tuple-element.110, bf16[256,4096]{1,0:T(8,128)(2,1)} %copy-done.7, bf16[4096,1024]{1,0:T(8,128)(2,1)} %param.27, f32[1024]{0:T(1024)S(1)} %copy-done.46), kind=kOutput, calls=%fused_computation.13 | convolution fusion | flops 2148270080 | bytes 12062720 | tf_op jit(solution)/shard_map/dot_general | solution.py:19
  302.5 5.9 %collective-permute-done.22 = bf16[256,512]{1,0:T(8,128)(2,1)S(1)} collective-permute-done((bf16[256,512]{1,0:T(8,128)(2,1)S(1)}, bf16[256,512]{1,0:T(8,128)(2,1)S(1)}, u32[]{:S(2)}, u32[]{:S(2)}) %collective-permute-start.22) | collective-permute-done | bytes 262176 | tf_op jit(solution)/shard_map/ppermute | solution.py:539
  309.5 4.8 %collective-permute-done.20 = bf16[128,1280]{1,0:T(8,128)(2,1)S(1)} collective-permute-done((bf16[128,1280]{1,0:T(8,128)(2,1)S(1)}, bf16[128,1280]{1,0:T(8,128)(2,1)S(1)}, u32[]{:S(2)}, u32[]{:S(2)}) %collective-permute-start.20) | collective-permute-done | bytes 327712 | tf_op jit(solution)/shard_map/ppermute | solution.py:539
  317.3 17.6 %all-to-all-done.3.got_ref = bf16[16,496,128]{2,1,0:T(8,128)(2,1)} async-done(((bf16[16,496,128]{2,1,0:T(8,128)(2,1)}), bf16[16,496,128]{2,1,0:T(8,128)(2,1)}, u32[]{:S(2)}, u32[]{:S(2)}) %all-to-all-start.3) | async-done | bytes 2031648 | tf_op jit(solution)/shard_map/all_to_all | solution.py:531
  336.5 2.2 pad_maximum_fusion
  338.7 2.8 copy-done
  342.7 6.6 %input_grad.1 = bf16[256,1024]{1,0:T(8,128)(2,1)} custom-call(s32[6]{0:T(128)S(1)} %stack.27.ids, bf16[16,496,128]{2,1,0:T(8,128)(2,1)} %all-to-all-done.3.got_ref, bf16[1024,3072]{1,0:T(8,128)(2,1)S(1)} %copy-done, bf16[1024,3072]{1,0:T(8,128)(2,1)S(1)} %copy-done, bf16[1024,3072]{1,0:T(8,128)(2,1)S(1)} %copy-done, bf16[256,1024]{1,0:T(8,128)(2,1)S(1)} %bitcast.51, ...), custom_call_target="tpu_custom_call" | custom-call | flops 1610612736 | bytes 22480896 | tf_op jit(solution)/shard_map/input_grad/pallas_call | solution.py:236
  (199 shorter events, 62.2 us)
Async XLA Ops:
  18.2 42.6 %all-to-all-start = ((bf16[16,384,128]{2,1,0:T(8,128)(2,1)}), bf16[16,384,128]{2,1,0:T(8,128)(2,1)S(1)}, u32[]{:S(2)}, u32[]{:S(2)}) async-start(bf16[16,384,128]{2,1,0:T(8,128)(2,1)} %copy-done.10), calls=%async_computation | async-start | bytes 3145728 | tf_op jit(solution)/shard_map/all_to_all | solution.py:531
  24.3 155.2 %all-gather.2.cloned.1.call-start = ((), (), s32[]{:S(2)}) async-start(), calls=%async_computation.4 | async-start | bytes 8912896 | tf_op jit(solution)/shard_map/all_gather | solution.py:610
  24.4 28.6 %collective-permute-start.1 = (bf16[256,1024]{1,0:T(8,128)(2,1)S(1)}, bf16[256,1024]{1,0:T(8,128)(2,1)S(1)}, u32[]{:S(2)}, u32[]{:S(2)}) collective-permute-start(bf16[256,1024]{1,0:T(8,128)(2,1)S(1)} %bitcast.52), channel_id=1, source_target_pairs={{0,2},{1,3},{2,0},{3,1},{4,6},{5,7},{6,4},{7,5},{8,10},{9,11},{10,... | collective-permute-start | bytes 1572872 | tf_op jit(solution)/shard_map/ppermute | solution.py:535
  25.9 27.1 %collective-permute-start = (bf16[256,1024]{1,0:T(8,128)(2,1)S(1)}, bf16[256,1024]{1,0:T(8,128)(2,1)S(1)}, u32[]{:S(2)}, u32[]{:S(2)}) collective-permute-start(bf16[256,1024]{1,0:T(8,128)(2,1)S(1)} %bitcast.53), channel_id=1, source_target_pairs={{0,1},{1,0},{2,3},{3,2},{4,5},{5,4},{6,7},{7,6},{8,9},{9,8},{10,11... | collective-permute-start | bytes 1572872 | tf_op jit(solution)/shard_map/ppermute | solution.py:535
  53.0 1.9 collective-permute-start.2
  61.0 60.7 %copy-start.1 = (bf16[1024,1024]{1,0:T(8,128)(2,1)S(1)}, bf16[1024,1024]{1,0:T(8,128)(2,1)}, u32[]{:S(2)}) copy-start(bf16[1024,1024]{1,0:T(8,128)(2,1)} %w_ref.4) | copy-start | bytes 6291460
  61.0 60.7 %copy-start.4 = (bf16[1,256,1024]{2,1,0:T(8,128)(2,1)S(1)}, bf16[1,256,1024]{2,1,0:T(8,128)(2,1)}, u32[]{:S(2)}) copy-start(bf16[1,256,1024]{2,1,0:T(8,128)(2,1)} %param.15) | copy-start | bytes 1572868
  61.0 60.7 %copy-start.26 = (f32[1024]{0:T(1024)S(1)}, f32[1024]{0:T(1024)}, u32[]{:S(2)}) copy-start(f32[1024]{0:T(1024)} %param.23) | copy-start | bytes 12292
  61.0 60.7 %copy-start.27 = (f32[1024]{0:T(1024)S(1)}, f32[1024]{0:T(1024)}, u32[]{:S(2)}) copy-start(f32[1024]{0:T(1024)} %param.22) | copy-start | bytes 12292
  61.0 60.7 %copy-start.28 = (f32[1024]{0:T(1024)S(1)}, f32[1024]{0:T(1024)}, u32[]{:S(2)}) copy-start(f32[1024]{0:T(1024)} %param.24) | copy-start | bytes 12292
  138.7 12.9 %collective-permute-start.5 = (bf16[256,4096]{1,0:T(8,128)(2,1)}, bf16[256,4096]{1,0:T(8,128)(2,1)}, u32[]{:S(2)}, u32[]{:S(2)}) collective-permute-start(bf16[256,4096]{1,0:T(8,128)(2,1)} %get-tuple-element.216.ua_ref.ub_ref), channel_id=1, source_target_pairs={{0,1},{1,0},{2,3},{3,2},{4,5},{5,4},{6,7},{7,6},{8,9},{9,8},{10,11... | collective-permute-start | bytes 6291464 | tf_op jit(solution)/shard_map/ppermute | solution.py:535
  147.4 1.9 collective-permute-start.6
  147.8 3.0 collective-permute-start.3
  148.0 3.6 %collective-permute-start.4 = (bf16[256,1024]{1,0:T(8,128)(2,1)S(1)}, bf16[256,1024]{1,0:T(8,128)(2,1)S(1)}, u32[]{:S(2)}, u32[]{:S(2)}) collective-permute-start(bf16[256,1024]{1,0:T(8,128)(2,1)S(1)} %copy-done.20), channel_id=1, source_target_pairs={{0,1},{1,0},{2,3},{3,2},{4,5},{5,4},{6,7},{7,6},{8,9},{9,8},{10,11... | collective-permute-start | bytes 1572872 | tf_op jit(solution)/shard_map/ppermute | solution.py:535
  148.3 17.8 %collective-permute-start.7 = (bf16[256,1024]{1,0:T(8,128)(2,1)}, bf16[256,1024]{1,0:T(8,128)(2,1)}, u32[]{:S(2)}, u32[]{:S(2)}) collective-permute-start(bf16[256,1024]{1,0:T(8,128)(2,1)} %get-tuple-element.120), channel_id=1, source_target_pairs={{0,1},{1,0},{2,3},{3,2},{4,5},{5,4},{6,7},{7,6},{8,9},{9,8},{10,11... | collective-permute-start | bytes 1572872 | tf_op jit(solution)/shard_map/ppermute | solution.py:535
  149.4 16.7 %collective-permute-start.8 = (bf16[256,1024]{1,0:T(8,128)(2,1)}, bf16[256,1024]{1,0:T(8,128)(2,1)}, u32[]{:S(2)}, u32[]{:S(2)}) collective-permute-start(bf16[256,1024]{1,0:T(8,128)(2,1)} %get-tuple-element.121), channel_id=1, source_target_pairs={{0,2},{1,3},{2,0},{3,1},{4,6},{5,7},{6,4},{7,5},{8,10},{9,11},{10,... | collective-permute-start | bytes 1572872 | tf_op jit(solution)/shard_map/ppermute | solution.py:535
  150.8 23.7 %collective-permute-start.9 = (bf16[256,1024]{1,0:T(8,128)(2,1)}, bf16[256,1024]{1,0:T(8,128)(2,1)}, u32[]{:S(2)}, u32[]{:S(2)}) collective-permute-start(bf16[256,1024]{1,0:T(8,128)(2,1)} %get-tuple-element.122), channel_id=1, source_target_pairs={{0,3},{1,2},{2,1},{3,0},{4,7},{5,6},{6,5},{7,4},{8,11},{9,10},{10,... | collective-permute-start | bytes 1572872 | tf_op jit(solution)/shard_map/ppermute | solution.py:535
  163.0 32.9 %collective-permute-start.11 = (bf16[512,1280]{1,0:T(8,128)(2,1)}, bf16[512,1280]{1,0:T(8,128)(2,1)}, u32[]{:S(2)}, u32[]{:S(2)}) collective-permute-start(bf16[512,1280]{1,0:T(8,128)(2,1)} %get-tuple-element.129), channel_id=1, source_target_pairs={{0,16},{16,0},{1,17},{17,1},{2,18},{18,2},{3,19},{19,3},{4,20},{20... | collective-permute-start | bytes 3932168 | tf_op jit(solution)/shard_map/ppermute | solution.py:539
  164.6 43.9 %collective-permute-start.10 = (bf16[4,64,2560]{2,1,0:T(8,128)(2,1)}, bf16[4,64,2560]{2,1,0:T(8,128)(2,1)}, u32[]{:S(2)}, u32[]{:S(2)}) collective-permute-start(bf16[4,64,2560]{2,1,0:T(8,128)(2,1)} %get-tuple-element.127), channel_id=1, source_target_pairs={{0,2},{1,3},{2,0},{3,1},{4,6},{5,7},{6,4},{7,5},{8,10},{9,11},{10,... | collective-permute-start | bytes 3932168 | tf_op jit(solution)/shard_map/ppermute | solution.py:535
  179.6 34.3 %all-to-all-start.2 = ((bf16[16,144,128]{2,1,0:T(8,128)(2,1)}), bf16[16,144,128]{2,1,0:T(8,128)(2,1)}, u32[]{:S(2)}, u32[]{:S(2)}) async-start(bf16[16,144,128]{2,1,0:T(8,128)(2,1)} %grad_pack.1), calls=%async_computation.2 | async-start | bytes 1179648 | tf_op jit(solution)/shard_map/all_to_all | solution.py:531
  213.9 24.3 %collective-permute-start.14 = (bf16[2,256,1024]{2,1,0:T(8,128)(2,1)}, bf16[2,256,1024]{2,1,0:T(8,128)(2,1)S(1)}, u32[]{:S(2)}, u32[]{:S(2)}) collective-permute-start(bf16[2,256,1024]{2,1,0:T(8,128)(2,1)} %copy-done.29), channel_id=1, source_target_pairs={{0,4},{1,5},{2,6},{3,7},{4,0},{5,1},{6,2},{7,3},{8,12},{9,13},{10,... | collective-permute-start | bytes 3145736 | tf_op jit(solution)/shard_map/ppermute | solution.py:535
  213.9 22.2 %collective-permute-start.12 = (bf16[4,64,1280]{2,1,0:T(8,128)(2,1)}, bf16[4,64,1280]{2,1,0:T(8,128)(2,1)S(1)}, u32[]{:S(2)}, u32[]{:S(2)}) collective-permute-start(bf16[4,64,1280]{2,1,0:T(8,128)(2,1)} %copy-done.31), channel_id=1, source_target_pairs={{0,16},{16,0},{1,17},{17,1},{2,18},{18,2},{3,19},{19,3},{4,20},{20... | collective-permute-start | bytes 1966088 | tf_op jit(solution)/shard_map/ppermute | solution.py:539
  215.5 20.6 %collective-permute-start.13 = (bf16[4,64,1280]{2,1,0:T(8,128)(2,1)}, bf16[4,64,1280]{2,1,0:T(8,128)(2,1)S(1)}, u32[]{:S(2)}, u32[]{:S(2)}) collective-permute-start(bf16[4,64,1280]{2,1,0:T(8,128)(2,1)} %copy-done.30), channel_id=1, source_target_pairs={{0,2},{1,3},{2,0},{3,1},{4,6},{5,7},{6,4},{7,5},{8,10},{9,11},{10,... | collective-permute-start | bytes 1966088 | tf_op jit(solution)/shard_map/ppermute | solution.py:535
  239.3 16.4 %collective-permute-start.15 = (bf16[2,128,1280]{2,1,0:T(8,128)(2,1)S(1)}, bf16[2,128,1280]{2,1,0:T(8,128)(2,1)S(1)}, u32[]{:S(2)}, u32[]{:S(2)}) collective-permute-start(bf16[2,128,1280]{2,1,0:T(8,128)(2,1)S(1)} %get-tuple-element.163), channel_id=1, source_target_pairs={{0,4},{1,5},{2,6},{3,7},{4,0},{5,1},{6,2},{7,3},{8,12},{9,13},{10,... | collective-permute-start | bytes 1966088 | tf_op jit(solution)/shard_map/ppermute | solution.py:535
  239.7 15.9 %collective-permute-start.16 = (bf16[2,256,512]{2,1,0:T(8,128)(2,1)S(1)}, bf16[2,256,512]{2,1,0:T(8,128)(2,1)S(1)}, u32[]{:S(2)}, u32[]{:S(2)}) collective-permute-start(bf16[2,256,512]{2,1,0:T(8,128)(2,1)S(1)} %get-tuple-element.164), channel_id=1, source_target_pairs={{0,16},{16,0},{1,17},{17,1},{2,18},{18,2},{3,19},{19,3},{4,20},{20... | collective-permute-start | bytes 1572872 | tf_op jit(solution)/shard_map/ppermute | solution.py:539
  256.5 24.3 %collective-permute-start.17 = (bf16[1,128,1280]{2,1,0:T(8,128)(2,1)S(1)}, bf16[1,128,1280]{2,1,0:T(8,128)(2,1)S(1)}, u32[]{:S(2)}, u32[]{:S(2)}) collective-permute-start(bf16[1,128,1280]{2,1,0:T(8,128)(2,1)S(1)} %get-tuple-element.179), channel_id=1, source_target_pairs={{0,8},{1,9},{2,10},{3,11},{4,12},{5,13},{6,14},{7,15},{8,0},{9,1},... | collective-permute-start | bytes 983048 | tf_op jit(solution)/shard_map/ppermute | solution.py:535
  257.6 23.2 %collective-permute-start.18 = (bf16[1,256,512]{2,1,0:T(8,128)(2,1)S(1)}, bf16[1,256,512]{2,1,0:T(8,128)(2,1)S(1)}, u32[]{:S(2)}, u32[]{:S(2)}) collective-permute-start(bf16[1,256,512]{2,1,0:T(8,128)(2,1)S(1)} %get-tuple-element.180), channel_id=1, source_target_pairs={{0,8},{1,9},{2,10},{3,11},{4,12},{5,13},{6,14},{7,15},{8,0},{9,1},... | collective-permute-start | bytes 786440 | tf_op jit(solution)/shard_map/ppermute | solution.py:535
  280.8 54.1 %all-to-all-start.3 = ((bf16[16,496,128]{2,1,0:T(8,128)(2,1)}), bf16[16,496,128]{2,1,0:T(8,128)(2,1)}, u32[]{:S(2)}, u32[]{:S(2)}) async-start(bf16[16,496,128]{2,1,0:T(8,128)(2,1)} %weight_message.1), calls=%async_computation.3 | async-start | bytes 4063232 | tf_op jit(solution)/shard_map/all_to_all | solution.py:531
  290.8 10.0 %collective-permute-start.21 = (bf16[512]{0:T(512)(128)(2,1)S(1)}, bf16[512]{0:T(512)(128)(2,1)S(1)}, u32[]{:S(2)}, u32[]{:S(2)}) collective-permute-start(bf16[512]{0:T(512)(128)(2,1)S(1)} %bitcast.72), channel_id=1, source_target_pairs={{0,16},{16,0},{1,17},{17,1},{2,18},{18,2},{3,19},{19,3},{4,20},{20... | collective-permute-start | bytes 3080 | tf_op jit(solution)/shard_map/ppermute | solution.py:526
  299.1 9.3 %collective-permute-start.22 = (bf16[256,512]{1,0:T(8,128)(2,1)S(1)}, bf16[256,512]{1,0:T(8,128)(2,1)S(1)}, u32[]{:S(2)}, u32[]{:S(2)}) collective-permute-start(bf16[256,512]{1,0:T(8,128)(2,1)S(1)} %bitcast.58), channel_id=1, source_target_pairs={{0,16},{16,0},{1,17},{17,1},{2,18},{18,2},{3,19},{19,3},{4,20},{20... | collective-permute-start | bytes 786440 | tf_op jit(solution)/shard_map/ppermute | solution.py:539
  302.0 12.3 %collective-permute-start.20 = (bf16[128,1280]{1,0:T(8,128)(2,1)S(1)}, bf16[128,1280]{1,0:T(8,128)(2,1)S(1)}, u32[]{:S(2)}, u32[]{:S(2)}) collective-permute-start(bf16[128,1280]{1,0:T(8,128)(2,1)S(1)} %bitcast.57), channel_id=1, source_target_pairs={{0,16},{16,0},{1,17},{17,1},{2,18},{18,2},{3,19},{19,3},{4,20},{20... | collective-permute-start | bytes 983048 | tf_op jit(solution)/shard_map/ppermute | solution.py:539
  336.0 13.3 %collective-permute-start.19 = (bf16[16,112,128]{2,1,0:T(8,128)(2,1)S(1)}, bf16[16,112,128]{2,1,0:T(8,128)(2,1)S(1)}, u32[]{:S(2)}, u32[]{:S(2)}) collective-permute-start(bf16[16,112,128]{2,1,0:T(8,128)(2,1)S(1)} %slice.44.one_ref), channel_id=1, source_target_pairs={{0,16},{16,0},{1,17},{17,1},{2,18},{18,2},{3,19},{19,3},{4,20},{20... | collective-permute-start | bytes 1376264 | tf_op jit(solution)/shard_map/ppermute | solution.py:539
  (49 other events, 535.2 us)
Sparse Core Ops, SparseCore 0:
  60.9 82.3 all-gather.1

commit v4 on v3

--- a/solution.py
+++ b/solution.py
@@ -10,7 +10,7 @@
 
 EPSILON = 1e-05
 HEADS=16; HEAD_DIM=64; NEGATIVE=-1e30
-FWD_TILE=(512,1024); BWD_TILE=(1024,1024)
+FWD_TILE=(1024,1024); BWD_TILE=(1024,1024)
 LOG2E=math.log2(math.e); LN2=math.log(2.0)
 BF=jnp.bfloat16; F32=jnp.float32
 NT=(((1,),(1,)),((),())); TN=(((0,),(0,)),((),())); NN=(((1,),(0,)),((),()))
@@ -51,7 +51,7 @@
 def pair_down(one, two):
     return jnp.where(lanes_low(one.shape),pltpu.roll(one,HEAD_DIM,1),two)
 
-def fwd_kernel(starts, part, x_ref, low_ref, out_ref, qa_ref, ka_ref, va_ref, s_ref, q_ref, *, bq, bk, segs, group, tokens):
+def fwd_kernel(starts, part, x_ref, low_ref, qa_ref, s_ref, q_ref, ka_ref, va_ref, *, bq, bk, segs, group, tokens):
     i=pl.program_id(0); full=q_ref.shape[0]; half=tokens//2
     @pl.when(i==0)
     def _():
@@ -67,7 +67,7 @@
             return 0
         lax.fori_loop(0,full//tokens,build,0)
     def skip():
-        low_ref[...]=jnp.zeros_like(low_ref); out_ref[...]=jnp.zeros_like(out_ref)
+        low_ref[...]=jnp.zeros_like(low_ref)
         qa_ref[...]=with_tail(jnp.zeros((bq,128),F32),jnp.full((bq,1),1e30,F32))
     def work():
         a=i*bq; last=a+bq-1
@@ -98,8 +98,7 @@
             return acc+dotf(p,va_ref[pl.ds(pl.multiple_of(j*bk,bk),bk),:],NN)
         acc=lax.fori_loop(lo,hi,gather,jnp.zeros((bq,128),F32))
         total=-acc[:,HEAD_DIM:HEAD_DIM+1]
-        out=jnp.where(lanes_low((bq,128)),acc/total,0.0)
-        out_ref[...]=out
+        out=acc/total
         for c in range(bq//tokens):
             mid=c*tokens+half
             low_ref[c]=pair_up(out[c*tokens:mid],out[mid:mid+half]).astype(BF)
@@ -112,43 +111,38 @@
 def attend(starts, part, x, *, bq, bk, group):
     ranks,rows,_=x.shape; tokens=rows//3*2; full=ranks*tokens; segs=starts.shape[0]
     if group>1: bq=tokens
-    whole=lambda w: pl.BlockSpec((full,w),lambda i,*_:(0,0))
-    blk=lambda w: pl.BlockSpec((bq,w),lambda i,*_:(i,0))
     return pl.pallas_call(
         functools.partial(fwd_kernel,bq=bq,bk=bk,segs=segs,group=group,tokens=tokens),
         grid_spec=pltpu.PrefetchScalarGridSpec(num_scalar_prefetch=2,grid=(full//bq,),
             in_specs=[pl.BlockSpec(x.shape,lambda i,*_:(0,0,0))],
-            out_specs=[pl.BlockSpec((bq//tokens,tokens//2,128),lambda i,*_:(i,0,0)),blk(128),blk(128),whole(128),whole(128)],
-            scratch_shapes=[pltpu.VMEM((full//bk,bq,bk),F32),pltpu.VMEM((full,128),BF)]),
-        out_shape=[jax.ShapeDtypeStruct((ranks,tokens//2,128),BF),jax.ShapeDtypeStruct((full,128),F32)]+[jax.ShapeDtypeStruct((full,128),BF)]*3,
-        compiler_params=pltpu.CompilerParams(vmem_limit_bytes=full//1024*(22<<18)),
+            out_specs=[pl.BlockSpec((bq//tokens,tokens//2,128),lambda i,*_:(i,0,0)),pl.BlockSpec((bq,128),lambda i,*_:(i,0))],
+            scratch_shapes=[pltpu.VMEM((full//bk,bq,bk),F32)]+[pltpu.VMEM((full,128),BF)]*3),
+        out_shape=[jax.ShapeDtypeStruct((ranks,tokens//2,128),BF),jax.ShapeDtypeStruct((full,128),BF)],
+        compiler_params=pltpu.CompilerParams(vmem_limit_bytes=min(60<<20,full//1024*(40<<18))),
         cost_estimate=pl.CostEstimate(flops=full*full*512,bytes_accessed=full*1600,transcendentals=full*full//2),
         name="attend")(starts,part,x)
 
 def bwd_kernel(starts, *refs, bq, bk, segs, begin, count, first, last, tokens):
     half=tokens//2
     refs=list(refs)
-    qa_ref,ka_ref,va_ref=refs[:3]; refs=refs[3:]
+    x_ref,qa_ref=refs[:2]; refs=refs[2:]
     full=qa_ref.shape[0]; nq=full//bq
-    if first:
-        do_ref,out_ref=refs[:2]; refs=refs[2:]
-    else:
-        da_ref,dq_in,early_ref=refs[:3]; refs=refs[3:]
-    if last:
-        dx_ref,dq_ref,kt_ref,kv_ref=refs[:4]; refs=refs[4:]
-        if first: da_ref=refs[0]
-    else:
-        if first: da_ref,refs=refs[0],refs[1:]
-        dq_ref,kv_ref,kt_ref=refs[:3]
+    if first: do_ref,low_ref=refs[:2]; refs=refs[2:]
+    else: da_ref,dq_in,early_ref=refs[:3]; refs=refs[3:]
+    if last: dx_ref,refs=refs[0],refs[1:]
+    elif first: da_ref,refs=refs[0],refs[1:]
+    dq_ref,kv_ref=refs[:2]
+    if first and last: da_ref=refs[2]
     j=pl.program_id(0)
+    low=lanes_low((tokens,128))
+    unfold=lambda v: jnp.concatenate([v,pltpu.roll(v,HEAD_DIM,1)],axis=0)
     @pl.when(j==0)
     def _():
         if first:
             def build(t,_):
                 rows=pl.ds(pl.multiple_of(t*tokens,tokens),tokens)
-                g=do_ref[t,:half,:].astype(F32)
-                g=jnp.concatenate([g,pltpu.roll(g,HEAD_DIM,1)],axis=0)
-                delta=jnp.sum(g*out_ref[rows,:],axis=1,keepdims=True)
+                g=unfold(do_ref[t,:half,:].astype(F32))
+                delta=jnp.sum(jnp.where(low,g*unfold(low_ref[t].astype(F32)),0.0),axis=1,keepdims=True)
                 da_ref[rows,:]=with_tail(g,delta)
                 return 0
             lax.fori_loop(0,full//tokens,build,0)
@@ -156,16 +150,15 @@
             dq_ref[t]=jnp.zeros(dq_ref.shape[1:],F32) if first else dq_in[t]
             return 0
         lax.fori_loop(0,nq,clear,0)
-        def trans(t,_):
-            kt_ref[t]=ka_ref[pl.ds(pl.multiple_of((begin+t)*bk,bk),bk),:].astype(F32).T[:HEAD_DIM].astype(BF)
-            return 0
-        lax.fori_loop(0,count,trans,0)
     c=(begin+j)*bk; d=c+bk
     e0=seg_end(starts,c,segs,full); e1=seg_end(starts,d-1,segs,full)
     lo=c//bq; hi=(e1+bq-1)//bq
     u0=jnp.minimum((d-1+bq-1)//bq,hi); u1=jnp.maximum(u0,e0//bq)
-    rows=pl.ds(pl.multiple_of(c,bk),bk)
-    ka=ka_ref[rows,:]; va=va_ref[rows,:]; kt=kt_ref[j]
+    mark=jnp.where(lax.broadcasted_iota(jnp.int32,(tokens,128),1)<HEAD_DIM+3,-1.0,0.0)
+    keys=[jnp.where(low,pltpu.roll(x_ref[t,:tokens,:].astype(F32),HEAD_DIM,1),mark) for t in range(bk//tokens)]
+    keys=jnp.concatenate(keys,axis=0)
+    values=[jnp.where(low,unfold(x_ref[t,tokens:,:].astype(F32)),mark) for t in range(bk//tokens)]
+    ka=keys.astype(BF); va=jnp.concatenate(values,axis=0).astype(BF); kt=keys.T[:HEAD_DIM].astype(BF)
     def step(i,carry,masked):
         dk,dv=carry
         qrows=pl.ds(pl.multiple_of(i*bq,bq),bq)
@@ -187,8 +180,7 @@
     carry=lax.fori_loop(lo,u0,lambda i,t:step(i,t,True),(z,z))
     carry=lax.fori_loop(u0,u1,lambda i,t:step(i,t,False),carry)
     dk,dv=lax.fori_loop(u1,hi,lambda i,t:step(i,t,True),carry)
-    mine=pair_up(dv,dk*LN2).astype(BF)
-    kv_ref[pl.ds(pl.multiple_of(j*bk,bk),bk),:]=mine
+    kv_ref[pl.ds(pl.multiple_of(j*bk,bk),bk),:]=pair_up(dv,dk*LN2).astype(BF)
     if last:
         @pl.when(j==count-1)
         def _():
@@ -199,37 +191,37 @@
                     r=t*bq+c*tokens
                     kv=early_ref[r:r+tokens,:] if r<begin*bk else kv_ref[r-begin*bk:r-begin*bk+tokens,:]
                     kv=kv.astype(F32)
-                    dx_ref[r//tokens,:tokens,:]=jnp.where(lanes_low(kv.shape),dq[c*tokens:(c+1)*tokens],kv).astype(BF)
+                    dx_ref[r//tokens,:tokens,:]=jnp.where(low,dq[c*tokens:(c+1)*tokens],kv).astype(BF)
                     dx_ref[r//tokens,tokens:,:]=pair_up(kv[:half],kv[half:]).astype(BF)
 
-def attend_back(starts, qa, ka, va, rest, *, bq, bk, begin, count, tokens, first, last):
+def attend_back(starts, x, qa, rest, *, bq, bk, begin, count, tokens, first, last):
     full=qa.shape[0]; segs=starts.shape[0]
     fixed=lambda shape: pl.BlockSpec(shape,lambda i,*_:(0,)*len(shape))
-    dq_shape=(full//bq,64,bq); kt=pltpu.VMEM((count,64,bk),BF)
+    dq_shape=(full//bq,64,bq)
     if last:
-        outs=[jax.ShapeDtypeStruct((full//tokens,tokens//2*3,128),BF)]
-        scratch=[pltpu.VMEM(dq_shape,F32),kt,pltpu.VMEM((count*bk,128),BF)]
-        if first: scratch.append(pltpu.VMEM((full,128),BF))
+        outs=[jax.ShapeDtypeStruct(x.shape,BF)]
+        scratch=[pltpu.VMEM(dq_shape,F32),pltpu.VMEM((count*bk,128),BF)]
+        if first: scratch+=[pltpu.VMEM((full,128),BF)]
     else:
         outs=[jax.ShapeDtypeStruct(dq_shape,F32),jax.ShapeDtypeStruct((count*bk,128),BF)]
-        if first: outs.insert(0,jax.ShapeDtypeStruct((full,128),BF))
-        scratch=[kt]
+        if first: outs=[jax.ShapeDtypeStruct((full,128),BF)]+outs
+        scratch=[]
     area=full*full*(count/(full//bk))
     return pl.pallas_call(
         functools.partial(bwd_kernel,bq=bq,bk=bk,segs=segs,begin=begin,count=count,first=first,last=last,tokens=tokens),
         grid_spec=pltpu.PrefetchScalarGridSpec(num_scalar_prefetch=1,grid=(count,),
-            in_specs=[fixed(v.shape) for v in (qa,ka,va)+tuple(rest)],
+            in_specs=[pl.BlockSpec((bk//tokens,)+x.shape[1:],lambda j,*_:(begin+j,0,0))]+[fixed(v.shape) for v in (qa,)+tuple(rest)],
             out_specs=[fixed(o.shape) for o in outs],
             scratch_shapes=scratch),
         out_shape=outs,
-        compiler_params=pltpu.CompilerParams(vmem_limit_bytes=full//1024*((48 if first else 24)<<18)),
+        compiler_params=pltpu.CompilerParams(vmem_limit_bytes=min(60<<20,full//1024*((48 if first else 24)<<18))),
         cost_estimate=pl.CostEstimate(flops=int(area*1280),bytes_accessed=full*2000,transcendentals=int(area/2)),
-        name="attend_back")(starts,qa,ka,va,*rest)
+        name="attend_back")(starts,x,qa,*rest)
 
 def fixed_block(shape):
     return pl.BlockSpec(shape,lambda s,*_:(0,)*len(shape))
 
-ROOM={"project": 48}
+ROOM={"project": 60}
 
 def run_kernel(kernel, ids, grid, ins, in_specs, outs, out_specs, scratch, name, flops):
     moved=sum(math.prod(v.shape)*2 for v in ins)+sum(math.prod(o.shape)*2 for o in outs)
@@ -610,7 +602,7 @@
     gather = lambda v: lax.all_gather(v, "seq", axis=0, tiled=True)
     normed_low, packed = lax.optimization_barrier((normed_low, packed))
     normed_all = gather(normed_low)
-    low, out, qa, ka, va = attend(starts, part, packed, bq=FWD_TILE[0], bk=FWD_TILE[1], group=group)
+    low, qa = attend(starts, part, packed, bq=FWD_TILE[0], bk=FWD_TILE[1], group=group)
     normed_two_low, attended_low, residual = mix(ids, fold(exchange(low)), w_out, frames[0], bias_out, ln2_gain, ln2_bias)
     unit_two, scale_two = statistics(residual)
     up_proj = dotf(normed_two_low, w_up, NN) + bias_up
@@ -623,8 +615,13 @@
         picked, cot_low = lax.optimization_barrier((pick_blocks(ids, hidden, ranks), cot_low))
     up_grad = (dotf(cot_low, w_down, NT) * slope).astype(BF)
     normed_two_grad = dotf(up_grad, w_up, NT)
-    residual_grad = cot + norm_back(unit_two, scale_two, ln2_gain, normed_two_grad)
+    gain_two = ln2_gain
+    if fast:
+        others = [swap(v, k + 1) for k, v in enumerate(picked)]
+    residual_grad = cot + norm_back(unit_two, scale_two, gain_two, normed_two_grad)
     branch_grad = residual_grad.astype(BF)
+    if fast:
+        others[1], branch_grad = lax.optimization_barrier((others[1], branch_grad))
     if fast:
         a_sent, a_keep, b_sent, b_keep = grads_up(
             ids,
@@ -639,7 +636,6 @@
             ranks,
         )
         branch_grad, a_sent, b_sent = lax.optimization_barrier((branch_grad, a_sent, b_sent))
-        others = [swap(v, k + 1) for k, v in enumerate(picked)]
         branch_grad, others = lax.optimization_barrier((branch_grad, others))
         a_got, b_got = swap(a_sent, 2), swap_row(b_sent)
 
@@ -668,19 +664,19 @@
     got = exchange(sent)
     small_total = row_sum(jnp.sum(got[:, tokens // 2 : tokens // 2 + lines].astype(F32), axis=0).reshape(-1))
 
-    back = functools.partial(attend_back, starts, qa, ka, va, bq=BWD_TILE[0], bk=BWD_TILE[1], tokens=tokens)
+    back = functools.partial(attend_back, starts, packed, qa, bq=BWD_TILE[0], bk=BWD_TILE[1], tokens=tokens)
     tiles = full // BWD_TILE[1]
     if fast:
         blocks = lambda v: v.reshape(ranks // 2, share, -1)
         a_sent, a_keep, b_sent, b_keep = add_split(
             ids, (("columns", 2, "a"), ("blocks", 1, "b")), [a_keep, a_got, blocks(b_keep), blocks(b_got)], "add_one"
         )
-        got, a_sent, b_sent = lax.optimization_barrier((got, a_sent, b_sent))
+        got, _, _ = lax.optimization_barrier((got, a_sent, b_sent))
         a_got, b_got = swap_row(a_sent), swap(b_sent, 2)
         down_sent, down_keep = grads_down(ids, hidden, others, cots, ranks)
-        got, down_sent = lax.optimization_barrier((got, down_sent))
+        got, _ = lax.optimization_barrier((got, down_sent))
         down_got = swap(down_sent, 4)
-        one = back((got, out), begin=tiles // 4, count=tiles // 4, first=True, last=False)
+        one = back((got, low), begin=tiles // 4, count=tiles // 4, first=True, last=False)
         a_got, b_got, down_got, one = lax.optimization_barrier((a_got, b_got, down_got, one))
         up_sent, up_keep, down_sent, down_keep = add_split(
             ids,
@@ -739,7 +735,7 @@
         total_down = reduced(dotf(halves(hidden), both(cot_low), TN))
         total_up = reduced(dotf(halves(normed_two_low), both(up_grad), TN))
         total_out = reduced(dotf(halves(attended_low), both(branch_grad), TN))
-        (dx,) = back((got, out), begin=0, count=tiles, first=True, last=True)
+        (dx,) = back((got, low), begin=0, count=tiles, first=True, last=True)
         everything = weight_message(ids, normed_all, dx)
     returned = fold(exchange(everything))
     grad_frames = input_grad(ids, returned, w_qkv, frames[0], ln1_gain, residual_grad)

time: 366 us -> 358 us (0.978)
  waiting for transfers between devices: 90.1 us -> 81 us
  Pallas kernels: 118 us -> 122 us
    ppermute x16, waiting for transfers between devices: 56.7 us -> 48.7 us  [swap(): lax.ppermute(value, 'seq', [(i, i ^ bit) for i in range(lax.axis_size('se...]
    pallas_call x13, Pallas kernels: 48.3 us -> 54.2 us  [run_kernel(): pl.pallas_call(kernel, grid_spec=pltpu.PrefetchScalarGridSpec(num_scalar_...]
    unnamed x108 -> x90, local copies, waits for them, and re-layouts: 26.1 us -> 22.9 us
  transfers between devices with their start and end apart: 27 -> 27, of which waited for: 13 -> 10; matrix products, arithmetic and copies ran while one was open for 10% -> 11% of each run, Pallas kernels for 30% -> 31%
where the time goes in v4:
time: 358 us; the launch traced here: 352 us
  Pallas kernels  122 us (34%)
  waiting for transfers between devices  81 us (23%)
  starting transfers between devices  37.9 us (11%)
  blocking collectives  32.8 us (9%)
  local copies, waits for them, and re-layouts  29.7 us (8%)
  matrix products  24.8 us (7%)
  between operations  14.8 us (4%)
  other arithmetic  9.03 us (3%)
    pallas_call x13, Pallas kernels, run_kernel(): pl.pallas_call(kernel, grid_spec=pltpu.PrefetchScalarGridSpec(num_scalar_...  54.2 us
    ppermute x16, waiting for transfers between devices, swap(): lax.ppermute(value, 'seq', [(i, i ^ bit) for i in range(lax.axis_size('se...  48.7 us
    pallas_call x3, Pallas kernels, attend_back(): pl.pallas_call(functools.partial(bwd_kernel, bq=bq, bk=bk, segs=segs, beg...  42.4 us
    all_to_all x1, blocking collectives, exchange(): return lax.all_to_all(value, 'seq', 0, 0, tiled=True)  32.8 us
    pallas_call x1, Pallas kernels, attend(): pl.pallas_call(functools.partial(fwd_kernel, bq=bq, bk=bk, segs=segs, gro...  25.1 us
    dot_general x4, matrix products, dotf(): return lax.dot_general(a, b, dims, preferred_element_type=F32)  24.8 us
    unnamed x90, local copies, waits for them, and re-layouts  22.9 us
    all_to_all x3, waiting for transfers between devices, exchange(): return lax.all_to_all(value, 'seq', 0, 0, tiled=True)  21.6 us
  transfers between devices with their start and end apart: 27, of which 10 were waited for; matrix products, arithmetic and copies ran while one was open for 11% of the time, Pallas kernels for 31%

profile of v4, /device:TPU:16, one launch (start us, length us, event | category | flops | bytes accessed | tf_op | source)
XLA Modules:
  0.0 351.8 jit_solution(10058166578304603096)
XLA Ops:
  7.9 7.5 %project.1 = (bf16[16,384,128]{2,1,0:T(8,128)(2,1)}, bf16[256,1024]{1,0:T(8,128)(2,1)}) custom-call(s32[6]{0:T(128)} %stack.27.ids, bf16[256,1024]{1,0:T(8,128)(2,1)} %bitcast.49, f32[1,1024]{1,0:T(1,128)} %bitcast.59, f32[1,1024]{1,0:T(1,128)} %bitcast.68, bf16[1024,3072]{1,0:T(8,128)(2,1)} %w_ref.5, bf16[1024,3072]{1,0:T(8,128)(2,1)} %w_ref.5, ...), custom_call_target="tpu_custom_call" | custom-call | flops 1610612736 | bytes 21508096 | tf_op jit(solution)/shard_map/project/pallas_call | solution.py:228
  15.3 6.2 %all-to-all-start = ((bf16[16,384,128]{2,1,0:T(8,128)(2,1)}), bf16[16,384,128]{2,1,0:T(8,128)(2,1)S(1)}, u32[]{:S(2)}, u32[]{:S(2)}) async-start(bf16[16,384,128]{2,1,0:T(8,128)(2,1)} %get-tuple-element.102), calls=%async_computation | async-start | bytes 3145728 | tf_op jit(solution)/shard_map/all_to_all | solution.py:523
  23.1 27.1 %collective-permute-done.1.refs_6_ = bf16[256,1024]{1,0:T(8,128)(2,1)S(1)} collective-permute-done((bf16[256,1024]{1,0:T(8,128)(2,1)S(1)}, bf16[256,1024]{1,0:T(8,128)(2,1)S(1)}, u32[]{:S(2)}, u32[]{:S(2)}) %collective-permute-start.1) | collective-permute-done | bytes 524320 | tf_op jit(solution)/shard_map/ppermute | solution.py:527
  52.8 5.1 %all-to-all-done.x_ref.refs_0_ = bf16[16,384,128]{2,1,0:T(8,128)(2,1)S(1)} async-done(((bf16[16,384,128]{2,1,0:T(8,128)(2,1)}), bf16[16,384,128]{2,1,0:T(8,128)(2,1)S(1)}, u32[]{:S(2)}, u32[]{:S(2)}) %all-to-all-start) | async-done | bytes 1572896 | tf_op jit(solution)/shard_map/all_to_all | solution.py:523
  58.2 25.1 %attend.1 = (bf16[16,128,128]{2,1,0:T(8,128)(2,1)S(1)}, bf16[4096,128]{1,0:T(8,128)(2,1)S(1)}) custom-call(s32[4]{0:T(128)S(1)} %bitcast_subtract_fusion.starts, s32[1]{0:T(128)} %constant.96.clone.1.part, bf16[16,384,128]{2,1,0:T(8,128)(2,1)S(1)} %all-to-all-done.x_ref.refs_0_), custom_call_target="tpu_custom_call" | custom-call | flops 8589934592 | bytes 6553600 | tf_op jit(solution)/shard_map/attend/pallas_call | solution.py:114
  84.2 32.8 %all_to_all.20.got_ref = bf16[16,128,128]{2,1,0:T(8,128)(2,1)S(1)} all-to-all(bf16[16,128,128]{2,1,0:T(8,128)(2,1)S(1)} %get-tuple-element.105.refs_3_), channel_id=1, replica_groups=mesh['row'=2,'seq'=16] {'seq'}, dimensions={0} | all-to-all | bytes 1048576 | tf_op jit(solution)/shard_map/all_to_all | solution.py:523
  117.1 3.6 %mix.1 = (bf16[256,1024]{1,0:T(8,128)(2,1)}, bf16[256,1024]{1,0:T(8,128)(2,1)}, f32[256,1024]{1,0:T(8,128)S(1)}) custom-call(s32[6]{0:T(128)S(1)} %copy-done.19, bf16[16,128,128]{2,1,0:T(8,128)(2,1)S(1)} %all_to_all.20.got_ref, bf16[1024,1024]{1,0:T(8,128)(2,1)S(1)} %copy-done.1, bf16[256,1024]{1,0:T(8,128)(2,1)S(1)} %bitcast.50, f32[1,1024]{1,0:T(1,128)S(1)} %bitcast.63, ...), custom_call_target="tpu_custom_call" | custom-call | flops 536870912 | bytes 4724736 | tf_op jit(solution)/shard_map/mix/pallas_call | solution.py:228
  121.3 5.9 %multiply_convert_fusion = (bf16[256,4096]{1,0:T(8,128)(2,1)S(1)}, f32[256,4096]{1,0:T(8,128)S(1)}) fusion(f32[4096]{0:T(1024)S(1)} %copy-done.36, bf16[256,1024]{1,0:T(8,128)(2,1)} %get-tuple-element.107.n_ref, bf16[1024,4096]{1,0:T(8,128)(2,1)} %param.25), kind=kOutput, calls=%fused_computation.8 | convolution fusion | flops 2153775104 | bytes 15220736 | tf_op jit(solution)/shard_map/dot_general | solution.py:19
  130.4 5.1 %fusion.12 = (bf16[4096]{0:T(1024)(128)(2,1)S(1)}, bf16[256,4096]{1,0:T(8,128)(2,1)}) fusion(f32[256,4096]{1,0:T(8,128)S(1)} %get-tuple-element.205, bf16[256,1024]{1,0:T(8,128)(2,1)S(1)} %bitcast.54, bf16[4096,1024]{1,0:T(8,128)(2,1)S(1)} %bitcast.75), kind=kOutput, calls=%fused_computation.41 | convolution fusion | flops 2159013888 | bytes 15212544 | tf_op jit(solution)/shard_map/dot_general | solution.py:19
  135.9 6.7 %multiply_reduce_fusion = (bf16[1024]{0:T(1024)(128)(2,1)S(1)}, f32[256]{0:T(256)S(1)}, f32[256]{0:T(256)S(1)}, bf16[1024]{0:T(1024)(128)(2,1)S(1)}, f32[256,1024]{1,0:T(8,128)S(1)}) fusion(f32[256,1024]{1,0:T(8,128)S(1)} %get-tuple-element.106, f32[256]{0:T(256)S(1)} %add_rsqrt_fusion, f32[256]{0:T(256)S(1)} %broadcast_multiply_fusion.1, ...), kind=kOutput, calls=%fused_computation.15 | convolution fusion | flops 2149840384 | bytes 12595200 | tf_op jit(solution)/shard_map/dot_general | solution.py:19
  144.1 6.0 %collective-permute-done.6.refs_2_ = bf16[256,1024]{1,0:T(8,128)(2,1)S(1)} collective-permute-done((bf16[256,1024]{1,0:T(8,128)(2,1)}, bf16[256,1024]{1,0:T(8,128)(2,1)S(1)}, u32[]{:S(2)}, u32[]{:S(2)}) %collective-permute-start.6) | collective-permute-done | bytes 524320 | tf_op jit(solution)/shard_map/ppermute | solution.py:527
  151.4 2.1 collective-permute-done.7.bao_ref.bbo_ref
  153.5 9.8 %grads_up.1 = (bf16[4,64,2560]{2,1,0:T(8,128)(2,1)}, bf16[4,64,2560]{2,1,0:T(8,128)(2,1)S(1)}, bf16[512,1280]{1,0:T(8,128)(2,1)}, bf16[512,1280]{1,0:T(8,128)(2,1)S(1)}) custom-call(s32[6]{0:T(128)S(1)} %copy-done.19, bf16[256,1024]{1,0:T(8,128)(2,1)} %get-tuple-element.107.n_ref, bf16[256,1024]{1,0:T(8,128)(2,1)} %collective-permute-done.3.no_ref, ...), custom_call_target="tpu_custom_call" | custom-call | flops 2684354560 | bytes 17825792 | tf_op jit(solution)/shard_map/grads_up/pallas_call | solution.py:228
  169.6 3.1 grad_pack.1
  172.7 5.7 %all-to-all-start.2 = ((bf16[16,144,128]{2,1,0:T(8,128)(2,1)}), bf16[16,144,128]{2,1,0:T(8,128)(2,1)}, u32[]{:S(2)}, u32[]{:S(2)}) async-start(bf16[16,144,128]{2,1,0:T(8,128)(2,1)} %grad_pack.1), calls=%async_computation.2 | async-start | bytes 1179648 | tf_op jit(solution)/shard_map/all_to_all | solution.py:523
  184.2 6.1 %grads_down.1 = (bf16[2,256,1024]{2,1,0:T(8,128)(2,1)}, bf16[2,256,1024]{2,1,0:T(8,128)(2,1)S(1)}) custom-call(s32[6]{0:T(128)S(1)} %copy-done.19, bf16[256,4096]{1,0:T(8,128)(2,1)S(1)} %copy-done.7, bf16[256,1024]{1,0:T(8,128)(2,1)} %collective-permute-done.12.refs_1_, bf16[256,1024]{1,0:T(8,128)(2,1)S(1)} %copy-done.31, ...), custom_call_target="tpu_custom_call" | custom-call | flops 2147483648 | bytes 7864320 | tf_op jit(solution)/shard_map/grads_down/pallas_call | solution.py:228
  191.8 10.4 %collective-permute-done.8.refs_1_ = bf16[4,64,2560]{2,1,0:T(8,128)(2,1)} collective-permute-done((bf16[4,64,2560]{2,1,0:T(8,128)(2,1)}, bf16[4,64,2560]{2,1,0:T(8,128)(2,1)}, u32[]{:S(2)}, u32[]{:S(2)}) %collective-permute-start.8) | collective-permute-done | bytes 1310752 | tf_op jit(solution)/shard_map/ppermute | solution.py:527
  202.2 3.8 %add_one.1 = (bf16[4,64,1280]{2,1,0:T(8,128)(2,1)}, bf16[4,64,1280]{2,1,0:T(8,128)(2,1)S(1)}, bf16[4,64,1280]{2,1,0:T(8,128)(2,1)}, bf16[4,64,1280]{2,1,0:T(8,128)(2,1)S(1)}) custom-call(s32[6]{0:T(128)S(1)} %copy-done.19, bf16[4,64,2560]{2,1,0:T(8,128)(2,1)S(1)} %copy-done.12, bf16[4,64,2560]{2,1,0:T(8,128)(2,1)} %collective-permute-done.8.refs_1_, ...), custom_call_target="tpu_custom_call" | custom-call | flops 1310720 | bytes 7864320 | tf_op jit(solution)/shard_map/add_one/pallas_call | solution.py:228
  212.4 14.6 %attend_back.3 = (bf16[4096,128]{1,0:T(8,128)(2,1)S(1)}, f32[4,64,1024]{2,1,0:T(8,128)S(1)}, bf16[1024,128]{1,0:T(8,128)(2,1)S(1)}) custom-call(s32[4]{0:T(128)S(1)} %bitcast_subtract_fusion.starts, bf16[16,384,128]{2,1,0:T(8,128)(2,1)S(1)} %copy-done.10, bf16[4096,128]{1,0:T(8,128)(2,1)S(1)} %copy-done.33, bf16[16,144,128]{2,1,0:T(8,128)(2,1)} %all-to-all-done.2.refs_2_, ...), custom_call_target="tpu_custom_call" | custom-call | flops 5368709120 | bytes 8192000 | tf_op jit(solution)/shard_map/attend_back/pallas_call | solution.py:210
  227.1 2.7 add_two.1
  230.9 14.9 %attend_back.4 = (f32[4,64,1024]{2,1,0:T(8,128)S(1)}, bf16[1024,128]{1,0:T(8,128)(2,1)S(1)}) custom-call(s32[4]{0:T(128)S(1)} %bitcast_subtract_fusion.starts, bf16[16,384,128]{2,1,0:T(8,128)(2,1)S(1)} %copy-done.10, bf16[4096,128]{1,0:T(8,128)(2,1)S(1)} %copy-done.34, bf16[4096,128]{1,0:T(8,128)(2,1)S(1)} %get-tuple-element.174.refs_2_, ...), custom_call_target="tpu_custom_call" | custom-call | flops 5368709120 | bytes 8192000 | tf_op jit(solution)/shard_map/attend_back/pallas_call | solution.py:210
  247.6 2.2 collective-permute-start.18
  249.8 12.8 %attend_back.5.dx_ref = bf16[16,384,128]{2,1,0:T(8,128)(2,1)S(1)} custom-call(s32[4]{0:T(128)S(1)} %bitcast_subtract_fusion.starts, bf16[16,384,128]{2,1,0:T(8,128)(2,1)S(1)} %copy-done.10, bf16[4096,128]{1,0:T(8,128)(2,1)S(1)} %copy-done.34, bf16[4096,128]{1,0:T(8,128)(2,1)S(1)} %get-tuple-element.174.refs_2_, ...), custom_call_target="tpu_custom_call" | custom-call | flops 10737418240 | bytes 8192000 | tf_op jit(solution)/shard_map/attend_back/pallas_call | solution.py:210
  262.7 5.7 %weight_message.1 = bf16[16,496,128]{2,1,0:T(8,128)(2,1)} custom-call(s32[6]{0:T(128)S(1)} %copy-done.19, bf16[4096,1024]{1,0:T(8,128)(2,1)S(1)} %bitcast.48, bf16[16,384,128]{2,1,0:T(8,128)(2,1)S(1)} %attend_back.5.dx_ref), custom_call_target="tpu_custom_call" | custom-call | flops 1610612736 | bytes 11993088 | tf_op jit(solution)/shard_map/weight_message/pallas_call | solution.py:228
  270.4 9.1 %all-to-all-start.3 = ((bf16[16,496,128]{2,1,0:T(8,128)(2,1)}), bf16[16,496,128]{2,1,0:T(8,128)(2,1)}, u32[]{:S(2)}, u32[]{:S(2)}) async-start(bf16[16,496,128]{2,1,0:T(8,128)(2,1)} %weight_message.1), calls=%async_computation.3 | async-start | bytes 4063232 | tf_op jit(solution)/shard_map/all_to_all | solution.py:523
  283.1 7.1 %fusion.7 = bf16[1,256,1024]{2,1,0:T(8,128)(2,1)} fusion(f32[256,1024]{1,0:T(8,128)S(1)} %get-tuple-element.106, bf16[256,4096]{1,0:T(8,128)(2,1)} %copy-done.6, bf16[4096,1024]{1,0:T(8,128)(2,1)} %param.27, f32[1024]{0:T(1024)S(1)} %copy-done.37), kind=kOutput, calls=%fused_computation.13 | convolution fusion | flops 2148270080 | bytes 12062720 | tf_op jit(solution)/shard_map/dot_general | solution.py:19
  294.3 5.9 %collective-permute-done.22 = bf16[256,512]{1,0:T(8,128)(2,1)S(1)} collective-permute-done((bf16[256,512]{1,0:T(8,128)(2,1)S(1)}, bf16[256,512]{1,0:T(8,128)(2,1)S(1)}, u32[]{:S(2)}, u32[]{:S(2)}) %collective-permute-start.22) | collective-permute-done | bytes 262176 | tf_op jit(solution)/shard_map/ppermute | solution.py:531
  301.3 4.8 %collective-permute-done.20 = bf16[128,1280]{1,0:T(8,128)(2,1)S(1)} collective-permute-done((bf16[128,1280]{1,0:T(8,128)(2,1)S(1)}, bf16[128,1280]{1,0:T(8,128)(2,1)S(1)}, u32[]{:S(2)}, u32[]{:S(2)}) %collective-permute-start.20) | collective-permute-done | bytes 327712 | tf_op jit(solution)/shard_map/ppermute | solution.py:531
  309.2 16.5 %all-to-all-done.3.got_ref = bf16[16,496,128]{2,1,0:T(8,128)(2,1)} async-done(((bf16[16,496,128]{2,1,0:T(8,128)(2,1)}), bf16[16,496,128]{2,1,0:T(8,128)(2,1)}, u32[]{:S(2)}, u32[]{:S(2)}) %all-to-all-start.3) | async-done | bytes 2031648 | tf_op jit(solution)/shard_map/all_to_all | solution.py:523
  328.3 2.2 pad_maximum_fusion
  330.5 2.8 copy-done
  334.5 6.6 %input_grad.1 = bf16[256,1024]{1,0:T(8,128)(2,1)} custom-call(s32[6]{0:T(128)S(1)} %copy-done.19, bf16[16,496,128]{2,1,0:T(8,128)(2,1)} %all-to-all-done.3.got_ref, bf16[1024,3072]{1,0:T(8,128)(2,1)S(1)} %copy-done, bf16[1024,3072]{1,0:T(8,128)(2,1)S(1)} %copy-done, bf16[1024,3072]{1,0:T(8,128)(2,1)S(1)} %copy-done, bf16[256,1024]{1,0:T(8,128)(2,1)S(1)} %bitcast.51, ...), custom_call_target="tpu_custom_call" | custom-call | flops 1610612736 | bytes 22480896 | tf_op jit(solution)/shard_map/input_grad/pallas_call | solution.py:228
  (181 shorter events, 56.9 us)
Async XLA Ops:
  15.3 42.6 %all-to-all-start = ((bf16[16,384,128]{2,1,0:T(8,128)(2,1)}), bf16[16,384,128]{2,1,0:T(8,128)(2,1)S(1)}, u32[]{:S(2)}, u32[]{:S(2)}) async-start(bf16[16,384,128]{2,1,0:T(8,128)(2,1)} %get-tuple-element.102), calls=%async_computation | async-start | bytes 3145728 | tf_op jit(solution)/shard_map/all_to_all | solution.py:523
  21.5 151.3 %all-gather.2.cloned.1.call-start = ((), (), s32[]{:S(2)}) async-start(), calls=%async_computation.4 | async-start | bytes 8912896 | tf_op jit(solution)/shard_map/all_gather | solution.py:602
  21.5 28.6 %collective-permute-start.1 = (bf16[256,1024]{1,0:T(8,128)(2,1)S(1)}, bf16[256,1024]{1,0:T(8,128)(2,1)S(1)}, u32[]{:S(2)}, u32[]{:S(2)}) collective-permute-start(bf16[256,1024]{1,0:T(8,128)(2,1)S(1)} %bitcast.52), channel_id=1, source_target_pairs={{0,2},{1,3},{2,0},{3,1},{4,6},{5,7},{6,4},{7,5},{8,10},{9,11},{10,... | collective-permute-start | bytes 1572872 | tf_op jit(solution)/shard_map/ppermute | solution.py:527
  23.1 27.1 %collective-permute-start = (bf16[256,1024]{1,0:T(8,128)(2,1)S(1)}, bf16[256,1024]{1,0:T(8,128)(2,1)S(1)}, u32[]{:S(2)}, u32[]{:S(2)}) collective-permute-start(bf16[256,1024]{1,0:T(8,128)(2,1)S(1)} %bitcast.53), channel_id=1, source_target_pairs={{0,1},{1,0},{2,3},{3,2},{4,5},{5,4},{6,7},{7,6},{8,9},{9,8},{10,11... | collective-permute-start | bytes 1572872 | tf_op jit(solution)/shard_map/ppermute | solution.py:527
  50.1 1.9 collective-permute-start.2
  58.1 59.0 %copy-start.1 = (bf16[1024,1024]{1,0:T(8,128)(2,1)S(1)}, bf16[1024,1024]{1,0:T(8,128)(2,1)}, u32[]{:S(2)}) copy-start(bf16[1024,1024]{1,0:T(8,128)(2,1)} %w_ref.4) | copy-start | bytes 6291460
  58.1 59.0 %copy-start.3 = (bf16[1,256,1024]{2,1,0:T(8,128)(2,1)S(1)}, bf16[1,256,1024]{2,1,0:T(8,128)(2,1)}, u32[]{:S(2)}) copy-start(bf16[1,256,1024]{2,1,0:T(8,128)(2,1)} %param.15) | copy-start | bytes 1572868
  58.1 59.0 %copy-start.19 = (s32[6]{0:T(128)S(1)}, s32[6]{0:T(128)}, u32[]{:S(2)}) copy-start(s32[6]{0:T(128)} %stack.27.ids) | copy-start | bytes 76
  58.1 59.0 %copy-start.21 = (f32[1024]{0:T(1024)S(1)}, f32[1024]{0:T(1024)}, u32[]{:S(2)}) copy-start(f32[1024]{0:T(1024)} %param.23) | copy-start | bytes 12292
  58.1 58.9 %copy-start.22 = (f32[1024]{0:T(1024)S(1)}, f32[1024]{0:T(1024)}, u32[]{:S(2)}) copy-start(f32[1024]{0:T(1024)} %param.22) | copy-start | bytes 12292
  120.8 30.6 %collective-permute-start.3 = (bf16[256,1024]{1,0:T(8,128)(2,1)}, bf16[256,1024]{1,0:T(8,128)(2,1)}, u32[]{:S(2)}, u32[]{:S(2)}) collective-permute-start(bf16[256,1024]{1,0:T(8,128)(2,1)} %get-tuple-element.107.n_ref), channel_id=1, source_target_pairs={{0,1},{1,0},{2,3},{3,2},{4,5},{5,4},{6,7},{7,6},{8,9},{9,8},{10,11... | collective-permute-start | bytes 1572872 | tf_op jit(solution)/shard_map/ppermute | solution.py:527
  120.8 30.6 %collective-permute-start.4 = (bf16[256,1024]{1,0:T(8,128)(2,1)}, bf16[256,1024]{1,0:T(8,128)(2,1)}, u32[]{:S(2)}, u32[]{:S(2)}) collective-permute-start(bf16[256,1024]{1,0:T(8,128)(2,1)} %get-tuple-element.108.a_ref), channel_id=1, source_target_pairs={{0,1},{1,0},{2,3},{3,2},{4,5},{5,4},{6,7},{7,6},{8,9},{9,8},{10,11... | collective-permute-start | bytes 1572872 | tf_op jit(solution)/shard_map/ppermute | solution.py:527
  135.5 18.0 %collective-permute-start.5 = (bf16[256,4096]{1,0:T(8,128)(2,1)}, bf16[256,4096]{1,0:T(8,128)(2,1)}, u32[]{:S(2)}, u32[]{:S(2)}) collective-permute-start(bf16[256,4096]{1,0:T(8,128)(2,1)} %get-tuple-element.208.ua_ref.ub_ref), channel_id=1, source_target_pairs={{0,1},{1,0},{2,3},{3,2},{4,5},{5,4},{6,7},{7,6},{8,9},{9,8},{10,11... | collective-permute-start | bytes 6291464 | tf_op jit(solution)/shard_map/ppermute | solution.py:527
  135.5 14.5 %collective-permute-start.6 = (bf16[256,1024]{1,0:T(8,128)(2,1)}, bf16[256,1024]{1,0:T(8,128)(2,1)S(1)}, u32[]{:S(2)}, u32[]{:S(2)}) collective-permute-start(bf16[256,1024]{1,0:T(8,128)(2,1)} %get-tuple-element.113), channel_id=1, source_target_pairs={{0,2},{1,3},{2,0},{3,1},{4,6},{5,7},{6,4},{7,5},{8,10},{9,11},{10,... | collective-permute-start | bytes 1572872 | tf_op jit(solution)/shard_map/ppermute | solution.py:527
  150.8 2.6 collective-permute-start.7
  150.8 16.8 %collective-permute-start.12 = (bf16[256,1024]{1,0:T(8,128)(2,1)}, bf16[256,1024]{1,0:T(8,128)(2,1)}, u32[]{:S(2)}, u32[]{:S(2)}) collective-permute-start(bf16[256,1024]{1,0:T(8,128)(2,1)} %get-tuple-element.124), channel_id=1, source_target_pairs={{0,1},{1,0},{2,3},{3,2},{4,5},{5,4},{6,7},{7,6},{8,9},{9,8},{10,11... | collective-permute-start | bytes 1572872 | tf_op jit(solution)/shard_map/ppermute | solution.py:527
  151.4 16.3 %collective-permute-start.13 = (bf16[256,1024]{1,0:T(8,128)(2,1)}, bf16[256,1024]{1,0:T(8,128)(2,1)}, u32[]{:S(2)}, u32[]{:S(2)}) collective-permute-start(bf16[256,1024]{1,0:T(8,128)(2,1)} %get-tuple-element.126), channel_id=1, source_target_pairs={{0,3},{1,2},{2,1},{3,0},{4,7},{5,6},{6,5},{7,4},{8,11},{9,10},{10,... | collective-permute-start | bytes 1572872 | tf_op jit(solution)/shard_map/ppermute | solution.py:527
  165.6 36.7 %collective-permute-start.8 = (bf16[4,64,2560]{2,1,0:T(8,128)(2,1)}, bf16[4,64,2560]{2,1,0:T(8,128)(2,1)}, u32[]{:S(2)}, u32[]{:S(2)}) collective-permute-start(bf16[4,64,2560]{2,1,0:T(8,128)(2,1)} %get-tuple-element.118), channel_id=1, source_target_pairs={{0,2},{1,3},{2,0},{3,1},{4,6},{5,7},{6,4},{7,5},{8,10},{9,11},{10,... | collective-permute-start | bytes 3932168 | tf_op jit(solution)/shard_map/ppermute | solution.py:527
  165.8 36.4 %collective-permute-start.9 = (bf16[512,1280]{1,0:T(8,128)(2,1)}, bf16[512,1280]{1,0:T(8,128)(2,1)}, u32[]{:S(2)}, u32[]{:S(2)}) collective-permute-start(bf16[512,1280]{1,0:T(8,128)(2,1)} %get-tuple-element.120), channel_id=1, source_target_pairs={{0,16},{16,0},{1,17},{17,1},{2,18},{18,2},{3,19},{19,3},{4,20},{20... | collective-permute-start | bytes 3932168 | tf_op jit(solution)/shard_map/ppermute | solution.py:531
  172.7 36.0 %all-to-all-start.2 = ((bf16[16,144,128]{2,1,0:T(8,128)(2,1)}), bf16[16,144,128]{2,1,0:T(8,128)(2,1)}, u32[]{:S(2)}, u32[]{:S(2)}) async-start(bf16[16,144,128]{2,1,0:T(8,128)(2,1)} %grad_pack.1), calls=%async_computation.2 | async-start | bytes 1179648 | tf_op jit(solution)/shard_map/all_to_all | solution.py:523
  190.3 36.8 %collective-permute-start.14 = (bf16[2,256,1024]{2,1,0:T(8,128)(2,1)}, bf16[2,256,1024]{2,1,0:T(8,128)(2,1)}, u32[]{:S(2)}, u32[]{:S(2)}) collective-permute-start(bf16[2,256,1024]{2,1,0:T(8,128)(2,1)} %get-tuple-element.134), channel_id=1, source_target_pairs={{0,4},{1,5},{2,6},{3,7},{4,0},{5,1},{6,2},{7,3},{8,12},{9,13},{10,... | collective-permute-start | bytes 3145736 | tf_op jit(solution)/shard_map/ppermute | solution.py:527
  206.9 20.2 %collective-permute-start.10 = (bf16[4,64,1280]{2,1,0:T(8,128)(2,1)}, bf16[4,64,1280]{2,1,0:T(8,128)(2,1)}, u32[]{:S(2)}, u32[]{:S(2)}) collective-permute-start(bf16[4,64,1280]{2,1,0:T(8,128)(2,1)} %get-tuple-element.121), channel_id=1, source_target_pairs={{0,16},{16,0},{1,17},{17,1},{2,18},{18,2},{3,19},{19,3},{4,20},{20... | collective-permute-start | bytes 1966088 | tf_op jit(solution)/shard_map/ppermute | solution.py:531
  208.4 18.7 %collective-permute-start.11 = (bf16[4,64,1280]{2,1,0:T(8,128)(2,1)}, bf16[4,64,1280]{2,1,0:T(8,128)(2,1)}, u32[]{:S(2)}, u32[]{:S(2)}) collective-permute-start(bf16[4,64,1280]{2,1,0:T(8,128)(2,1)} %get-tuple-element.122), channel_id=1, source_target_pairs={{0,2},{1,3},{2,0},{3,1},{4,6},{5,7},{6,4},{7,5},{8,10},{9,11},{10,... | collective-permute-start | bytes 1966088 | tf_op jit(solution)/shard_map/ppermute | solution.py:527
  229.8 16.1 %collective-permute-start.15 = (bf16[2,128,1280]{2,1,0:T(8,128)(2,1)S(1)}, bf16[2,128,1280]{2,1,0:T(8,128)(2,1)S(1)}, u32[]{:S(2)}, u32[]{:S(2)}) collective-permute-start(bf16[2,128,1280]{2,1,0:T(8,128)(2,1)S(1)} %get-tuple-element.155), channel_id=1, source_target_pairs={{0,4},{1,5},{2,6},{3,7},{4,0},{5,1},{6,2},{7,3},{8,12},{9,13},{10,... | collective-permute-start | bytes 1966088 | tf_op jit(solution)/shard_map/ppermute | solution.py:527
  230.4 15.5 %collective-permute-start.16 = (bf16[2,256,512]{2,1,0:T(8,128)(2,1)S(1)}, bf16[2,256,512]{2,1,0:T(8,128)(2,1)S(1)}, u32[]{:S(2)}, u32[]{:S(2)}) collective-permute-start(bf16[2,256,512]{2,1,0:T(8,128)(2,1)S(1)} %get-tuple-element.156), channel_id=1, source_target_pairs={{0,16},{16,0},{1,17},{17,1},{2,18},{18,2},{3,19},{19,3},{4,20},{20... | collective-permute-start | bytes 1572872 | tf_op jit(solution)/shard_map/ppermute | solution.py:531
  246.8 23.6 %collective-permute-start.17 = (bf16[1,128,1280]{2,1,0:T(8,128)(2,1)S(1)}, bf16[1,128,1280]{2,1,0:T(8,128)(2,1)S(1)}, u32[]{:S(2)}, u32[]{:S(2)}) collective-permute-start(bf16[1,128,1280]{2,1,0:T(8,128)(2,1)S(1)} %get-tuple-element.171), channel_id=1, source_target_pairs={{0,8},{1,9},{2,10},{3,11},{4,12},{5,13},{6,14},{7,15},{8,0},{9,1},... | collective-permute-start | bytes 983048 | tf_op jit(solution)/shard_map/ppermute | solution.py:527
  247.6 22.8 %collective-permute-start.18 = (bf16[1,256,512]{2,1,0:T(8,128)(2,1)S(1)}, bf16[1,256,512]{2,1,0:T(8,128)(2,1)S(1)}, u32[]{:S(2)}, u32[]{:S(2)}) collective-permute-start(bf16[1,256,512]{2,1,0:T(8,128)(2,1)S(1)} %get-tuple-element.172), channel_id=1, source_target_pairs={{0,8},{1,9},{2,10},{3,11},{4,12},{5,13},{6,14},{7,15},{8,0},{9,1},... | collective-permute-start | bytes 786440 | tf_op jit(solution)/shard_map/ppermute | solution.py:527
  270.4 55.3 %all-to-all-start.3 = ((bf16[16,496,128]{2,1,0:T(8,128)(2,1)}), bf16[16,496,128]{2,1,0:T(8,128)(2,1)}, u32[]{:S(2)}, u32[]{:S(2)}) async-start(bf16[16,496,128]{2,1,0:T(8,128)(2,1)} %weight_message.1), calls=%async_computation.3 | async-start | bytes 4063232 | tf_op jit(solution)/shard_map/all_to_all | solution.py:523
  281.5 10.0 %collective-permute-start.21 = (bf16[512]{0:T(512)(128)(2,1)S(1)}, bf16[512]{0:T(512)(128)(2,1)S(1)}, u32[]{:S(2)}, u32[]{:S(2)}) collective-permute-start(bf16[512]{0:T(512)(128)(2,1)S(1)} %bitcast.72), channel_id=1, source_target_pairs={{0,16},{16,0},{1,17},{17,1},{2,18},{18,2},{3,19},{19,3},{4,20},{20... | collective-permute-start | bytes 3080 | tf_op jit(solution)/shard_map/ppermute | solution.py:518
  291.0 9.3 %collective-permute-start.22 = (bf16[256,512]{1,0:T(8,128)(2,1)S(1)}, bf16[256,512]{1,0:T(8,128)(2,1)S(1)}, u32[]{:S(2)}, u32[]{:S(2)}) collective-permute-start(bf16[256,512]{1,0:T(8,128)(2,1)S(1)} %bitcast.58), channel_id=1, source_target_pairs={{0,16},{16,0},{1,17},{17,1},{2,18},{18,2},{3,19},{19,3},{4,20},{20... | collective-permute-start | bytes 786440 | tf_op jit(solution)/shard_map/ppermute | solution.py:531
  292.8 13.4 %collective-permute-start.20 = (bf16[128,1280]{1,0:T(8,128)(2,1)S(1)}, bf16[128,1280]{1,0:T(8,128)(2,1)S(1)}, u32[]{:S(2)}, u32[]{:S(2)}) collective-permute-start(bf16[128,1280]{1,0:T(8,128)(2,1)S(1)} %bitcast.57), channel_id=1, source_target_pairs={{0,16},{16,0},{1,17},{17,1},{2,18},{18,2},{3,19},{19,3},{4,20},{20... | collective-permute-start | bytes 983048 | tf_op jit(solution)/shard_map/ppermute | solution.py:531
  326.7 14.4 %collective-permute-start.19 = (bf16[16,112,128]{2,1,0:T(8,128)(2,1)S(1)}, bf16[16,112,128]{2,1,0:T(8,128)(2,1)S(1)}, u32[]{:S(2)}, u32[]{:S(2)}) collective-permute-start(bf16[16,112,128]{2,1,0:T(8,128)(2,1)S(1)} %slice.44.one_ref), channel_id=1, source_target_pairs={{0,16},{16,0},{1,17},{17,1},{2,18},{18,2},{3,19},{19,3},{4,20},{20... | collective-permute-start | bytes 1376264 | tf_op jit(solution)/shard_map/ppermute | solution.py:531
  (40 other events, 481.4 us)
Sparse Core Ops, SparseCore 0:
  58.0 78.4 all-gather.1

commit v5 on v4

--- a/solution.py
+++ b/solution.py
@@ -263,50 +263,45 @@
          pl.BlockSpec((1,wide,width),lambda s,ids:(jnp.maximum(s-2,0),0,0))],[],"grads_down",2*tokens*inner*width)
 
 def up_kernel(ids, n_ref, no_ref, a_ref, ao_ref, ua_ref, uao_ref, ub_ref, ubo_ref, ba_ref, bao_ref, bb_ref, bbo_ref,
-              as_ref, ak_ref, bs_ref, bk_ref, ln_ref, la_ref, *, share):
+              a_out, b_out, left_ref, part_ref, *, share, keep):
     s=pl.program_id(0); tokens,width=n_ref.shape; tile=width//2
+    across=ids[1] if keep else 1-ids[1]
     @pl.when(s==0)
     def _():
-        f=lax.broadcasted_iota(jnp.int32,(width,tile),0); j=lax.broadcasted_iota(jnp.int32,(width,tile),1)
+        f=lax.broadcasted_iota(jnp.int32,(tile,width),1); j=lax.broadcasted_iota(jnp.int32,(tile,width),0)
         pick=jnp.where(f==(j//share*2+ids[0])*share+j%share,1.0,0.0).astype(BF)
-        for ref,pair in ((ln_ref,(n_ref,no_ref)),(la_ref,(a_ref,ao_ref))):
+        for p,pair in enumerate(((n_ref,no_ref),(a_ref,ao_ref))):
             for e,src in enumerate(pair):
-                ref[e*tokens:(e+1)*tokens,:]=dotf(src[...],pick,NN).astype(BF)
+                v=dotf(pick,src[...],NT)
+                left_ref[p,:,e*tokens:(e+1)*tokens]=v.astype(BF)
+                v=v.reshape(-1,2,share,tokens)
+                part_ref[p,:,e*tokens:(e+1)*tokens]=jnp.where(across==0,v[:,0],v[:,1]).reshape(tile//2,tokens).astype(BF)
     def product(left,one,two):
-        return (dotf(left[:tokens],one[...],TN)+dotf(left[tokens:],two[...],TN)).astype(BF)
-    def put_a(v):
-        v=v.reshape(as_ref.shape[0],2,share,tile)
-        low,high=v[:,0],v[:,1]
-        cols=pl.ds(pl.multiple_of(s*tile,tile),tile)
-        ak_ref[:,:,cols]=jnp.where(ids[1]==0,low,high)
-        as_ref[:,:,cols]=jnp.where(ids[1]==0,high,low)
+        return (dotf(left[:,:tokens],one[...],NN)+dotf(left[:,tokens:],two[...],NN)).astype(BF)
     @pl.when(s<4)
-    def _():
-        put_a(product(ln_ref,ua_ref,uao_ref))
-        v=product(ln_ref,ub_ref,ubo_ref)
-        cols=pl.ds(pl.multiple_of(s%2*tile,tile),tile)
-        @pl.when(s//2==ids[2])
-        def _(): bk_ref[:,cols]=v
-        @pl.when(s//2!=ids[2])
-        def _(): bs_ref[:,cols]=v
+    def _(): a_out[...]=product(part_ref[0],ua_ref,uao_ref).reshape(a_out.shape)
     @pl.when(s==4)
-    def _():
-        put_a(product(la_ref,ba_ref,bao_ref))
-        v=product(la_ref,bb_ref,bbo_ref)
-        low,high=v[:,:tile//2],v[:,tile//2:]
-        bk_ref[:,2*tile:]=jnp.where(ids[2]==0,low,high)
-        bs_ref[:,2*tile:]=jnp.where(ids[2]==0,high,low)
-
-def grads_up(ids, normed, normed_other, att, att_other, up, up_other, branch, branch_other, ranks):
+    def _(): a_out[...]=product(part_ref[1],ba_ref,bao_ref).reshape(a_out.shape)
+    for t in range(2):
+        @pl.when(s==t)
+        def _(): b_out[:,t*tile:(t+1)*tile]=product(left_ref[0],ub_ref,ubo_ref)
+    @pl.when(s==2)
+    def _(): b_out[:,2*tile:]=product(left_ref[1],bb_ref,bbo_ref)
+
+def grads_up(ids, normed, normed_other, att, att_other, up, up_other, branch, branch_other, ranks, keep):
     tokens,width=normed.shape; share=width//ranks; tile=width//2
     f=fixed_block(normed.shape)
-    at=lambda base:pl.BlockSpec((tokens,tile),lambda s,ids:(0,base+jnp.minimum(s,3)))
-    fix=lambda col:pl.BlockSpec((tokens,tile),lambda s,ids:(0,col))
-    a=jax.ShapeDtypeStruct((ranks//4,share,5*tile),BF); b=jax.ShapeDtypeStruct((tile,5*tile//2),BF)
-    return run_kernel(functools.partial(up_kernel,share=share),ids,(5,),
+    side=lambda ids: ids[2] if keep else 1-ids[2]
+    ua=pl.BlockSpec((tokens,tile),lambda s,ids:(0,jnp.minimum(s,3)))
+    ub=pl.BlockSpec((tokens,tile),lambda s,ids:(0,4+2*side(ids)+jnp.minimum(s,1)))
+    ba=pl.BlockSpec((tokens,tile),lambda s,ids:(0,0))
+    bb=pl.BlockSpec((tokens,tile//2),lambda s,ids:(0,2+side(ids)))
+    outs=[jax.ShapeDtypeStruct((ranks//4,share,5*tile),BF),jax.ShapeDtypeStruct((tile,5*tile//2),BF)]
+    return run_kernel(functools.partial(up_kernel,share=share,keep=keep),ids,(5,),
         [normed,normed_other,att,att_other,up,up_other,up,up_other,branch,branch_other,branch,branch_other],
-        [f,f,f,f,at(0),at(0),at(4),at(4),fix(0),fix(0),fix(1),fix(1)],[a,a,b,b],[fixed_block(v.shape) for v in (a,a,b,b)],
-        [pltpu.VMEM((2*tokens,tile),BF)]*2,"grads_up",2*tokens*width*(up.shape[1]+width))
+        [f,f,f,f,ua,ua,ub,ub,ba,ba,bb,bb],outs,
+        [pl.BlockSpec((ranks//4,share,tile),lambda s,ids:(0,0,s)),fixed_block(outs[1].shape)],
+        [pltpu.VMEM((2,tile,2*tokens),BF),pltpu.VMEM((2,tile//2,2*tokens),BF)],"grads_up",tokens*width*(up.shape[1]+width))
 
 def add_kernel(ids, *refs, plan):
     n=sum(len(parts) for _,_,parts in plan)
@@ -623,8 +618,7 @@
     if fast:
         others[1], branch_grad = lax.optimization_barrier((others[1], branch_grad))
     if fast:
-        a_sent, a_keep, b_sent, b_keep = grads_up(
-            ids,
+        factors = [
             normed_two_low,
             swap(normed_two_low, 1),
             attended_low,
@@ -633,8 +627,8 @@
             swap(up_grad, 1),
             branch_grad,
             swap(branch_grad, 1),
-            ranks,
-        )
+        ]
+        a_sent, b_sent = grads_up(ids, *factors, ranks, False)
         branch_grad, a_sent, b_sent = lax.optimization_barrier((branch_grad, a_sent, b_sent))
         branch_grad, others = lax.optimization_barrier((branch_grad, others))
         a_got, b_got = swap(a_sent, 2), swap_row(b_sent)
@@ -668,6 +662,8 @@
     tiles = full // BWD_TILE[1]
     if fast:
         blocks = lambda v: v.reshape(ranks // 2, share, -1)
+        factors, _ = lax.optimization_barrier((factors, sent))
+        a_keep, b_keep = grads_up(ids, *factors, ranks, True)
         a_sent, a_keep, b_sent, b_keep = add_split(
             ids, (("columns", 2, "a"), ("blocks", 1, "b")), [a_keep, a_got, blocks(b_keep), blocks(b_got)], "add_one"
         )

time: 358 us -> 346 us (0.966)
  waiting for transfers between devices: 81 us -> 64.2 us
  local copies, waits for them, and re-layouts: 29.7 us -> 24.8 us
  starting transfers between devices: 37.9 us -> 42.3 us
  Pallas kernels: 122 us -> 126 us
    ppermute x16, waiting for transfers between devices: 48.7 us -> 31.9 us  [swap(): lax.ppermute(value, 'seq', [(i, i ^ bit) for i in range(lax.axis_size('se...]
    unnamed x90 -> x92, local copies, waits for them, and re-layouts: 22.9 us -> 18 us
    pallas_call x13 -> x14, Pallas kernels: 54.2 us -> 58.7 us  [run_kernel(): pl.pallas_call(kernel, grid_spec=pltpu.PrefetchScalarGridSpec(num_scalar_...]
    ppermute x16, starting transfers between devices: 8.17 us -> 12.6 us  [swap(): lax.ppermute(value, 'seq', [(i, i ^ bit) for i in range(lax.axis_size('se...]
  transfers between devices with their start and end apart: 27 -> 27, of which waited for: 10 -> 9; matrix products, arithmetic and copies ran while one was open for 11% -> 11% of each run, Pallas kernels for 31% -> 33%
where the time goes in v5:
time: 346 us; the launch traced here: 340 us
  Pallas kernels  126 us (36%)
  waiting for transfers between devices  64.2 us (19%)
  starting transfers between devices  42.3 us (12%)
  blocking collectives  32.5 us (9%)
  local copies, waits for them, and re-layouts  24.8 us (7%)
  matrix products  23.6 us (7%)
  between operations  15.2 us (4%)
  other arithmetic  11.2 us (3%)
    pallas_call x14, Pallas kernels, run_kernel(): pl.pallas_call(kernel, grid_spec=pltpu.PrefetchScalarGridSpec(num_scalar_...  58.7 us
    pallas_call x3, Pallas kernels, attend_back(): pl.pallas_call(functools.partial(bwd_kernel, bq=bq, bk=bk, segs=segs, beg...  42 us
    all_to_all x1, blocking collectives, exchange(): return lax.all_to_all(value, 'seq', 0, 0, tiled=True)  32.5 us
    ppermute x16, waiting for transfers between devices, swap(): lax.ppermute(value, 'seq', [(i, i ^ bit) for i in range(lax.axis_size('se...  31.9 us
    pallas_call x1, Pallas kernels, attend(): pl.pallas_call(functools.partial(fwd_kernel, bq=bq, bk=bk, segs=segs, gro...  25.1 us
    dot_general x4, matrix products, dotf(): return lax.dot_general(a, b, dims, preferred_element_type=F32)  23.6 us
    all_to_all x3, waiting for transfers between devices, exchange(): return lax.all_to_all(value, 'seq', 0, 0, tiled=True)  21.5 us
    all_to_all x3, starting transfers between devices, exchange(): return lax.all_to_all(value, 'seq', 0, 0, tiled=True)  20.8 us
  transfers between devices with their start and end apart: 27, of which 9 were waited for; matrix products, arithmetic and copies ran while one was open for 11% of the time, Pallas kernels for 33%

profile of v5, /device:TPU:16, one launch (start us, length us, event | category | flops | bytes accessed | tf_op | source)
XLA Modules:
  0.0 339.6 jit_solution(8134913557207272064)
XLA Ops:
  7.9 7.4 %project.1 = (bf16[16,384,128]{2,1,0:T(8,128)(2,1)}, bf16[256,1024]{1,0:T(8,128)(2,1)}) custom-call(s32[6]{0:T(128)} %stack.27.ids, bf16[256,1024]{1,0:T(8,128)(2,1)} %bitcast.49, f32[1,1024]{1,0:T(1,128)} %bitcast.59, f32[1,1024]{1,0:T(1,128)} %bitcast.68, bf16[1024,3072]{1,0:T(8,128)(2,1)} %w_ref.5, bf16[1024,3072]{1,0:T(8,128)(2,1)} %w_ref.5, ...), custom_call_target="tpu_custom_call" | custom-call | flops 1610612736 | bytes 21508096 | tf_op jit(solution)/shard_map/project/pallas_call | solution.py:228
  15.3 6.2 %all-to-all-start = ((bf16[16,384,128]{2,1,0:T(8,128)(2,1)}), bf16[16,384,128]{2,1,0:T(8,128)(2,1)S(1)}, u32[]{:S(2)}, u32[]{:S(2)}) async-start(bf16[16,384,128]{2,1,0:T(8,128)(2,1)} %get-tuple-element.110), calls=%async_computation | async-start | bytes 3145728 | tf_op jit(solution)/shard_map/all_to_all | solution.py:518
  23.1 27.1 %collective-permute-done.1.refs_6_ = bf16[256,1024]{1,0:T(8,128)(2,1)S(1)} collective-permute-done((bf16[256,1024]{1,0:T(8,128)(2,1)S(1)}, bf16[256,1024]{1,0:T(8,128)(2,1)S(1)}, u32[]{:S(2)}, u32[]{:S(2)}) %collective-permute-start.1) | collective-permute-done | bytes 524320 | tf_op jit(solution)/shard_map/ppermute | solution.py:522
  52.8 5.1 %all-to-all-done.x_ref.refs_0_ = bf16[16,384,128]{2,1,0:T(8,128)(2,1)S(1)} async-done(((bf16[16,384,128]{2,1,0:T(8,128)(2,1)}), bf16[16,384,128]{2,1,0:T(8,128)(2,1)S(1)}, u32[]{:S(2)}, u32[]{:S(2)}) %all-to-all-start) | async-done | bytes 1572896 | tf_op jit(solution)/shard_map/all_to_all | solution.py:518
  58.1 25.1 %attend.1 = (bf16[16,128,128]{2,1,0:T(8,128)(2,1)S(1)}, bf16[4096,128]{1,0:T(8,128)(2,1)S(1)}) custom-call(s32[4]{0:T(128)S(1)} %bitcast_subtract_fusion.starts, s32[1]{0:T(128)} %constant.96.clone.1.part, bf16[16,384,128]{2,1,0:T(8,128)(2,1)S(1)} %all-to-all-done.x_ref.refs_0_), custom_call_target="tpu_custom_call" | custom-call | flops 8589934592 | bytes 6553600 | tf_op jit(solution)/shard_map/attend/pallas_call | solution.py:114
  84.2 32.5 %all_to_all.20.got_ref = bf16[16,128,128]{2,1,0:T(8,128)(2,1)S(1)} all-to-all(bf16[16,128,128]{2,1,0:T(8,128)(2,1)S(1)} %get-tuple-element.113.refs_3_), channel_id=1, replica_groups=mesh['row'=2,'seq'=16] {'seq'}, dimensions={0} | all-to-all | bytes 1048576 | tf_op jit(solution)/shard_map/all_to_all | solution.py:518
  116.8 3.7 %mix.1 = (bf16[256,1024]{1,0:T(8,128)(2,1)}, bf16[256,1024]{1,0:T(8,128)(2,1)}, f32[256,1024]{1,0:T(8,128)S(1)}) custom-call(s32[6]{0:T(128)S(1)} %copy-done.22, bf16[16,128,128]{2,1,0:T(8,128)(2,1)S(1)} %all_to_all.20.got_ref, bf16[1024,1024]{1,0:T(8,128)(2,1)S(1)} %copy-done.3, bf16[256,1024]{1,0:T(8,128)(2,1)S(1)} %bitcast.50, f32[1,1024]{1,0:T(1,128)S(1)} %bitcast.63, ...), custom_call_target="tpu_custom_call" | custom-call | flops 536870912 | bytes 4724736 | tf_op jit(solution)/shard_map/mix/pallas_call | solution.py:228
  120.9 6.0 %multiply_convert_fusion = (bf16[256,4096]{1,0:T(8,128)(2,1)S(1)}, f32[256,4096]{1,0:T(8,128)S(1)}) fusion(f32[4096]{0:T(1024)S(1)} %copy-done.37, bf16[256,1024]{1,0:T(8,128)(2,1)} %get-tuple-element.132.n_ref, bf16[1024,4096]{1,0:T(8,128)(2,1)} %param.25), kind=kOutput, calls=%fused_computation.8 | convolution fusion | flops 2153775104 | bytes 15220736 | tf_op jit(solution)/shard_map/dot_general | solution.py:19
  129.1 4.2 %fusion.12 = (bf16[4096]{0:T(1024)(128)(2,1)S(1)}, bf16[256,4096]{1,0:T(8,128)(2,1)S(1)}) fusion(f32[256,4096]{1,0:T(8,128)S(1)} %get-tuple-element.221, bf16[256,1024]{1,0:T(8,128)(2,1)S(1)} %bitcast.54, bf16[4096,1024]{1,0:T(8,128)(2,1)S(1)} %bitcast.75), kind=kOutput, calls=%fused_computation.41 | convolution fusion | flops 2159013888 | bytes 15212544 | tf_op jit(solution)/shard_map/dot_general | solution.py:19
  133.8 6.2 %multiply_reduce_fusion = (bf16[1024]{0:T(1024)(128)(2,1)S(1)}, f32[256]{0:T(256)S(1)}, f32[256]{0:T(256)S(1)}, bf16[1024]{0:T(1024)(128)(2,1)S(1)}, f32[256,1024]{1,0:T(8,128)S(1)}) fusion(f32[256,1024]{1,0:T(8,128)S(1)} %get-tuple-element.114, f32[256]{0:T(256)S(1)} %add_rsqrt_fusion, f32[256]{0:T(256)S(1)} %broadcast_multiply_fusion.1, ...), kind=kOutput, calls=%fused_computation.15 | convolution fusion | flops 2149840384 | bytes 12595200 | tf_op jit(solution)/shard_map/dot_general | solution.py:19
  140.0 2.6 fusion.9
  145.2 8.2 %grads_up.2 = (bf16[4,64,2560]{2,1,0:T(8,128)(2,1)}, bf16[512,1280]{1,0:T(8,128)(2,1)}) custom-call(s32[6]{0:T(128)S(1)} %copy-done.22, bf16[256,1024]{1,0:T(8,128)(2,1)} %get-tuple-element.132.n_ref, bf16[256,1024]{1,0:T(8,128)(2,1)} %collective-permute-done.3.no_ref, bf16[256,1024]{1,0:T(8,128)(2,1)} %get-tuple-element.134.a_ref, ...), custom_call_target="tpu_custom_call" | custom-call | flops 1342177280 | bytes 15204352 | tf_op jit(solution)/shard_map/grads_up/pallas_call | solution.py:228
  159.9 2.2 grad_pack.1
  163.0 6.3 %all-to-all-start.2 = ((bf16[16,144,128]{2,1,0:T(8,128)(2,1)}), bf16[16,144,128]{2,1,0:T(8,128)(2,1)}, u32[]{:S(2)}, u32[]{:S(2)}) async-start(bf16[16,144,128]{2,1,0:T(8,128)(2,1)} %copy-done.8), calls=%async_computation.2 | async-start | bytes 1179648 | tf_op jit(solution)/shard_map/all_to_all | solution.py:518
  175.0 6.1 %grads_down.1 = (bf16[2,256,1024]{2,1,0:T(8,128)(2,1)}, bf16[2,256,1024]{2,1,0:T(8,128)(2,1)S(1)}) custom-call(s32[6]{0:T(128)S(1)} %copy-done.22, bf16[256,4096]{1,0:T(8,128)(2,1)S(1)} %copy-done.11, bf16[256,1024]{1,0:T(8,128)(2,1)} %collective-permute-done.8.refs_1_, bf16[256,1024]{1,0:T(8,128)(2,1)} %collective-permute-done.6.refs_2_, ...), custom_call_target="tpu_custom_call" | custom-call | flops 2147483648 | bytes 7864320 | tf_op jit(solution)/shard_map/grads_down/pallas_call | solution.py:228
  182.6 7.1 %grads_up.3 = (bf16[4,64,2560]{2,1,0:T(8,128)(2,1)S(1)}, bf16[512,1280]{1,0:T(8,128)(2,1)S(1)}) custom-call(s32[6]{0:T(128)S(1)} %copy-done.22, bf16[256,1024]{1,0:T(8,128)(2,1)} %get-tuple-element.132.n_ref, bf16[256,1024]{1,0:T(8,128)(2,1)} %collective-permute-done.3.no_ref, bf16[256,1024]{1,0:T(8,128)(2,1)} %get-tuple-element.134.a_ref, ...), custom_call_target="tpu_custom_call" | custom-call | flops 1342177280 | bytes 15204352 | tf_op jit(solution)/shard_map/grads_up/pallas_call | solution.py:228
  191.1 3.8 %add_one.1 = (bf16[4,64,1280]{2,1,0:T(8,128)(2,1)}, bf16[4,64,1280]{2,1,0:T(8,128)(2,1)S(1)}, bf16[4,64,1280]{2,1,0:T(8,128)(2,1)}, bf16[4,64,1280]{2,1,0:T(8,128)(2,1)S(1)}) custom-call(s32[6]{0:T(128)S(1)} %copy-done.22, bf16[4,64,2560]{2,1,0:T(8,128)(2,1)S(1)} %get-tuple-element.140.refs_0_, bf16[4,64,2560]{2,1,0:T(8,128)(2,1)} %collective-permute-done.10.refs_1_, ...), custom_call_target="tpu_custom_call" | custom-call | flops 1310720 | bytes 7864320 | tf_op jit(solution)/shard_map/add_one/pallas_call | solution.py:228
  200.7 14.5 %attend_back.3 = (bf16[4096,128]{1,0:T(8,128)(2,1)S(1)}, f32[4,64,1024]{2,1,0:T(8,128)S(1)}, bf16[1024,128]{1,0:T(8,128)(2,1)S(1)}) custom-call(s32[4]{0:T(128)S(1)} %bitcast_subtract_fusion.starts, bf16[16,384,128]{2,1,0:T(8,128)(2,1)S(1)} %copy-done.17, bf16[4096,128]{1,0:T(8,128)(2,1)S(1)} %copy-done.34, bf16[16,144,128]{2,1,0:T(8,128)(2,1)} %all-to-all-done.2.refs_2_, ...), custom_call_target="tpu_custom_call" | custom-call | flops 5368709120 | bytes 8192000 | tf_op jit(solution)/shard_map/attend_back/pallas_call | solution.py:210
  215.3 2.5 add_two.1
  218.4 14.9 %attend_back.4 = (f32[4,64,1024]{2,1,0:T(8,128)S(1)}, bf16[1024,128]{1,0:T(8,128)(2,1)S(1)}) custom-call(s32[4]{0:T(128)S(1)} %bitcast_subtract_fusion.starts, bf16[16,384,128]{2,1,0:T(8,128)(2,1)S(1)} %copy-done.17, bf16[4096,128]{1,0:T(8,128)(2,1)S(1)} %copy-done.35, bf16[4096,128]{1,0:T(8,128)(2,1)S(1)} %get-tuple-element.190.refs_2_, ...), custom_call_target="tpu_custom_call" | custom-call | flops 5368709120 | bytes 8192000 | tf_op jit(solution)/shard_map/attend_back/pallas_call | solution.py:210
  234.7 2.5 collective-permute-start.17
  237.2 12.6 %attend_back.5.dx_ref = bf16[16,384,128]{2,1,0:T(8,128)(2,1)S(1)} custom-call(s32[4]{0:T(128)S(1)} %bitcast_subtract_fusion.starts, bf16[16,384,128]{2,1,0:T(8,128)(2,1)S(1)} %copy-done.17, bf16[4096,128]{1,0:T(8,128)(2,1)S(1)} %copy-done.35, bf16[4096,128]{1,0:T(8,128)(2,1)S(1)} %get-tuple-element.190.refs_2_, ...), custom_call_target="tpu_custom_call" | custom-call | flops 10737418240 | bytes 8192000 | tf_op jit(solution)/shard_map/attend_back/pallas_call | solution.py:210
  249.8 5.8 %weight_message.1 = bf16[16,496,128]{2,1,0:T(8,128)(2,1)} custom-call(s32[6]{0:T(128)S(1)} %copy-done.22, bf16[4096,1024]{1,0:T(8,128)(2,1)S(1)} %bitcast.48, bf16[16,384,128]{2,1,0:T(8,128)(2,1)S(1)} %attend_back.5.dx_ref), custom_call_target="tpu_custom_call" | custom-call | flops 1610612736 | bytes 11993088 | tf_op jit(solution)/shard_map/weight_message/pallas_call | solution.py:228
  255.6 3.0 collective-permute-done.17.refs_1_
  258.7 8.4 %all-to-all-start.3 = ((bf16[16,496,128]{2,1,0:T(8,128)(2,1)}), bf16[16,496,128]{2,1,0:T(8,128)(2,1)}, u32[]{:S(2)}, u32[]{:S(2)}) async-start(bf16[16,496,128]{2,1,0:T(8,128)(2,1)} %weight_message.1), calls=%async_computation.3 | async-start | bytes 4063232 | tf_op jit(solution)/shard_map/all_to_all | solution.py:518
  270.7 7.1 %fusion.7 = bf16[1,256,1024]{2,1,0:T(8,128)(2,1)} fusion(f32[256,1024]{1,0:T(8,128)S(1)} %copy-done.2, bf16[256,4096]{1,0:T(8,128)(2,1)} %copy-done.10, bf16[4096,1024]{1,0:T(8,128)(2,1)} %param.27, f32[1024]{0:T(1024)S(1)} %copy-done.38), kind=kOutput, calls=%fused_computation.13 | convolution fusion | flops 2148270080 | bytes 12062720 | tf_op jit(solution)/shard_map/dot_general | solution.py:19
  281.9 5.9 %collective-permute-done.22 = bf16[256,512]{1,0:T(8,128)(2,1)S(1)} collective-permute-done((bf16[256,512]{1,0:T(8,128)(2,1)S(1)}, bf16[256,512]{1,0:T(8,128)(2,1)S(1)}, u32[]{:S(2)}, u32[]{:S(2)}) %collective-permute-start.22) | collective-permute-done | bytes 262176 | tf_op jit(solution)/shard_map/ppermute | solution.py:526
  288.9 4.8 %collective-permute-done.20 = bf16[128,1280]{1,0:T(8,128)(2,1)S(1)} collective-permute-done((bf16[128,1280]{1,0:T(8,128)(2,1)S(1)}, bf16[128,1280]{1,0:T(8,128)(2,1)S(1)}, u32[]{:S(2)}, u32[]{:S(2)}) %collective-permute-start.20) | collective-permute-done | bytes 327712 | tf_op jit(solution)/shard_map/ppermute | solution.py:526
  296.8 16.5 %all-to-all-done.3.got_ref = bf16[16,496,128]{2,1,0:T(8,128)(2,1)} async-done(((bf16[16,496,128]{2,1,0:T(8,128)(2,1)}), bf16[16,496,128]{2,1,0:T(8,128)(2,1)}, u32[]{:S(2)}, u32[]{:S(2)}) %all-to-all-start.3) | async-done | bytes 2031648 | tf_op jit(solution)/shard_map/all_to_all | solution.py:518
  315.9 2.2 pad_maximum_fusion
  318.1 2.8 copy-done
  322.1 6.6 %input_grad.1 = bf16[256,1024]{1,0:T(8,128)(2,1)} custom-call(s32[6]{0:T(128)S(1)} %copy-done.22, bf16[16,496,128]{2,1,0:T(8,128)(2,1)} %all-to-all-done.3.got_ref, bf16[1024,3072]{1,0:T(8,128)(2,1)S(1)} %copy-done, bf16[1024,3072]{1,0:T(8,128)(2,1)S(1)} %copy-done, bf16[1024,3072]{1,0:T(8,128)(2,1)S(1)} %copy-done, bf16[256,1024]{1,0:T(8,128)(2,1)S(1)} %bitcast.51, ...), custom_call_target="tpu_custom_call" | custom-call | flops 1610612736 | bytes 22480896 | tf_op jit(solution)/shard_map/input_grad/pallas_call | solution.py:228
  (184 shorter events, 54.6 us)
Async XLA Ops:
  15.3 42.6 %all-to-all-start = ((bf16[16,384,128]{2,1,0:T(8,128)(2,1)}), bf16[16,384,128]{2,1,0:T(8,128)(2,1)S(1)}, u32[]{:S(2)}, u32[]{:S(2)}) async-start(bf16[16,384,128]{2,1,0:T(8,128)(2,1)} %get-tuple-element.110), calls=%async_computation | async-start | bytes 3145728 | tf_op jit(solution)/shard_map/all_to_all | solution.py:518
  21.5 141.5 %all-gather.2.cloned.1.call-start = ((), (), s32[]{:S(2)}) async-start(), calls=%async_computation.4 | async-start | bytes 8912896 | tf_op jit(solution)/shard_map/all_gather | solution.py:597
  21.5 28.6 %collective-permute-start.1 = (bf16[256,1024]{1,0:T(8,128)(2,1)S(1)}, bf16[256,1024]{1,0:T(8,128)(2,1)S(1)}, u32[]{:S(2)}, u32[]{:S(2)}) collective-permute-start(bf16[256,1024]{1,0:T(8,128)(2,1)S(1)} %bitcast.52), channel_id=1, source_target_pairs={{0,2},{1,3},{2,0},{3,1},{4,6},{5,7},{6,4},{7,5},{8,10},{9,11},{10,... | collective-permute-start | bytes 1572872 | tf_op jit(solution)/shard_map/ppermute | solution.py:522
  23.0 27.9 %collective-permute-start = (bf16[256,1024]{1,0:T(8,128)(2,1)S(1)}, bf16[256,1024]{1,0:T(8,128)(2,1)S(1)}, u32[]{:S(2)}, u32[]{:S(2)}) collective-permute-start(bf16[256,1024]{1,0:T(8,128)(2,1)S(1)} %bitcast.53), channel_id=1, source_target_pairs={{0,1},{1,0},{2,3},{3,2},{4,5},{5,4},{6,7},{7,6},{8,9},{9,8},{10,11... | collective-permute-start | bytes 1572872 | tf_op jit(solution)/shard_map/ppermute | solution.py:522
  50.1 1.9 collective-permute-start.2
  58.1 58.6 %copy-start.3 = (bf16[1024,1024]{1,0:T(8,128)(2,1)S(1)}, bf16[1024,1024]{1,0:T(8,128)(2,1)}, u32[]{:S(2)}) copy-start(bf16[1024,1024]{1,0:T(8,128)(2,1)} %w_ref.4) | copy-start | bytes 6291460
  58.1 58.6 %copy-start.5 = (bf16[1,256,1024]{2,1,0:T(8,128)(2,1)S(1)}, bf16[1,256,1024]{2,1,0:T(8,128)(2,1)}, u32[]{:S(2)}) copy-start(bf16[1,256,1024]{2,1,0:T(8,128)(2,1)} %param.15) | copy-start | bytes 1572868
  58.1 58.6 %copy-start.22 = (s32[6]{0:T(128)S(1)}, s32[6]{0:T(128)}, u32[]{:S(2)}) copy-start(s32[6]{0:T(128)} %stack.27.ids) | copy-start | bytes 76
  58.1 58.6 %copy-start.24 = (f32[1024]{0:T(1024)S(1)}, f32[1024]{0:T(1024)}, u32[]{:S(2)}) copy-start(f32[1024]{0:T(1024)} %param.23) | copy-start | bytes 12292
  58.1 58.6 %copy-start.25 = (f32[1024]{0:T(1024)S(1)}, f32[1024]{0:T(1024)}, u32[]{:S(2)}) copy-start(f32[1024]{0:T(1024)} %param.22) | copy-start | bytes 12292
  120.4 22.8 %collective-permute-start.4 = (bf16[256,1024]{1,0:T(8,128)(2,1)}, bf16[256,1024]{1,0:T(8,128)(2,1)}, u32[]{:S(2)}, u32[]{:S(2)}) collective-permute-start(bf16[256,1024]{1,0:T(8,128)(2,1)} %get-tuple-element.134.a_ref), channel_id=1, source_target_pairs={{0,1},{1,0},{2,3},{3,2},{4,5},{5,4},{6,7},{7,6},{8,9},{9,8},{10,11... | collective-permute-start | bytes 1572872 | tf_op jit(solution)/shard_map/ppermute | solution.py:522
  120.4 24.8 %collective-permute-start.3 = (bf16[256,1024]{1,0:T(8,128)(2,1)}, bf16[256,1024]{1,0:T(8,128)(2,1)}, u32[]{:S(2)}, u32[]{:S(2)}) collective-permute-start(bf16[256,1024]{1,0:T(8,128)(2,1)} %get-tuple-element.132.n_ref), channel_id=1, source_target_pairs={{0,1},{1,0},{2,3},{3,2},{4,5},{5,4},{6,7},{7,6},{8,9},{9,8},{10,11... | collective-permute-start | bytes 1572872 | tf_op jit(solution)/shard_map/ppermute | solution.py:522
  129.0 13.7 %collective-permute-start.6 = (bf16[256,1024]{1,0:T(8,128)(2,1)}, bf16[256,1024]{1,0:T(8,128)(2,1)}, u32[]{:S(2)}, u32[]{:S(2)}) collective-permute-start(bf16[256,1024]{1,0:T(8,128)(2,1)} %get-tuple-element.121), channel_id=1, source_target_pairs={{0,2},{1,3},{2,0},{3,1},{4,6},{5,7},{6,4},{7,5},{8,10},{9,11},{10,... | collective-permute-start | bytes 1572872 | tf_op jit(solution)/shard_map/ppermute | solution.py:522
  133.3 12.0 %collective-permute-start.5 = (bf16[256,4096]{1,0:T(8,128)(2,1)S(1)}, bf16[256,4096]{1,0:T(8,128)(2,1)}, u32[]{:S(2)}, u32[]{:S(2)}) collective-permute-start(bf16[256,4096]{1,0:T(8,128)(2,1)S(1)} %get-tuple-element.136.ua_ref.ub_ref), channel_id=1, source_target_pairs={{0,1},{1,0},{2,3},{3,2},{4,5},{5,4},{6,7},{7,6},{8,9},{9,8},{10,11... | collective-permute-start | bytes 6291464 | tf_op jit(solution)/shard_map/ppermute | solution.py:522
  142.7 2.5 collective-permute-start.7
  143.1 14.8 %collective-permute-start.8 = (bf16[256,1024]{1,0:T(8,128)(2,1)}, bf16[256,1024]{1,0:T(8,128)(2,1)}, u32[]{:S(2)}, u32[]{:S(2)}) collective-permute-start(bf16[256,1024]{1,0:T(8,128)(2,1)} %get-tuple-element.126), channel_id=1, source_target_pairs={{0,1},{1,0},{2,3},{3,2},{4,5},{5,4},{6,7},{7,6},{8,9},{9,8},{10,11... | collective-permute-start | bytes 1572872 | tf_op jit(solution)/shard_map/ppermute | solution.py:522
  143.2 14.7 %collective-permute-start.9 = (bf16[256,1024]{1,0:T(8,128)(2,1)}, bf16[256,1024]{1,0:T(8,128)(2,1)}, u32[]{:S(2)}, u32[]{:S(2)}) collective-permute-start(bf16[256,1024]{1,0:T(8,128)(2,1)} %get-tuple-element.128), channel_id=1, source_target_pairs={{0,3},{1,2},{2,1},{3,0},{4,7},{5,6},{6,5},{7,4},{8,11},{9,10},{10,... | collective-permute-start | bytes 1572872 | tf_op jit(solution)/shard_map/ppermute | solution.py:522
  153.5 37.6 %collective-permute-start.10 = (bf16[4,64,2560]{2,1,0:T(8,128)(2,1)}, bf16[4,64,2560]{2,1,0:T(8,128)(2,1)}, u32[]{:S(2)}, u32[]{:S(2)}) collective-permute-start(bf16[4,64,2560]{2,1,0:T(8,128)(2,1)} %get-tuple-element.141), channel_id=1, source_target_pairs={{0,2},{1,3},{2,0},{3,1},{4,6},{5,7},{6,4},{7,5},{8,10},{9,11},{10,... | collective-permute-start | bytes 3932168 | tf_op jit(solution)/shard_map/ppermute | solution.py:522
  155.0 36.1 %collective-permute-start.11 = (bf16[512,1280]{1,0:T(8,128)(2,1)}, bf16[512,1280]{1,0:T(8,128)(2,1)}, u32[]{:S(2)}, u32[]{:S(2)}) collective-permute-start(bf16[512,1280]{1,0:T(8,128)(2,1)} %get-tuple-element.143), channel_id=1, source_target_pairs={{0,16},{16,0},{1,17},{17,1},{2,18},{18,2},{3,19},{19,3},{4,20},{20... | collective-permute-start | bytes 3932168 | tf_op jit(solution)/shard_map/ppermute | solution.py:526
  163.0 35.5 %all-to-all-start.2 = ((bf16[16,144,128]{2,1,0:T(8,128)(2,1)}), bf16[16,144,128]{2,1,0:T(8,128)(2,1)}, u32[]{:S(2)}, u32[]{:S(2)}) async-start(bf16[16,144,128]{2,1,0:T(8,128)(2,1)} %copy-done.8), calls=%async_computation.2 | async-start | bytes 1179648 | tf_op jit(solution)/shard_map/all_to_all | solution.py:518
  181.1 34.2 %collective-permute-start.14 = (bf16[2,256,1024]{2,1,0:T(8,128)(2,1)}, bf16[2,256,1024]{2,1,0:T(8,128)(2,1)}, u32[]{:S(2)}, u32[]{:S(2)}) collective-permute-start(bf16[2,256,1024]{2,1,0:T(8,128)(2,1)} %get-tuple-element.153), channel_id=1, source_target_pairs={{0,4},{1,5},{2,6},{3,7},{4,0},{5,1},{6,2},{7,3},{8,12},{9,13},{10,... | collective-permute-start | bytes 3145736 | tf_op jit(solution)/shard_map/ppermute | solution.py:522
  195.0 20.4 %collective-permute-start.12 = (bf16[4,64,1280]{2,1,0:T(8,128)(2,1)}, bf16[4,64,1280]{2,1,0:T(8,128)(2,1)S(1)}, u32[]{:S(2)}, u32[]{:S(2)}) collective-permute-start(bf16[4,64,1280]{2,1,0:T(8,128)(2,1)} %get-tuple-element.144), channel_id=1, source_target_pairs={{0,16},{16,0},{1,17},{17,1},{2,18},{18,2},{3,19},{19,3},{4,20},{20... | collective-permute-start | bytes 1966088 | tf_op jit(solution)/shard_map/ppermute | solution.py:526
  196.5 18.8 %collective-permute-start.13 = (bf16[4,64,1280]{2,1,0:T(8,128)(2,1)}, bf16[4,64,1280]{2,1,0:T(8,128)(2,1)}, u32[]{:S(2)}, u32[]{:S(2)}) collective-permute-start(bf16[4,64,1280]{2,1,0:T(8,128)(2,1)} %get-tuple-element.145), channel_id=1, source_target_pairs={{0,2},{1,3},{2,0},{3,1},{4,6},{5,7},{6,4},{7,5},{8,10},{9,11},{10,... | collective-permute-start | bytes 1966088 | tf_op jit(solution)/shard_map/ppermute | solution.py:522
  217.8 15.5 %collective-permute-start.16 = (bf16[2,256,512]{2,1,0:T(8,128)(2,1)S(1)}, bf16[2,256,512]{2,1,0:T(8,128)(2,1)S(1)}, u32[]{:S(2)}, u32[]{:S(2)}) collective-permute-start(bf16[2,256,512]{2,1,0:T(8,128)(2,1)S(1)} %get-tuple-element.172), channel_id=1, source_target_pairs={{0,16},{16,0},{1,17},{17,1},{2,18},{18,2},{3,19},{19,3},{4,20},{20... | collective-permute-start | bytes 1572872 | tf_op jit(solution)/shard_map/ppermute | solution.py:526
  218.4 15.0 %collective-permute-start.15 = (bf16[2,128,1280]{2,1,0:T(8,128)(2,1)S(1)}, bf16[2,128,1280]{2,1,0:T(8,128)(2,1)S(1)}, u32[]{:S(2)}, u32[]{:S(2)}) collective-permute-start(bf16[2,128,1280]{2,1,0:T(8,128)(2,1)S(1)} %get-tuple-element.171), channel_id=1, source_target_pairs={{0,4},{1,5},{2,6},{3,7},{4,0},{5,1},{6,2},{7,3},{8,12},{9,13},{10,... | collective-permute-start | bytes 1966088 | tf_op jit(solution)/shard_map/ppermute | solution.py:522
  234.2 21.4 %collective-permute-start.18 = (bf16[1,256,512]{2,1,0:T(8,128)(2,1)S(1)}, bf16[1,256,512]{2,1,0:T(8,128)(2,1)S(1)}, u32[]{:S(2)}, u32[]{:S(2)}) collective-permute-start(bf16[1,256,512]{2,1,0:T(8,128)(2,1)S(1)} %get-tuple-element.188), channel_id=1, source_target_pairs={{0,8},{1,9},{2,10},{3,11},{4,12},{5,13},{6,14},{7,15},{8,0},{9,1},... | collective-permute-start | bytes 786440 | tf_op jit(solution)/shard_map/ppermute | solution.py:522
  234.7 24.0 %collective-permute-start.17 = (bf16[1,128,1280]{2,1,0:T(8,128)(2,1)S(1)}, bf16[1,128,1280]{2,1,0:T(8,128)(2,1)S(1)}, u32[]{:S(2)}, u32[]{:S(2)}) collective-permute-start(bf16[1,128,1280]{2,1,0:T(8,128)(2,1)S(1)} %get-tuple-element.187), channel_id=1, source_target_pairs={{0,8},{1,9},{2,10},{3,11},{4,12},{5,13},{6,14},{7,15},{8,0},{9,1},... | collective-permute-start | bytes 983048 | tf_op jit(solution)/shard_map/ppermute | solution.py:522
  258.7 54.6 %all-to-all-start.3 = ((bf16[16,496,128]{2,1,0:T(8,128)(2,1)}), bf16[16,496,128]{2,1,0:T(8,128)(2,1)}, u32[]{:S(2)}, u32[]{:S(2)}) async-start(bf16[16,496,128]{2,1,0:T(8,128)(2,1)} %weight_message.1), calls=%async_computation.3 | async-start | bytes 4063232 | tf_op jit(solution)/shard_map/all_to_all | solution.py:518
  269.1 10.0 %collective-permute-start.21 = (bf16[512]{0:T(512)(128)(2,1)S(1)}, bf16[512]{0:T(512)(128)(2,1)S(1)}, u32[]{:S(2)}, u32[]{:S(2)}) collective-permute-start(bf16[512]{0:T(512)(128)(2,1)S(1)} %bitcast.72), channel_id=1, source_target_pairs={{0,16},{16,0},{1,17},{17,1},{2,18},{18,2},{3,19},{19,3},{4,20},{20... | collective-permute-start | bytes 3080 | tf_op jit(solution)/shard_map/ppermute | solution.py:513
  278.5 9.3 %collective-permute-start.22 = (bf16[256,512]{1,0:T(8,128)(2,1)S(1)}, bf16[256,512]{1,0:T(8,128)(2,1)S(1)}, u32[]{:S(2)}, u32[]{:S(2)}) collective-permute-start(bf16[256,512]{1,0:T(8,128)(2,1)S(1)} %bitcast.58), channel_id=1, source_target_pairs={{0,16},{16,0},{1,17},{17,1},{2,18},{18,2},{3,19},{19,3},{4,20},{20... | collective-permute-start | bytes 786440 | tf_op jit(solution)/shard_map/ppermute | solution.py:526
  280.4 13.4 %collective-permute-start.20 = (bf16[128,1280]{1,0:T(8,128)(2,1)S(1)}, bf16[128,1280]{1,0:T(8,128)(2,1)S(1)}, u32[]{:S(2)}, u32[]{:S(2)}) collective-permute-start(bf16[128,1280]{1,0:T(8,128)(2,1)S(1)} %bitcast.57), channel_id=1, source_target_pairs={{0,16},{16,0},{1,17},{17,1},{2,18},{18,2},{3,19},{19,3},{4,20},{20... | collective-permute-start | bytes 983048 | tf_op jit(solution)/shard_map/ppermute | solution.py:526
  314.3 14.4 %collective-permute-start.19 = (bf16[16,112,128]{2,1,0:T(8,128)(2,1)S(1)}, bf16[16,112,128]{2,1,0:T(8,128)(2,1)S(1)}, u32[]{:S(2)}, u32[]{:S(2)}) collective-permute-start(bf16[16,112,128]{2,1,0:T(8,128)(2,1)S(1)} %slice.44.one_ref), channel_id=1, source_target_pairs={{0,16},{16,0},{1,17},{17,1},{2,18},{18,2},{3,19},{19,3},{4,20},{20... | collective-permute-start | bytes 1376264 | tf_op jit(solution)/shard_map/ppermute | solution.py:526
  (41 other events, 496.1 us)
Sparse Core Ops, SparseCore 0:
  58.0 80.0 all-gather.1

commit v6 on v5

--- a/solution.py
+++ b/solution.py
@@ -83,15 +83,18 @@
             s=dotf(qb,ka_ref[pl.ds(pl.multiple_of(j*bk,bk),bk),:],NT)
             if masked:
                 key=j*bk+lax.broadcasted_iota(jnp.int32,(bq,bk),1)
-                s=jnp.where((key<=row)&(key>=first),s,NEGATIVE)
+                keep=key>=first if masked=="start" else key<=row
+                s=jnp.where(keep&(key>=first) if masked=="both" else keep,s,NEGATIVE)
             s_ref[j]=s
             for c in range(bk//128):
                 top=jnp.maximum(top,s[:,c*128:(c+1)*128])
             return top
         top=jnp.full((bq,128),NEGATIVE,F32)
-        top=lax.fori_loop(lo,u0,lambda j,t:score(j,t,True),top)
-        top=lax.fori_loop(u0,u1,lambda j,t:score(j,t,False),top)
-        top=lax.fori_loop(u1,hi,lambda j,t:score(j,t,True),top)
+        below=(a+1)//bk
+        top=lax.fori_loop(lo,jnp.minimum(u0,below),lambda j,t:score(j,t,"start"),top)
+        top=lax.fori_loop(u0,u1,lambda j,t:score(j,t,""),top)
+        top=lax.fori_loop(jnp.maximum(below,lo),u0,lambda j,t:score(j,t,"both"),top)
+        top=lax.fori_loop(u1,hi,lambda j,t:score(j,t,"order"),top)
         peak=jnp.max(top,axis=1,keepdims=True)
         def gather(j,acc):
             p=jnp.exp2(s_ref[j]-peak).astype(BF)

time: 346 us -> 345 us (level)
  transfers between devices with their start and end apart: 27 -> 27, of which waited for: 9 -> 8; matrix products, arithmetic and copies ran while one was open for 11% -> 11% of each run, Pallas kernels for 33% -> 33%
where the time goes in v6:
time: 345 us; the launch traced here: 338 us
  Pallas kernels  124 us (36%)
  waiting for transfers between devices  64.3 us (19%)
  starting transfers between devices  42.4 us (12%)
  blocking collectives  32.5 us (9%)
  local copies, waits for them, and re-layouts  24.8 us (7%)
  matrix products  23.8 us (7%)
  between operations  15.2 us (4%)
  other arithmetic  11.2 us (3%)
    pallas_call x14, Pallas kernels, run_kernel(): pl.pallas_call(kernel, grid_spec=pltpu.PrefetchScalarGridSpec(num_scalar_...  58.7 us
    pallas_call x3, Pallas kernels, attend_back(): pl.pallas_call(functools.partial(bwd_kernel, bq=bq, bk=bk, segs=segs, beg...  41.6 us
    all_to_all x1, blocking collectives, exchange(): return lax.all_to_all(value, 'seq', 0, 0, tiled=True)  32.5 us
    ppermute x16, waiting for transfers between devices, swap(): lax.ppermute(value, 'seq', [(i, i ^ bit) for i in range(lax.axis_size('se...  31.9 us
    dot_general x4, matrix products, dotf(): return lax.dot_general(a, b, dims, preferred_element_type=F32)  23.8 us
    pallas_call x1, Pallas kernels, attend(): pl.pallas_call(functools.partial(fwd_kernel, bq=bq, bk=bk, segs=segs, gro...  23.8 us
    all_to_all x3, waiting for transfers between devices, exchange(): return lax.all_to_all(value, 'seq', 0, 0, tiled=True)  21.7 us
    all_to_all x3, starting transfers between devices, exchange(): return lax.all_to_all(value, 'seq', 0, 0, tiled=True)  21 us
  transfers between devices with their start and end apart: 27, of which 8 were waited for; matrix products, arithmetic and copies ran while one was open for 11% of the time, Pallas kernels for 33%

profile of v6, /device:TPU:16, one launch (start us, length us, event | category | flops | bytes accessed | tf_op | source)
XLA Modules:
  0.0 338.3 jit_solution(2629967380919309478)
XLA Ops:
  7.9 7.4 %project.1 = (bf16[16,384,128]{2,1,0:T(8,128)(2,1)}, bf16[256,1024]{1,0:T(8,128)(2,1)}) custom-call(s32[6]{0:T(128)} %stack.27.ids, bf16[256,1024]{1,0:T(8,128)(2,1)} %bitcast.49, f32[1,1024]{1,0:T(1,128)} %bitcast.59, f32[1,1024]{1,0:T(1,128)} %bitcast.68, bf16[1024,3072]{1,0:T(8,128)(2,1)} %w_ref.5, bf16[1024,3072]{1,0:T(8,128)(2,1)} %w_ref.5, ...), custom_call_target="tpu_custom_call" | custom-call | flops 1610612736 | bytes 21508096 | tf_op jit(solution)/shard_map/project/pallas_call | solution.py:231
  15.3 6.2 %all-to-all-start = ((bf16[16,384,128]{2,1,0:T(8,128)(2,1)}), bf16[16,384,128]{2,1,0:T(8,128)(2,1)S(1)}, u32[]{:S(2)}, u32[]{:S(2)}) async-start(bf16[16,384,128]{2,1,0:T(8,128)(2,1)} %get-tuple-element.110), calls=%async_computation | async-start | bytes 3145728 | tf_op jit(solution)/shard_map/all_to_all | solution.py:521
  23.1 27.1 %collective-permute-done.1.refs_6_ = bf16[256,1024]{1,0:T(8,128)(2,1)S(1)} collective-permute-done((bf16[256,1024]{1,0:T(8,128)(2,1)S(1)}, bf16[256,1024]{1,0:T(8,128)(2,1)S(1)}, u32[]{:S(2)}, u32[]{:S(2)}) %collective-permute-start.1) | collective-permute-done | bytes 524320 | tf_op jit(solution)/shard_map/ppermute | solution.py:525
  52.8 5.1 %all-to-all-done.x_ref.refs_0_ = bf16[16,384,128]{2,1,0:T(8,128)(2,1)S(1)} async-done(((bf16[16,384,128]{2,1,0:T(8,128)(2,1)}), bf16[16,384,128]{2,1,0:T(8,128)(2,1)S(1)}, u32[]{:S(2)}, u32[]{:S(2)}) %all-to-all-start) | async-done | bytes 1572896 | tf_op jit(solution)/shard_map/all_to_all | solution.py:521
  58.1 23.8 %attend.1 = (bf16[16,128,128]{2,1,0:T(8,128)(2,1)S(1)}, bf16[4096,128]{1,0:T(8,128)(2,1)S(1)}) custom-call(s32[4]{0:T(128)S(1)} %bitcast_subtract_fusion.starts, s32[1]{0:T(128)} %constant.96.clone.1.part, bf16[16,384,128]{2,1,0:T(8,128)(2,1)S(1)} %all-to-all-done.x_ref.refs_0_), custom_call_target="tpu_custom_call" | custom-call | flops 8589934592 | bytes 6553600 | tf_op jit(solution)/shard_map/attend/pallas_call | solution.py:117
  82.9 32.5 %all_to_all.20.got_ref = bf16[16,128,128]{2,1,0:T(8,128)(2,1)S(1)} all-to-all(bf16[16,128,128]{2,1,0:T(8,128)(2,1)S(1)} %get-tuple-element.113.refs_3_), channel_id=1, replica_groups=mesh['row'=2,'seq'=16] {'seq'}, dimensions={0} | all-to-all | bytes 1048576 | tf_op jit(solution)/shard_map/all_to_all | solution.py:521
  115.5 3.6 %mix.1 = (bf16[256,1024]{1,0:T(8,128)(2,1)}, bf16[256,1024]{1,0:T(8,128)(2,1)}, f32[256,1024]{1,0:T(8,128)S(1)}) custom-call(s32[6]{0:T(128)S(1)} %copy-done.22, bf16[16,128,128]{2,1,0:T(8,128)(2,1)S(1)} %all_to_all.20.got_ref, bf16[1024,1024]{1,0:T(8,128)(2,1)S(1)} %copy-done.3, bf16[256,1024]{1,0:T(8,128)(2,1)S(1)} %bitcast.50, f32[1,1024]{1,0:T(1,128)S(1)} %bitcast.63, ...), custom_call_target="tpu_custom_call" | custom-call | flops 536870912 | bytes 4724736 | tf_op jit(solution)/shard_map/mix/pallas_call | solution.py:231
  119.7 6.3 %multiply_convert_fusion = (bf16[256,4096]{1,0:T(8,128)(2,1)S(1)}, f32[256,4096]{1,0:T(8,128)S(1)}) fusion(f32[4096]{0:T(1024)S(1)} %copy-done.37, bf16[256,1024]{1,0:T(8,128)(2,1)} %get-tuple-element.132.n_ref, bf16[1024,4096]{1,0:T(8,128)(2,1)} %param.25), kind=kOutput, calls=%fused_computation.8 | convolution fusion | flops 2153775104 | bytes 15220736 | tf_op jit(solution)/shard_map/dot_general | solution.py:19
  128.0 4.2 %fusion.12 = (bf16[4096]{0:T(1024)(128)(2,1)S(1)}, bf16[256,4096]{1,0:T(8,128)(2,1)S(1)}) fusion(f32[256,4096]{1,0:T(8,128)S(1)} %get-tuple-element.221, bf16[256,1024]{1,0:T(8,128)(2,1)S(1)} %bitcast.54, bf16[4096,1024]{1,0:T(8,128)(2,1)S(1)} %bitcast.75), kind=kOutput, calls=%fused_computation.41 | convolution fusion | flops 2159013888 | bytes 15212544 | tf_op jit(solution)/shard_map/dot_general | solution.py:19
  132.7 6.2 %multiply_reduce_fusion = (bf16[1024]{0:T(1024)(128)(2,1)S(1)}, f32[256]{0:T(256)S(1)}, f32[256]{0:T(256)S(1)}, bf16[1024]{0:T(1024)(128)(2,1)S(1)}, f32[256,1024]{1,0:T(8,128)S(1)}) fusion(f32[256,1024]{1,0:T(8,128)S(1)} %get-tuple-element.114, f32[256]{0:T(256)S(1)} %add_rsqrt_fusion, f32[256]{0:T(256)S(1)} %broadcast_multiply_fusion.1, ...), kind=kOutput, calls=%fused_computation.15 | convolution fusion | flops 2149840384 | bytes 12595200 | tf_op jit(solution)/shard_map/dot_general | solution.py:19
  139.0 2.6 fusion.9
  144.1 8.2 %grads_up.2 = (bf16[4,64,2560]{2,1,0:T(8,128)(2,1)}, bf16[512,1280]{1,0:T(8,128)(2,1)}) custom-call(s32[6]{0:T(128)S(1)} %copy-done.22, bf16[256,1024]{1,0:T(8,128)(2,1)} %get-tuple-element.132.n_ref, bf16[256,1024]{1,0:T(8,128)(2,1)} %collective-permute-done.3.no_ref, bf16[256,1024]{1,0:T(8,128)(2,1)} %get-tuple-element.134.a_ref, ...), custom_call_target="tpu_custom_call" | custom-call | flops 1342177280 | bytes 15204352 | tf_op jit(solution)/shard_map/grads_up/pallas_call | solution.py:231
  158.7 2.2 grad_pack.1
  161.8 6.2 %all-to-all-start.2 = ((bf16[16,144,128]{2,1,0:T(8,128)(2,1)}), bf16[16,144,128]{2,1,0:T(8,128)(2,1)}, u32[]{:S(2)}, u32[]{:S(2)}) async-start(bf16[16,144,128]{2,1,0:T(8,128)(2,1)} %copy-done.8), calls=%async_computation.2 | async-start | bytes 1179648 | tf_op jit(solution)/shard_map/all_to_all | solution.py:521
  173.8 6.1 %grads_down.1 = (bf16[2,256,1024]{2,1,0:T(8,128)(2,1)}, bf16[2,256,1024]{2,1,0:T(8,128)(2,1)S(1)}) custom-call(s32[6]{0:T(128)S(1)} %copy-done.22, bf16[256,4096]{1,0:T(8,128)(2,1)S(1)} %copy-done.11, bf16[256,1024]{1,0:T(8,128)(2,1)} %collective-permute-done.8.refs_1_, bf16[256,1024]{1,0:T(8,128)(2,1)} %collective-permute-done.6.refs_2_, ...), custom_call_target="tpu_custom_call" | custom-call | flops 2147483648 | bytes 7864320 | tf_op jit(solution)/shard_map/grads_down/pallas_call | solution.py:231
  181.4 7.1 %grads_up.3 = (bf16[4,64,2560]{2,1,0:T(8,128)(2,1)S(1)}, bf16[512,1280]{1,0:T(8,128)(2,1)S(1)}) custom-call(s32[6]{0:T(128)S(1)} %copy-done.22, bf16[256,1024]{1,0:T(8,128)(2,1)} %get-tuple-element.132.n_ref, bf16[256,1024]{1,0:T(8,128)(2,1)} %collective-permute-done.3.no_ref, bf16[256,1024]{1,0:T(8,128)(2,1)} %get-tuple-element.134.a_ref, ...), custom_call_target="tpu_custom_call" | custom-call | flops 1342177280 | bytes 15204352 | tf_op jit(solution)/shard_map/grads_up/pallas_call | solution.py:231
  190.1 3.8 %add_one.1 = (bf16[4,64,1280]{2,1,0:T(8,128)(2,1)}, bf16[4,64,1280]{2,1,0:T(8,128)(2,1)S(1)}, bf16[4,64,1280]{2,1,0:T(8,128)(2,1)}, bf16[4,64,1280]{2,1,0:T(8,128)(2,1)S(1)}) custom-call(s32[6]{0:T(128)S(1)} %copy-done.22, bf16[4,64,2560]{2,1,0:T(8,128)(2,1)S(1)} %get-tuple-element.140.refs_0_, bf16[4,64,2560]{2,1,0:T(8,128)(2,1)} %collective-permute-done.10.refs_1_, ...), custom_call_target="tpu_custom_call" | custom-call | flops 1310720 | bytes 7864320 | tf_op jit(solution)/shard_map/add_one/pallas_call | solution.py:231
  199.7 14.3 %attend_back.3 = (bf16[4096,128]{1,0:T(8,128)(2,1)S(1)}, f32[4,64,1024]{2,1,0:T(8,128)S(1)}, bf16[1024,128]{1,0:T(8,128)(2,1)S(1)}) custom-call(s32[4]{0:T(128)S(1)} %bitcast_subtract_fusion.starts, bf16[16,384,128]{2,1,0:T(8,128)(2,1)S(1)} %copy-done.17, bf16[4096,128]{1,0:T(8,128)(2,1)S(1)} %copy-done.34, bf16[16,144,128]{2,1,0:T(8,128)(2,1)} %all-to-all-done.2.refs_2_, ...), custom_call_target="tpu_custom_call" | custom-call | flops 5368709120 | bytes 8192000 | tf_op jit(solution)/shard_map/attend_back/pallas_call | solution.py:213
  214.1 2.5 add_two.1
  217.3 14.9 %attend_back.4 = (f32[4,64,1024]{2,1,0:T(8,128)S(1)}, bf16[1024,128]{1,0:T(8,128)(2,1)S(1)}) custom-call(s32[4]{0:T(128)S(1)} %bitcast_subtract_fusion.starts, bf16[16,384,128]{2,1,0:T(8,128)(2,1)S(1)} %copy-done.17, bf16[4096,128]{1,0:T(8,128)(2,1)S(1)} %copy-done.35, bf16[4096,128]{1,0:T(8,128)(2,1)S(1)} %get-tuple-element.190.refs_2_, ...), custom_call_target="tpu_custom_call" | custom-call | flops 5368709120 | bytes 8192000 | tf_op jit(solution)/shard_map/attend_back/pallas_call | solution.py:213
  233.4 2.7 collective-permute-start.17
  236.1 12.4 %attend_back.5.dx_ref = bf16[16,384,128]{2,1,0:T(8,128)(2,1)S(1)} custom-call(s32[4]{0:T(128)S(1)} %bitcast_subtract_fusion.starts, bf16[16,384,128]{2,1,0:T(8,128)(2,1)S(1)} %copy-done.17, bf16[4096,128]{1,0:T(8,128)(2,1)S(1)} %copy-done.35, bf16[4096,128]{1,0:T(8,128)(2,1)S(1)} %get-tuple-element.190.refs_2_, ...), custom_call_target="tpu_custom_call" | custom-call | flops 10737418240 | bytes 8192000 | tf_op jit(solution)/shard_map/attend_back/pallas_call | solution.py:213
  248.6 5.8 %weight_message.1 = bf16[16,496,128]{2,1,0:T(8,128)(2,1)} custom-call(s32[6]{0:T(128)S(1)} %copy-done.22, bf16[4096,1024]{1,0:T(8,128)(2,1)S(1)} %bitcast.48, bf16[16,384,128]{2,1,0:T(8,128)(2,1)S(1)} %attend_back.5.dx_ref), custom_call_target="tpu_custom_call" | custom-call | flops 1610612736 | bytes 11993088 | tf_op jit(solution)/shard_map/weight_message/pallas_call | solution.py:231
  254.4 2.9 collective-permute-done.17.refs_1_
  257.3 8.6 %all-to-all-start.3 = ((bf16[16,496,128]{2,1,0:T(8,128)(2,1)}), bf16[16,496,128]{2,1,0:T(8,128)(2,1)}, u32[]{:S(2)}, u32[]{:S(2)}) async-start(bf16[16,496,128]{2,1,0:T(8,128)(2,1)} %weight_message.1), calls=%async_computation.3 | async-start | bytes 4063232 | tf_op jit(solution)/shard_map/all_to_all | solution.py:521
  269.4 7.1 %fusion.7 = bf16[1,256,1024]{2,1,0:T(8,128)(2,1)} fusion(f32[256,1024]{1,0:T(8,128)S(1)} %copy-done.2, bf16[256,4096]{1,0:T(8,128)(2,1)} %copy-done.10, bf16[4096,1024]{1,0:T(8,128)(2,1)} %param.27, f32[1024]{0:T(1024)S(1)} %copy-done.38), kind=kOutput, calls=%fused_computation.13 | convolution fusion | flops 2148270080 | bytes 12062720 | tf_op jit(solution)/shard_map/dot_general | solution.py:19
  280.6 5.9 %collective-permute-done.22 = bf16[256,512]{1,0:T(8,128)(2,1)S(1)} collective-permute-done((bf16[256,512]{1,0:T(8,128)(2,1)S(1)}, bf16[256,512]{1,0:T(8,128)(2,1)S(1)}, u32[]{:S(2)}, u32[]{:S(2)}) %collective-permute-start.22) | collective-permute-done | bytes 262176 | tf_op jit(solution)/shard_map/ppermute | solution.py:529
  287.6 4.8 %collective-permute-done.20 = bf16[128,1280]{1,0:T(8,128)(2,1)S(1)} collective-permute-done((bf16[128,1280]{1,0:T(8,128)(2,1)S(1)}, bf16[128,1280]{1,0:T(8,128)(2,1)S(1)}, u32[]{:S(2)}, u32[]{:S(2)}) %collective-permute-start.20) | collective-permute-done | bytes 327712 | tf_op jit(solution)/shard_map/ppermute | solution.py:529
  295.5 16.6 %all-to-all-done.3.got_ref = bf16[16,496,128]{2,1,0:T(8,128)(2,1)} async-done(((bf16[16,496,128]{2,1,0:T(8,128)(2,1)}), bf16[16,496,128]{2,1,0:T(8,128)(2,1)}, u32[]{:S(2)}, u32[]{:S(2)}) %all-to-all-start.3) | async-done | bytes 2031648 | tf_op jit(solution)/shard_map/all_to_all | solution.py:521
  314.6 2.2 pad_maximum_fusion
  316.8 2.8 copy-done
  320.8 6.6 %input_grad.1 = bf16[256,1024]{1,0:T(8,128)(2,1)} custom-call(s32[6]{0:T(128)S(1)} %copy-done.22, bf16[16,496,128]{2,1,0:T(8,128)(2,1)} %all-to-all-done.3.got_ref, bf16[1024,3072]{1,0:T(8,128)(2,1)S(1)} %copy-done, bf16[1024,3072]{1,0:T(8,128)(2,1)S(1)} %copy-done, bf16[1024,3072]{1,0:T(8,128)(2,1)S(1)} %copy-done, bf16[256,1024]{1,0:T(8,128)(2,1)S(1)} %bitcast.51, ...), custom_call_target="tpu_custom_call" | custom-call | flops 1610612736 | bytes 22480896 | tf_op jit(solution)/shard_map/input_grad/pallas_call | solution.py:231
  (184 shorter events, 54.3 us)
Async XLA Ops:
  15.3 42.6 %all-to-all-start = ((bf16[16,384,128]{2,1,0:T(8,128)(2,1)}), bf16[16,384,128]{2,1,0:T(8,128)(2,1)S(1)}, u32[]{:S(2)}, u32[]{:S(2)}) async-start(bf16[16,384,128]{2,1,0:T(8,128)(2,1)} %get-tuple-element.110), calls=%async_computation | async-start | bytes 3145728 | tf_op jit(solution)/shard_map/all_to_all | solution.py:521
  21.5 140.4 %all-gather.2.cloned.1.call-start = ((), (), s32[]{:S(2)}) async-start(), calls=%async_computation.4 | async-start | bytes 8912896 | tf_op jit(solution)/shard_map/all_gather | solution.py:600
  21.5 28.6 %collective-permute-start.1 = (bf16[256,1024]{1,0:T(8,128)(2,1)S(1)}, bf16[256,1024]{1,0:T(8,128)(2,1)S(1)}, u32[]{:S(2)}, u32[]{:S(2)}) collective-permute-start(bf16[256,1024]{1,0:T(8,128)(2,1)S(1)} %bitcast.52), channel_id=1, source_target_pairs={{0,2},{1,3},{2,0},{3,1},{4,6},{5,7},{6,4},{7,5},{8,10},{9,11},{10,... | collective-permute-start | bytes 1572872 | tf_op jit(solution)/shard_map/ppermute | solution.py:525
  23.0 27.9 %collective-permute-start = (bf16[256,1024]{1,0:T(8,128)(2,1)S(1)}, bf16[256,1024]{1,0:T(8,128)(2,1)S(1)}, u32[]{:S(2)}, u32[]{:S(2)}) collective-permute-start(bf16[256,1024]{1,0:T(8,128)(2,1)S(1)} %bitcast.53), channel_id=1, source_target_pairs={{0,1},{1,0},{2,3},{3,2},{4,5},{5,4},{6,7},{7,6},{8,9},{9,8},{10,11... | collective-permute-start | bytes 1572872 | tf_op jit(solution)/shard_map/ppermute | solution.py:525
  50.1 1.9 collective-permute-start.2
  58.1 57.3 %copy-start.3 = (bf16[1024,1024]{1,0:T(8,128)(2,1)S(1)}, bf16[1024,1024]{1,0:T(8,128)(2,1)}, u32[]{:S(2)}) copy-start(bf16[1024,1024]{1,0:T(8,128)(2,1)} %w_ref.4) | copy-start | bytes 6291460
  58.1 57.3 %copy-start.5 = (bf16[1,256,1024]{2,1,0:T(8,128)(2,1)S(1)}, bf16[1,256,1024]{2,1,0:T(8,128)(2,1)}, u32[]{:S(2)}) copy-start(bf16[1,256,1024]{2,1,0:T(8,128)(2,1)} %param.15) | copy-start | bytes 1572868
  58.1 57.4 %copy-start.22 = (s32[6]{0:T(128)S(1)}, s32[6]{0:T(128)}, u32[]{:S(2)}) copy-start(s32[6]{0:T(128)} %stack.27.ids) | copy-start | bytes 76
  58.1 57.3 %copy-start.24 = (f32[1024]{0:T(1024)S(1)}, f32[1024]{0:T(1024)}, u32[]{:S(2)}) copy-start(f32[1024]{0:T(1024)} %param.23) | copy-start | bytes 12292
  58.1 57.3 %copy-start.25 = (f32[1024]{0:T(1024)S(1)}, f32[1024]{0:T(1024)}, u32[]{:S(2)}) copy-start(f32[1024]{0:T(1024)} %param.22) | copy-start | bytes 12292
  119.1 23.0 %collective-permute-start.4 = (bf16[256,1024]{1,0:T(8,128)(2,1)}, bf16[256,1024]{1,0:T(8,128)(2,1)}, u32[]{:S(2)}, u32[]{:S(2)}) collective-permute-start(bf16[256,1024]{1,0:T(8,128)(2,1)} %get-tuple-element.134.a_ref), channel_id=1, source_target_pairs={{0,1},{1,0},{2,3},{3,2},{4,5},{5,4},{6,7},{7,6},{8,9},{9,8},{10,11... | collective-permute-start | bytes 1572872 | tf_op jit(solution)/shard_map/ppermute | solution.py:525
  119.2 24.9 %collective-permute-start.3 = (bf16[256,1024]{1,0:T(8,128)(2,1)}, bf16[256,1024]{1,0:T(8,128)(2,1)}, u32[]{:S(2)}, u32[]{:S(2)}) collective-permute-start(bf16[256,1024]{1,0:T(8,128)(2,1)} %get-tuple-element.132.n_ref), channel_id=1, source_target_pairs={{0,1},{1,0},{2,3},{3,2},{4,5},{5,4},{6,7},{7,6},{8,9},{9,8},{10,11... | collective-permute-start | bytes 1572872 | tf_op jit(solution)/shard_map/ppermute | solution.py:525
  128.0 13.7 %collective-permute-start.6 = (bf16[256,1024]{1,0:T(8,128)(2,1)}, bf16[256,1024]{1,0:T(8,128)(2,1)}, u32[]{:S(2)}, u32[]{:S(2)}) collective-permute-start(bf16[256,1024]{1,0:T(8,128)(2,1)} %get-tuple-element.121), channel_id=1, source_target_pairs={{0,2},{1,3},{2,0},{3,1},{4,6},{5,7},{6,4},{7,5},{8,10},{9,11},{10,... | collective-permute-start | bytes 1572872 | tf_op jit(solution)/shard_map/ppermute | solution.py:525
  132.2 11.9 %collective-permute-start.5 = (bf16[256,4096]{1,0:T(8,128)(2,1)S(1)}, bf16[256,4096]{1,0:T(8,128)(2,1)}, u32[]{:S(2)}, u32[]{:S(2)}) collective-permute-start(bf16[256,4096]{1,0:T(8,128)(2,1)S(1)} %get-tuple-element.136.ua_ref.ub_ref), channel_id=1, source_target_pairs={{0,1},{1,0},{2,3},{3,2},{4,5},{5,4},{6,7},{7,6},{8,9},{9,8},{10,11... | collective-permute-start | bytes 6291464 | tf_op jit(solution)/shard_map/ppermute | solution.py:525
  141.6 2.5 collective-permute-start.7
  142.0 14.8 %collective-permute-start.8 = (bf16[256,1024]{1,0:T(8,128)(2,1)}, bf16[256,1024]{1,0:T(8,128)(2,1)}, u32[]{:S(2)}, u32[]{:S(2)}) collective-permute-start(bf16[256,1024]{1,0:T(8,128)(2,1)} %get-tuple-element.126), channel_id=1, source_target_pairs={{0,1},{1,0},{2,3},{3,2},{4,5},{5,4},{6,7},{7,6},{8,9},{9,8},{10,11... | collective-permute-start | bytes 1572872 | tf_op jit(solution)/shard_map/ppermute | solution.py:525
  142.1 14.7 %collective-permute-start.9 = (bf16[256,1024]{1,0:T(8,128)(2,1)}, bf16[256,1024]{1,0:T(8,128)(2,1)}, u32[]{:S(2)}, u32[]{:S(2)}) collective-permute-start(bf16[256,1024]{1,0:T(8,128)(2,1)} %get-tuple-element.128), channel_id=1, source_target_pairs={{0,3},{1,2},{2,1},{3,0},{4,7},{5,6},{6,5},{7,4},{8,11},{9,10},{10,... | collective-permute-start | bytes 1572872 | tf_op jit(solution)/shard_map/ppermute | solution.py:525
  152.4 37.7 %collective-permute-start.10 = (bf16[4,64,2560]{2,1,0:T(8,128)(2,1)}, bf16[4,64,2560]{2,1,0:T(8,128)(2,1)}, u32[]{:S(2)}, u32[]{:S(2)}) collective-permute-start(bf16[4,64,2560]{2,1,0:T(8,128)(2,1)} %get-tuple-element.141), channel_id=1, source_target_pairs={{0,2},{1,3},{2,0},{3,1},{4,6},{5,7},{6,4},{7,5},{8,10},{9,11},{10,... | collective-permute-start | bytes 3932168 | tf_op jit(solution)/shard_map/ppermute | solution.py:525
  153.8 36.3 %collective-permute-start.11 = (bf16[512,1280]{1,0:T(8,128)(2,1)}, bf16[512,1280]{1,0:T(8,128)(2,1)}, u32[]{:S(2)}, u32[]{:S(2)}) collective-permute-start(bf16[512,1280]{1,0:T(8,128)(2,1)} %get-tuple-element.143), channel_id=1, source_target_pairs={{0,16},{16,0},{1,17},{17,1},{2,18},{18,2},{3,19},{19,3},{4,20},{20... | collective-permute-start | bytes 3932168 | tf_op jit(solution)/shard_map/ppermute | solution.py:529
  161.8 35.6 %all-to-all-start.2 = ((bf16[16,144,128]{2,1,0:T(8,128)(2,1)}), bf16[16,144,128]{2,1,0:T(8,128)(2,1)}, u32[]{:S(2)}, u32[]{:S(2)}) async-start(bf16[16,144,128]{2,1,0:T(8,128)(2,1)} %copy-done.8), calls=%async_computation.2 | async-start | bytes 1179648 | tf_op jit(solution)/shard_map/all_to_all | solution.py:521
  179.9 34.1 %collective-permute-start.14 = (bf16[2,256,1024]{2,1,0:T(8,128)(2,1)}, bf16[2,256,1024]{2,1,0:T(8,128)(2,1)}, u32[]{:S(2)}, u32[]{:S(2)}) collective-permute-start(bf16[2,256,1024]{2,1,0:T(8,128)(2,1)} %get-tuple-element.153), channel_id=1, source_target_pairs={{0,4},{1,5},{2,6},{3,7},{4,0},{5,1},{6,2},{7,3},{8,12},{9,13},{10,... | collective-permute-start | bytes 3145736 | tf_op jit(solution)/shard_map/ppermute | solution.py:525
  193.9 20.2 %collective-permute-start.12 = (bf16[4,64,1280]{2,1,0:T(8,128)(2,1)}, bf16[4,64,1280]{2,1,0:T(8,128)(2,1)S(1)}, u32[]{:S(2)}, u32[]{:S(2)}) collective-permute-start(bf16[4,64,1280]{2,1,0:T(8,128)(2,1)} %get-tuple-element.144), channel_id=1, source_target_pairs={{0,16},{16,0},{1,17},{17,1},{2,18},{18,2},{3,19},{19,3},{4,20},{20... | collective-permute-start | bytes 1966088 | tf_op jit(solution)/shard_map/ppermute | solution.py:529
  195.5 18.5 %collective-permute-start.13 = (bf16[4,64,1280]{2,1,0:T(8,128)(2,1)}, bf16[4,64,1280]{2,1,0:T(8,128)(2,1)}, u32[]{:S(2)}, u32[]{:S(2)}) collective-permute-start(bf16[4,64,1280]{2,1,0:T(8,128)(2,1)} %get-tuple-element.145), channel_id=1, source_target_pairs={{0,2},{1,3},{2,0},{3,1},{4,6},{5,7},{6,4},{7,5},{8,10},{9,11},{10,... | collective-permute-start | bytes 1966088 | tf_op jit(solution)/shard_map/ppermute | solution.py:525
  216.6 15.6 %collective-permute-start.16 = (bf16[2,256,512]{2,1,0:T(8,128)(2,1)S(1)}, bf16[2,256,512]{2,1,0:T(8,128)(2,1)S(1)}, u32[]{:S(2)}, u32[]{:S(2)}) collective-permute-start(bf16[2,256,512]{2,1,0:T(8,128)(2,1)S(1)} %get-tuple-element.172), channel_id=1, source_target_pairs={{0,16},{16,0},{1,17},{17,1},{2,18},{18,2},{3,19},{19,3},{4,20},{20... | collective-permute-start | bytes 1572872 | tf_op jit(solution)/shard_map/ppermute | solution.py:529
  217.3 15.0 %collective-permute-start.15 = (bf16[2,128,1280]{2,1,0:T(8,128)(2,1)S(1)}, bf16[2,128,1280]{2,1,0:T(8,128)(2,1)S(1)}, u32[]{:S(2)}, u32[]{:S(2)}) collective-permute-start(bf16[2,128,1280]{2,1,0:T(8,128)(2,1)S(1)} %get-tuple-element.171), channel_id=1, source_target_pairs={{0,4},{1,5},{2,6},{3,7},{4,0},{5,1},{6,2},{7,3},{8,12},{9,13},{10,... | collective-permute-start | bytes 1966088 | tf_op jit(solution)/shard_map/ppermute | solution.py:525
  233.1 21.3 %collective-permute-start.18 = (bf16[1,256,512]{2,1,0:T(8,128)(2,1)S(1)}, bf16[1,256,512]{2,1,0:T(8,128)(2,1)S(1)}, u32[]{:S(2)}, u32[]{:S(2)}) collective-permute-start(bf16[1,256,512]{2,1,0:T(8,128)(2,1)S(1)} %get-tuple-element.188), channel_id=1, source_target_pairs={{0,8},{1,9},{2,10},{3,11},{4,12},{5,13},{6,14},{7,15},{8,0},{9,1},... | collective-permute-start | bytes 786440 | tf_op jit(solution)/shard_map/ppermute | solution.py:525
  233.4 23.9 %collective-permute-start.17 = (bf16[1,128,1280]{2,1,0:T(8,128)(2,1)S(1)}, bf16[1,128,1280]{2,1,0:T(8,128)(2,1)S(1)}, u32[]{:S(2)}, u32[]{:S(2)}) collective-permute-start(bf16[1,128,1280]{2,1,0:T(8,128)(2,1)S(1)} %get-tuple-element.187), channel_id=1, source_target_pairs={{0,8},{1,9},{2,10},{3,11},{4,12},{5,13},{6,14},{7,15},{8,0},{9,1},... | collective-permute-start | bytes 983048 | tf_op jit(solution)/shard_map/ppermute | solution.py:525
  257.3 54.8 %all-to-all-start.3 = ((bf16[16,496,128]{2,1,0:T(8,128)(2,1)}), bf16[16,496,128]{2,1,0:T(8,128)(2,1)}, u32[]{:S(2)}, u32[]{:S(2)}) async-start(bf16[16,496,128]{2,1,0:T(8,128)(2,1)} %weight_message.1), calls=%async_computation.3 | async-start | bytes 4063232 | tf_op jit(solution)/shard_map/all_to_all | solution.py:521
  268.0 10.0 %collective-permute-start.21 = (bf16[512]{0:T(512)(128)(2,1)S(1)}, bf16[512]{0:T(512)(128)(2,1)S(1)}, u32[]{:S(2)}, u32[]{:S(2)}) collective-permute-start(bf16[512]{0:T(512)(128)(2,1)S(1)} %bitcast.72), channel_id=1, source_target_pairs={{0,16},{16,0},{1,17},{17,1},{2,18},{18,2},{3,19},{19,3},{4,20},{20... | collective-permute-start | bytes 3080 | tf_op jit(solution)/shard_map/ppermute | solution.py:516
  277.2 9.3 %collective-permute-start.22 = (bf16[256,512]{1,0:T(8,128)(2,1)S(1)}, bf16[256,512]{1,0:T(8,128)(2,1)S(1)}, u32[]{:S(2)}, u32[]{:S(2)}) collective-permute-start(bf16[256,512]{1,0:T(8,128)(2,1)S(1)} %bitcast.58), channel_id=1, source_target_pairs={{0,16},{16,0},{1,17},{17,1},{2,18},{18,2},{3,19},{19,3},{4,20},{20... | collective-permute-start | bytes 786440 | tf_op jit(solution)/shard_map/ppermute | solution.py:529
  279.2 13.2 %collective-permute-start.20 = (bf16[128,1280]{1,0:T(8,128)(2,1)S(1)}, bf16[128,1280]{1,0:T(8,128)(2,1)S(1)}, u32[]{:S(2)}, u32[]{:S(2)}) collective-permute-start(bf16[128,1280]{1,0:T(8,128)(2,1)S(1)} %bitcast.57), channel_id=1, source_target_pairs={{0,16},{16,0},{1,17},{17,1},{2,18},{18,2},{3,19},{19,3},{4,20},{20... | collective-permute-start | bytes 983048 | tf_op jit(solution)/shard_map/ppermute | solution.py:529
  313.1 14.2 %collective-permute-start.19 = (bf16[16,112,128]{2,1,0:T(8,128)(2,1)S(1)}, bf16[16,112,128]{2,1,0:T(8,128)(2,1)S(1)}, u32[]{:S(2)}, u32[]{:S(2)}) collective-permute-start(bf16[16,112,128]{2,1,0:T(8,128)(2,1)S(1)} %slice.44.one_ref), channel_id=1, source_target_pairs={{0,16},{16,0},{1,17},{17,1},{2,18},{18,2},{3,19},{19,3},{4,20},{20... | collective-permute-start | bytes 1376264 | tf_op jit(solution)/shard_map/ppermute | solution.py:529
  (41 other events, 494.4 us)
Sparse Core Ops, SparseCore 0:
  58.0 78.9 all-gather.1
